TPU v7x, 256 devices: a whole 4x4x8 slice. The times are simulated.
256 devices in a mesh: face: 8 (over y_hi, x), tile: 32 (over y_lo, z, core).
Axes of the slice: x: 4, y: 4 (y_hi: 2, y_lo: 2; y = y_hi * 2 + y_lo), z: 8, core: 2. Of those that a mesh axis runs over, the one named last changes fastest.
Arguments:
- inputs: bfloat16 [8, 256, 256, 128], P('face', 'tile'), may hold values from -6 to 6
- kernel: float32 [7, 7, 128], replicated, may hold values from -0.875 to 0.875
- conv_bias: float32 [128], replicated, may hold values from -3 to 3
- norm_gain: float32 [128], replicated, may hold values from 0.5 to 1.5
- norm_bias: float32 [128], replicated, may hold values from -3 to 3
- expand_weight: bfloat16 [128, 512], replicated, may hold values from -0.5 to 0.5
- expand_bias: float32 [512], replicated, may hold values from -3 to 3
- reduce_weight: bfloat16 [512, 128], replicated, may hold values from -0.25 to 0.25
- reduce_bias: float32 [128], replicated, may hold values from -3 to 3
- layer_scale: float32 [128], replicated, may hold values from 0.5 to 1.5
- neighbours: int32 [8, 4, 3], replicated, may hold values from 0 to 7, as said below
- cotangent: bfloat16 [8, 256, 256, 128], P('face', 'tile'), may hold values from -6 to 6
Outputs:
- output: bfloat16 [8, 256, 256, 128], P('face', 'tile')
- kernel_grad: float32 [7, 7, 128], replicated
- conv_bias_grad: float32 [128], replicated
- gain_grad: float32 [128], replicated
- norm_bias_grad: float32 [128], replicated
- expand_grad: float32 [128, 512], replicated
- expand_bias_grad: float32 [512], replicated
- reduce_grad: float32 [512, 128], replicated
- reduce_bias_grad: float32 [128], replicated
- scale_grad: float32 [128], replicated
Inputs may be any that keep to these rules, and one draw needn't show every extreme that they name: neighbours[f, s] = (partner face, partner side, reversal flag 0 or 1); the partner face is never f itself; sides numbered 0 north, 1 east, 2 south, 3 west; side 0 is always glued to side 2 and side 1 to side 3; the gluing is reciprocal: if side s of f takes side s2 of g, then side s2 of g takes side s of f with the same flag.
All inputs are finite; a program needn't handle non-finite values.
Results may differ from a plain program's by a relative error of at most 0.0075.
Values may be sent and summed in bfloat16 or wider, within the bound.
A program may use at most 64 MiB of HBM per device.

v0:
```python
import math

import jax
import jax.numpy as jnp
from jax import lax
from jax.sharding import PartitionSpec as P

EPS = 1e-06


def extended_2(block, sides, width):
    for axis, dim in sides:
        count = lax.axis_size(axis)
        forward = [(i, i + 1) for i in range(count - 1)]
        backward = [(target, source) for source, target in forward]
        low = lax.ppermute(
            lax.slice_in_dim(block, block.shape[dim] - width, None, axis=dim), axis, forward
        )
        high = lax.ppermute(lax.slice_in_dim(block, 0, width, axis=dim), axis, backward)
        block = jnp.concatenate([low, block, high], axis=dim)
    return block


def from_root(block, axis, owner):
    block = jnp.where(lax.axis_index(axis) == owner, block, jnp.zeros_like(block))
    return lax.psum(block, axis)


def contract_rows(left, right):
    return lax.dot_general(
        left, right, (((0,), (0,)), ((), ())), preferred_element_type=jnp.float32
    )


def contract_cols(left, right):
    return lax.dot_general(
        left, right, (((1,), (1,)), ((), ())), preferred_element_type=jnp.float32
    )


def block_pass(
    padded,
    residual,
    cotangent,
    kernel,
    conv_bias,
    norm_gain,
    norm_bias,
    expand_weight,
    expand_bias,
    reduce_weight,
    reduce_bias,
    layer_scale,
):
    rows, width, chans = residual.shape
    side = kernel.shape[0]
    conv = jnp.zeros((rows, width, chans), jnp.float32) + conv_bias
    for first in range(side):
        for second in range(side):
            conv = conv + kernel[first, second] * padded[
                first : first + rows, second : second + width
            ].astype(jnp.float32)
    flat = conv.reshape(-1, chans)
    mean = jnp.mean(flat, -1, keepdims=True)
    centred = flat - mean
    variance = jnp.mean(centred * centred, -1, keepdims=True)
    inverse = lax.rsqrt(variance + EPS)
    normed = centred * inverse
    scaled = (normed * norm_gain + norm_bias).astype(jnp.bfloat16)
    hidden = jnp.dot(scaled, expand_weight, preferred_element_type=jnp.float32) + expand_bias
    active, gelu_back = jax.vjp(jax.nn.gelu, hidden)
    active_low = active.astype(jnp.bfloat16)
    branch = jnp.dot(active_low, reduce_weight, preferred_element_type=jnp.float32) + reduce_bias
    output = (residual.reshape(-1, chans).astype(jnp.float32) + layer_scale * branch).astype(
        jnp.bfloat16
    )
    cot = cotangent.reshape(-1, chans).astype(jnp.float32)
    scale_grad = jnp.sum(cot * branch, 0)
    branch_cot = (cot * layer_scale).astype(jnp.bfloat16)
    reduce_grad = contract_rows(active_low, branch_cot)
    reduce_bias_grad = jnp.sum(branch_cot.astype(jnp.float32), 0)
    active_cot = contract_cols(branch_cot, reduce_weight)
    hidden_cot = gelu_back(active_cot)[0].astype(jnp.bfloat16)
    expand_grad = contract_rows(scaled, hidden_cot)
    expand_bias_grad = jnp.sum(hidden_cot.astype(jnp.float32), 0)
    scaled_cot = contract_cols(hidden_cot, expand_weight)
    gain_grad = jnp.sum(scaled_cot * normed, 0)
    norm_bias_grad = jnp.sum(scaled_cot, 0)
    normed_cot = scaled_cot * norm_gain
    conv_cot = inverse * (
        normed_cot
        - jnp.mean(normed_cot, -1, keepdims=True)
        - normed * jnp.mean(normed_cot * normed, -1, keepdims=True)
    )
    conv_bias_grad = jnp.sum(conv_cot, 0)
    conv_cot = conv_cot.reshape(rows, width, chans)
    kernel_grad = jnp.stack(
        [
            jnp.stack(
                [
                    jnp.sum(
                        padded[first : first + rows, second : second + width].astype(jnp.float32)
                        * conv_cot,
                        (0, 1),
                    )
                    for second in range(side)
                ]
            )
            for first in range(side)
        ]
    )
    grads = (
        kernel_grad,
        conv_bias_grad,
        gain_grad,
        norm_bias_grad,
        expand_grad,
        expand_bias_grad,
        reduce_grad,
        reduce_bias_grad,
        scale_grad,
    )
    return (output.reshape(rows, width, chans), grads)


def pick_source(received, source, member):
    return lax.dynamic_index_in_dim(received, source, 0, keepdims=False)[member]


def window_pair(band, rows, tiles, tile_id):
    widened = jnp.pad(band, ((0, 0), (3, 3), (0, 0)))
    direct = lax.dynamic_slice_in_dim(widened, tile_id * rows, rows + 6, 1)
    mirror = lax.dynamic_slice_in_dim(widened, (tiles - 1 - tile_id) * rows, rows + 6, 1)
    return (direct, mirror)


def body(
    inputs,
    kernel,
    conv_bias,
    norm_gain,
    norm_bias,
    expand_weight,
    expand_bias,
    reduce_weight,
    reduce_bias,
    layer_scale,
    neighbours,
    cotangent,
):
    local = inputs[0]
    rows, width, chans = local.shape
    tiles = lax.axis_size("tile")
    faces = lax.axis_size("face")
    tile_id = lax.axis_index("tile")
    face_id = lax.axis_index("face")
    extended = extended_2(local, (("tile", 0),), 3)
    west_piece = jnp.swapaxes(local[:, 0:3], 0, 1)
    east_piece = jnp.swapaxes(local[:, ::-1][:, 0:3], 0, 1)
    west_band, east_band = (
        lax.all_gather(west_piece, "tile", axis=1, tiled=True),
        lax.all_gather(east_piece, "tile", axis=1, tiled=True),
    )
    east_direct, east_mirror = window_pair(east_band, rows, tiles, tile_id)
    west_direct, west_mirror = window_pair(west_band, rows, tiles, tile_id)
    north_band = from_root(local[0:3], "tile", 0)
    south_band = from_root(local[::-1][0:3], "tile", tiles - 1)
    north_direct, north_mirror = window_pair(north_band, rows, tiles, tile_id)
    south_direct, south_mirror = window_pair(south_band, rows, tiles, tile_id)
    directs = jnp.stack([north_direct, east_direct, south_direct, west_direct])
    mirrors = jnp.stack([north_mirror, east_mirror, south_mirror, west_mirror])

    def orient(entry):
        straight = lax.dynamic_index_in_dim(directs, entry[1], 0, keepdims=False)
        turned = lax.dynamic_index_in_dim(mirrors, entry[1], 0, keepdims=False)
        window = jnp.where(entry[2] == 1, turned[:, ::-1], straight)
        return jnp.where(entry[0] == face_id, window, jnp.zeros_like(window))

    oriented = jax.vmap(jax.vmap(orient))(neighbours)
    side_rows = jnp.stack([oriented[:, 1], oriented[:, 3]], 1)
    polar_part = jnp.stack([oriented[:, 0], oriented[:, 2]], 1)[:, :, :, 3 : 3 + rows]
    mine = lax.dynamic_index_in_dim(neighbours, face_id, 0, keepdims=False)
    got_sides, got_polar = (
        lax.all_to_all(side_rows, "face", split_axis=0, concat_axis=0, tiled=True),
        lax.all_to_all(polar_part, "face", split_axis=0, concat_axis=0, tiled=True),
    )
    my_polar = jnp.stack(
        [pick_source(got_polar, mine[0, 0], 0), pick_source(got_polar, mine[2, 0], 1)]
    )
    polar_full = lax.all_gather(my_polar, "tile", axis=2, tiled=True)
    north_halo = polar_full[0]
    south_halo = polar_full[1]
    east_halo = pick_source(got_sides, mine[1, 0], 0)
    west_halo = pick_source(got_sides, mine[3, 0], 1)
    top = jnp.where(tile_id == 0, north_halo[::-1], extended[0:3])
    bottom = jnp.where(tile_id == tiles - 1, south_halo, extended[rows + 3 : rows + 6])
    middle = jnp.concatenate([top, local, bottom], 0)
    west_cols = jnp.swapaxes(west_halo[::-1], 0, 1)
    east_cols = jnp.swapaxes(east_halo, 0, 1)
    padded = jnp.concatenate([west_cols, middle, east_cols], 1)
    output, grads = block_pass(
        padded,
        local,
        cotangent[0],
        kernel,
        conv_bias,
        norm_gain,
        norm_bias,
        expand_weight,
        expand_bias,
        reduce_weight,
        reduce_bias,
        layer_scale,
    )
    summed = lax.psum(
        (grads[0], grads[1], grads[2], grads[3], grads[4], grads[5], grads[6], grads[7], grads[8]),
        ("face", "tile"),
    )
    factor = 1.0 / math.sqrt(faces * width * width)
    result = [item * factor for item in summed]
    return (
        output[None],
        result[0],
        result[1],
        result[2],
        result[3],
        result[4],
        result[5],
        result[6],
        result[7],
        result[8],
    )


def solution(mesh):
    return jax.shard_map(
        body,
        mesh=mesh,
        in_specs=(
            P("face", "tile", None, None),
            P(),
            P(),
            P(),
            P(),
            P(),
            P(),
            P(),
            P(),
            P(),
            P(),
            P("face", "tile", None, None),
        ),
        out_specs=(P("face", "tile", None, None), P(), P(), P(), P(), P(), P(), P(), P(), P()),
        check_vma=False,
    )
```

profile of v0, /device:TPU:1, one launch (start us, length us, event | category | flops | bytes accessed | tf_op | source)
XLA Modules:
  0.0 679.4 jit_solution(420640332184254526)
XLA Ops:
  7.3 1.5 copy.391
  8.9 4.9 collective-permute-start
  13.9 1.9 collective-permute-start.1
  17.1 0.8 broadcast_select_fusion
  18.1 37.8 %all_gather.9 = bf16[3,256,128]{2,1,0:T(8,128)(2,1)S(1)} all-gather(bf16[3,8,128]{2,1,0:T(8,128)(2,1)S(1)} %reverse_bitcast_fusion.1), channel_id=1, replica_groups=mesh['face'=8,'tile'=32] {'tile'}, dimensions={1}, use_global_device_ids=true | all-gather | bytes 202752 | tf_op jit(solution)/shard_map/all_gather | solution.py:162
  55.9 31.2 %all_gather.10 = bf16[3,256,128]{2,1,0:T(8,128)(2,1)S(1)} all-gather(bf16[3,8,128]{2,1,0:T(8,128)(2,1)S(1)} %get-tuple-element.95), channel_id=1, replica_groups=mesh['face'=8,'tile'=32] {'tile'}, dimensions={1}, use_global_device_ids=true | all-gather | bytes 202752 | tf_op jit(solution)/shard_map/all_gather | solution.py:161
  97.5 147.0 %all-reduce.12.cloned.1.call-done = (bf16[3,256,128]{2,0,1:T(4,128)(2,1)}, bf16[3,256,128]{2,0,1:T(4,128)(2,1)}) async-done(((bf16[3,256,128]{2,0,1:T(4,128)(2,1)}, bf16[3,256,128]{2,0,1:T(4,128)(2,1)}), (bf16[3,256,128]{2,0,1:T(4,128)(2,1)}, bf16[3,256,128]{2,0,1:T(4,128)(2,1)})) %all-reduce.12.cloned.1.call-update) | async-done | bytes 393232 | tf_op jit(solution)/shard_map/psum | solution.py:26
  248.8 6.1 all-to-all-start.1
  254.9 1.1 pad_maximum_fusion.3
  256.0 5.7 all-to-all-done.1
  261.7 3.4 all-to-all-start
  265.2 33.7 %all_gather.11 = bf16[2,3,256,128]{3,1,2,0:T(4,128)(2,1)S(1)} all-gather(bf16[2,3,8,128]{3,1,2,0:T(4,128)(2,1)S(1)} %pad_maximum_fusion.7), channel_id=1, replica_groups=mesh['face'=8,'tile'=32] {'tile'}, dimensions={2}, use_global_device_ids=true | all-gather | bytes 405504 | tf_op jit(solution)/shard_map/all_gather | solution.py:190
  300.8 10.7 %fusion.126 = (f32[8,256]{0,1:T(8,128)S(1)}, f32[8,256,128]{2,0,1:T(8,128)}) fusion(bf16[14,259,128]{2,0,1:T(8,128)(2,1)S(1)} %get-tuple-element.90, f32[128]{0:T(128)S(1)} %get-tuple-element.161, f32[128]{0:T(128)S(1)} %get-tuple-element.162, f32[128]{0:T(128)S(1)} %get-tuple-element.115, bf16[3,256,128]{2,0,1:T(4,128)(2,1)S(1)} %fusion.115, ...), kind=kLoop, calls=%fused_computation.364 | loop fusion | flops 43513856 | bytes 24019968 | tf_op jit(solution)/shard_map/reduce_sum | solution.py:64
  311.8 2.4 copy.260
  314.2 2.5 multiply_reduce_fusion.2
  316.7 1.0 copy.263
  317.7 1.9 add_convert_fusion
  319.6 1.8 multiply_convert_fusion
  321.5 1.5 fusion.108
  323.0 1.5 fusion.133
  324.5 3.3 convert_reduce_fusion
  327.8 1.3 copy-done.2
  329.2 1.2 fusion.132
  330.4 3.2 multiply_reduce_fusion
  333.7 1.4 fusion.125
  335.0 3.0 fusion.103
  338.1 3.3 fusion.99
  341.4 2.5 fusion.100
  344.1 76.5 %all-reduce.4 = (f32[7,7,128]{2,1,0:T(8,128)S(1)}, f32[128]{0:T(128)S(1)}, f32[128]{0:T(128)S(1)}, f32[128]{0:T(128)S(1)}, f32[512]{0:T(512)S(1)}, /*index=5*/f32[128]{0:T(128)S(1)}, f32[128]{0:T(128)S(1)}) all-reduce(f32[7,7,128]{2,1,0:T(8,128)S(1)} %constant_dynamic-update-slice_fusion, ...), channel_id=1, replica_groups=mesh['face'=8,'tile'=32] {'face','tile'}, use_global_device_ids=true, to_apply=%region_55.56 | all-reduce | flops 7424 | bytes 59392 | tf_op jit(solution)/shard_map/psum | solution.py:215
  424.4 244.7 %all-reduce.10.cloned.1.call-done = (f32[128,512]{1,0:T(8,128)}, f32[512,128]{1,0:T(8,128)}) async-done(((f32[128,512]{1,0:T(8,128)}, f32[512,128]{1,0:T(8,128)}), (f32[128,512]{1,0:T(8,128)}, f32[512,128]{1,0:T(8,128)})) %all-reduce.10.cloned.1.call-update) | async-done | bytes 524304 | tf_op jit(solution)/shard_map/psum | solution.py:215
  669.2 1.7 broadcast_multiply_fusion
  670.8 1.7 broadcast_multiply_fusion.1
  (114 shorter events, 14.5 us)
Async XLA Ops:
  7.2 312.4 %copy-start = (bf16[128,512]{1,0:T(8,128)(2,1)S(1)}, bf16[128,512]{1,0:T(8,128)(2,1)}, u32[]{:S(2)}) copy-start(bf16[128,512]{1,0:T(8,128)(2,1)} %param.17) | copy-start | bytes 393220
  7.2 10.8 %copy-start.7 = (s32[8,4,3]{0,1,2:T(4,128)S(1)}, s32[8,4,3]{0,1,2:T(4,128)}, u32[]{:S(2)}) copy-start(s32[8,4,3]{0,1,2:T(4,128)} %param.22) | copy-start | bytes 1156
  7.2 10.8 %copy-start.8 = (f32[7,7,128]{2,1,0:T(8,128)S(1)}, f32[7,7,128]{2,1,0:T(8,128)}, u32[]{:S(2)}) copy-start(f32[7,7,128]{2,1,0:T(8,128)} %param.13) | copy-start | bytes 75268
  7.2 88.9 %copy-start.11 = (f32[128]{0:T(128)S(1)}, f32[128]{0:T(128)}, u32[]{:S(2)}) copy-start(f32[128]{0:T(128)} %param.21) | copy-start | bytes 1540
  7.2 88.9 %copy-start.5 = (bf16[1,8,256,128]{3,2,1,0:T(8,128)(2,1)S(1)}, bf16[1,8,256,128]{3,2,1,0:T(8,128)(2,1)}, u32[]{:S(2)}) copy-start(bf16[1,8,256,128]{3,2,1,0:T(8,128)(2,1)} %param.23) | copy-start | bytes 1572868
  7.2 237.3 %all-reduce.12.cloned.1.call-start = ((), (), s32[]{:S(2)}) async-start(), calls=%async_computation.3 | async-start | bytes 1048576 | tf_op jit(solution)/shard_map/psum | solution.py:26
  8.9 291.0 %collective-permute-start = (bf16[3,256,128]{2,0,1:T(4,128)(2,1)S(1)}, bf16[3,256,128]{2,0,1:T(4,128)(2,1)S(1)}, u32[]{:S(2)}, u32[]{:S(2)}) collective-permute-start(bf16[3,256,128]{2,0,1:T(4,128)(2,1)S(1)} %get-tuple-element.93), channel_id=1, source_target_pairs={{0,1},{1,2},{2,3},{3,4},{4,5},{5,6},{6,7},{7,8},{8,9},{9,10},{10,1... | collective-permute-start | bytes 589832 | tf_op jit(solution)/shard_map/ppermute | solution.py:16
  13.9 285.9 %collective-permute-start.1 = (bf16[3,256,128]{2,0,1:T(4,128)(2,1)S(1)}, bf16[3,256,128]{2,0,1:T(4,128)(2,1)S(1)}, u32[]{:S(2)}, u32[]{:S(2)}) collective-permute-start(bf16[3,256,128]{2,0,1:T(4,128)(2,1)S(1)} %get-tuple-element.92), channel_id=1, source_target_pairs={{1,0},{2,1},{3,2},{4,3},{5,4},{6,5},{7,6},{8,7},{9,8},{10,9},{11,1... | collective-permute-start | bytes 589832 | tf_op jit(solution)/shard_map/ppermute | solution.py:19
  248.8 12.9 %all-to-all-start.1 = ((bf16[8,2,3,8,128]{4,3,2,1,0:T(8,128)(2,1)}), bf16[8,2,3,8,128]{4,3,2,1,0:T(8,128)(2,1)S(1)}, u32[]{:S(2)}, u32[]{:S(2)}) async-start(bf16[8,2,3,8,128]{4,3,2,1,0:T(8,128)(2,1)} %copy.256), calls=%async_computation.1 | async-start | bytes 196608 | tf_op jit(solution)/shard_map/all_to_all | solution.py:185
  261.7 38.3 %all-to-all-start = ((bf16[8,2,3,14,128]{4,1,3,2,0:T(2,128)(2,1)}), bf16[8,2,3,14,128]{4,1,3,2,0:T(2,128)(2,1)S(1)}, u32[]{:S(2)}, u32[]{:S(2)}) async-start(bf16[8,2,3,14,128]{4,1,3,2,0:T(2,128)(2,1)} %pad_maximum_fusion.3), calls=%async_computation | async-start | bytes 344064 | tf_op jit(solution)/shard_map/all_to_all | solution.py:184
  265.1 404.1 %all-reduce.10.cloned.1.call-start = ((), (), s32[]{:S(2)}) async-start(), calls=%async_computation.2 | async-start | bytes 1048576 | tf_op jit(solution)/shard_map/psum | solution.py:215
  311.5 8.0 %copy-start.14 = (f32[512]{0:T(512)S(1)}, f32[512]{0:T(512)}, u32[]{:S(2)}) copy-start(f32[512]{0:T(512)} %param.18) | copy-start | bytes 6148
  319.6 1.9 copy-start.3
  319.6 1.9 copy-start.6
  319.6 1.9 copy-start.12
  319.6 1.9 copy-start.13
  319.6 1.9 copy-start.15
  324.5 5.9 copy-start.9
  327.8 1.4 copy-start.2
  330.4 3.3 copy-start.1
  330.4 3.3 copy-start.4
  341.4 2.7 copy-start.10
Sparse Core Ops, SparseCore 0:
  18.1 226.4 all-reduce.11
  423.4 245.7 all-reduce.9
where the time goes:
time: 681 us; the launch traced here: 679 us
  waiting for transfers between devices  398 us (58%)
  blocking collectives  179 us (26%)
  other arithmetic  37.4 us (5%)
  between operations  22.5 us (3%)
  starting transfers between devices  16.5 us (2%)
  local copies, waits for them, and re-layouts  13.7 us (2%)
  matrix products  12.5 us (2%)
    psum x1, waiting for transfers between devices, body(): lax.psum((grads[0], grads[1], grads[2], grads[3], grads[4], grads[5], gra...  245 us
    psum x1, waiting for transfers between devices, from_root(): return lax.psum(block, axis)  147 us
    psum x1, blocking collectives, body(): lax.psum((grads[0], grads[1], grads[2], grads[3], grads[4], grads[5], gra...  76.5 us
    all_gather x1, blocking collectives, body(): lax.all_gather(east_piece, 'tile', axis=1, tiled=True)  37.8 us
    all_gather x1, blocking collectives, body(): polar_full = lax.all_gather(my_polar, 'tile', axis=2, tiled=True)  33.7 us
    all_gather x1, blocking collectives, body(): lax.all_gather(west_piece, 'tile', axis=1, tiled=True)  31.2 us
  transfers between devices with their start and end apart: 6, of which 3 were waited for; matrix products, arithmetic and copies ran while one was open for 2% of the time, Pallas kernels for 0%

commit v1 on v0

v1 whole, which is shorter than its diff:
```python
import functools
import math

import jax
import jax.numpy as jnp
from jax import lax
from jax.experimental import pallas as pl
from jax.experimental.pallas import tpu as pltpu
from jax.sharding import PartitionSpec as P

EPS = 1e-06
MESH = pl.DeviceIdType.MESH
BF = jnp.bfloat16
F32 = jnp.float32
ROOT = math.sqrt(2.0 / math.pi)
CUBE = 0.044715
FACES = 8
TILES = 32
VMEM = pl.BlockSpec(memory_space=pltpu.VMEM)
SMEM = pl.BlockSpec(memory_space=pltpu.SMEM)
ANY = pl.BlockSpec(memory_space=pl.ANY)


def place():
    return lax.axis_index("face"), lax.axis_index("tile")


def remote(src, dst, send, recv, face, tile):
    return pltpu.make_async_remote_copy(
        src_ref=src, dst_ref=dst, send_sem=send, recv_sem=recv,
        device_id=(face, tile), device_id_type=MESH,
    )


def halo_kernel(
    nbr, x, top, bot, hbuf, side,
    pieces, chosen, nsbuf, nsend,
    row_send, row_recv, piece_send, piece_recv, band_send, band_recv,
    side_send, side_recv, fwd_send, fwd_recv, local_sem,
):
    f, t = place()
    last = TILES - 1
    mirror = last - t
    is_first = t == 0
    is_last = t == last

    barrier = pltpu.get_barrier_semaphore()

    def hello(face, tile):
        pl.semaphore_signal(barrier, inc=1, device_id=(face, tile), device_id_type=MESH)

    others = [lax.rem(f + k, FACES) for k in range(1, FACES)]
    for g in others:
        hello(g, t)
    hello(f, mirror)
    has_up = t > 0
    has_down = t < last
    mir_up = jnp.logical_and(mirror < last, mirror + 1 != t)
    mir_down = jnp.logical_and(mirror > 0, mirror - 1 != t)

    @pl.when(has_up)
    def _():
        hello(f, t - 1)

    @pl.when(has_down)
    def _():
        hello(f, t + 1)

    @pl.when(mir_up)
    def _():
        hello(f, mirror + 1)

    @pl.when(mir_down)
    def _():
        hello(f, mirror - 1)

    edge = jnp.logical_or(is_first, is_last)

    @pl.when(edge)
    def _():
        for g in range(FACES):
            hello(g, mirror)

    for d in range(3):
        west = x[:, d : d + 1, :].astype(F32).reshape(8, 128)
        east = x[:, 255 - d : 256 - d, :].astype(F32).reshape(8, 128)
        pieces[f, d] = jnp.concatenate([west, east], 0).astype(BF)

    one = lambda cond: cond.astype(jnp.int32)
    count = 8 + one(has_up) + one(has_down) + one(mir_up) + one(mir_down) + 8 * one(edge)
    pl.semaphore_wait(barrier, count)

    def band_copy(rows, k, g):
        return remote(
            x.at[pl.ds(rows, 3), pl.ds(g * 32, 32), :], nsbuf.at[f],
            band_send.at[k], band_recv.at[f], g, t,
        )

    def piece_copy(k, g):
        return remote(pieces.at[f], pieces.at[f], piece_send.at[k], piece_recv.at[f], g, t)

    def up_copy():
        return remote(x.at[pl.ds(0, 3)], bot, row_send.at[0], row_recv.at[0], f, t - 1)

    def down_copy():
        return remote(x.at[pl.ds(5, 3)], top, row_send.at[1], row_recv.at[1], f, t + 1)

    for rows, cond in ((0, is_first), (5, is_last)):

        @pl.when(cond)
        def _(rows=rows):
            for k, g in enumerate(others):
                band_copy(rows, k, g).start()
            nsbuf[f] = x[rows : rows + 3, pl.ds(pl.multiple_of(f * 32, 32), 32), :]

    for k, g in enumerate(others):
        piece_copy(k, g).start()

    @pl.when(has_up)
    def _():
        up_copy().start()

    @pl.when(has_down)
    def _():
        down_copy().start()

    def forward(g):
        return remote(nsend.at[g], hbuf.at[f], fwd_send.at[g], fwd_recv.at[f], g, mirror)

    for side_id, rows, cond in ((0, 5, is_last), (2, 0, is_first)):

        @pl.when(cond)
        def _(side_id=side_id, rows=rows):
            for k, g in enumerate(others):
                remote(
                    x.at[pl.ds(rows, 3), pl.ds(g * 32, 32), :], nsbuf.at[g],
                    band_send.at[k], band_recv.at[g], g, t,
                ).wait_recv()
            for g in range(FACES):
                nsend[g] = nsbuf[nbr[g, side_id, 0]]
                forward(g).start()

    for k, g in enumerate(others):
        remote(pieces.at[f], pieces.at[g], piece_send.at[k], piece_recv.at[g], g, t).wait_recv()
    from_west = pieces[nbr[f, 3, 0]]
    from_east = pieces[nbr[f, 1, 0]]
    chosen[...] = jnp.concatenate(
        [from_west.astype(F32)[:, 8:16], from_east.astype(F32)[:, 0:8]], 1
    ).astype(BF)

    def side_copy(slot, tile):
        return remote(chosen, side.at[slot], side_send.at[slot], side_recv.at[slot], f, tile)

    own = pltpu.make_async_copy(chosen, side.at[1], local_sem.at[0])
    own.start()
    side_copy(4, mirror).start()

    @pl.when(has_down)
    def _():
        side_copy(0, t + 1).start()

    @pl.when(has_up)
    def _():
        side_copy(2, t - 1).start()

    @pl.when(mir_up)
    def _():
        side_copy(3, mirror + 1).start()

    @pl.when(mir_down)
    def _():
        side_copy(5, mirror - 1).start()

    @pl.when(mirror + 1 == t)
    def _():
        same = pltpu.make_async_copy(chosen, side.at[3], local_sem.at[1])
        same.start()
        same.wait()

    @pl.when(mirror - 1 == t)
    def _():
        same = pltpu.make_async_copy(chosen, side.at[5], local_sem.at[1])
        same.start()
        same.wait()

    own.wait()

    side_copy(4, mirror).wait_recv()

    @pl.when(has_up)
    def _():
        side_copy(0, t - 1).wait_recv()
        down_copy().wait_recv()

    @pl.when(has_down)
    def _():
        side_copy(2, t + 1).wait_recv()
        up_copy().wait_recv()

    @pl.when(mir_up)
    def _():
        side_copy(3, mirror + 1).wait_recv()

    @pl.when(mir_down)
    def _():
        side_copy(5, mirror - 1).wait_recv()

    @pl.when(edge)
    def _():
        for g in range(FACES):
            remote(
                nsend.at[g], hbuf.at[g], fwd_send.at[g], fwd_recv.at[g], g, mirror
            ).wait_recv()

    for k, g in enumerate(others):
        piece_copy(k, g).wait_send()
    side_copy(4, mirror).wait_send()

    @pl.when(has_up)
    def _():
        side_copy(2, t - 1).wait_send()
        up_copy().wait_send()

    @pl.when(has_down)
    def _():
        side_copy(0, t + 1).wait_send()
        down_copy().wait_send()

    @pl.when(mir_up)
    def _():
        side_copy(3, mirror + 1).wait_send()

    @pl.when(mir_down)
    def _():
        side_copy(5, mirror - 1).wait_send()

    @pl.when(edge)
    def _():
        for k, g in enumerate(others):
            band_copy(0, k, g).wait_send()
        for g in range(FACES):
            forward(g).wait_send()


def exchange_halos(neighbours, x):
    dma = pltpu.SemaphoreType.DMA
    return pl.pallas_call(
        halo_kernel,
        out_shape=(
            jax.ShapeDtypeStruct((3, 256, 128), BF),
            jax.ShapeDtypeStruct((3, 256, 128), BF),
            jax.ShapeDtypeStruct((8, 3, 32, 128), BF),
            jax.ShapeDtypeStruct((6, 3, 16, 128), BF),
        ),
        in_specs=[SMEM, VMEM],
        out_specs=(ANY, ANY, ANY, ANY),
        scratch_shapes=[
            pltpu.VMEM((8, 3, 16, 128), BF),
            pltpu.VMEM((3, 16, 128), BF),
            pltpu.VMEM((8, 3, 32, 128), BF),
            pltpu.VMEM((8, 3, 32, 128), BF),
            dma((2,)), dma((2,)), dma((8,)), dma((8,)), dma((8,)), dma((8,)),
            dma((6,)), dma((6,)), dma((8,)), dma((8,)), dma((2,)),
        ],
        compiler_params=pltpu.CompilerParams(
            collective_id=0, has_side_effects=True, vmem_limit_bytes=16 * 1024 * 1024
        ),
        name="halo",
    )(neighbours, x)


def nt(left, right):
    return lax.dot_general(left, right, (((1,), (1,)), ((), ())), preferred_element_type=F32)


def nn(left, right):
    return lax.dot_general(left, right, (((1,), (0,)), ((), ())), preferred_element_type=F32)


def one_hot(rows, cols, index):
    r = lax.broadcasted_iota(jnp.int32, (rows, cols), 0)
    c = lax.broadcasted_iota(jnp.int32, (rows, cols), 1)
    return jnp.where(c == index(r), 1.0, 0.0).astype(BF)


def fold(v):
    rows, chans = v.shape
    return jnp.sum(v.reshape(rows // 8, 8, chans), 0)


def block_kernel(
    nbr, x, cot, top, bot, hbuf, side, kern, cb, gain, nb, we, be, wr, br, ls,
    out, big, small,
    pad, conv, taps, acc_e, acc_r, sums,
):
    f, t = place()
    pad[3:11, 8:264, :] = x[...].astype(F32)

    @pl.when(t > 0)
    def _():
        pad[0:3, 8:264, :] = top[...].astype(F32)

    @pl.when(t < TILES - 1)
    def _():
        pad[11:14, 8:264, :] = bot[...].astype(F32)

    def polar(flag, rows):
        turn = one_hot(256, 256, lambda r: 255 - r)
        for d in range(3):
            band = jnp.concatenate([hbuf[k, d] for k in range(8)], 0)
            turned = nn(turn, band)
            pad[rows[d], 8:264, :] = jnp.where(flag == 1, turned, band.astype(F32))

    @pl.when(t == 0)
    def _():
        polar(nbr[f, 0, 2], (0, 1, 2))

    @pl.when(t == TILES - 1)
    def _():
        polar(nbr[f, 2, 2], (11, 12, 13))

    keep_up = t > 0
    keep_down = t < TILES - 1
    turn = one_hot(24, 24, lambda r: r // 8 * 8 + 7 - r % 8)
    for d in range(3):
        slots = [side[s, d].astype(F32) for s in range(6)]
        for s in (0, 3):
            slots[s] = jnp.where(keep_up, slots[s], 0.0)
        for s in (2, 5):
            slots[s] = jnp.where(keep_down, slots[s], 0.0)
        for first, side_id, col in ((0, 3, 7 - d), (8, 1, 264 + d)):
            straight = jnp.concatenate([slots[s][first : first + 8] for s in (0, 1, 2)], 0)
            turned = jnp.concatenate([slots[s][first : first + 8] for s in (3, 4, 5)], 0)
            turned = nn(turn, turned.astype(BF))
            halo = jnp.where(nbr[f, side_id, 2] == 1, turned, straight)
            pad[0:14, col : col + 1, :] = halo[5:19].reshape(14, 1, 128)

    for a in range(7):
        for b in range(7):
            taps[a * 7 + b] = jnp.broadcast_to(kern[a, b : b + 1, :], (8, 128))

    bias = jnp.broadcast_to(cb[...].reshape(1, 128), (8, 128))

    @pl.loop(0, 32)
    def _(jb):
        col = pl.multiple_of(jb * 8, 8)
        acc = [bias] * 8
        for b in range(7):
            tap = [taps[a * 7 + b] for a in range(7)]
            for row in range(14):
                v = pad[row, pl.ds(col + 5 + b, 8), :]
                for a in range(7):
                    if 0 <= row - a < 8:
                        acc[row - a] = acc[row - a] + tap[a] * v
        for r in range(8):
            conv[r, pl.ds(col, 8), :] = acc[r]

    acc_e[...] = jnp.zeros_like(acc_e)
    acc_r[...] = jnp.zeros_like(acc_r)
    sums[...] = jnp.zeros_like(sums)
    mean_of = jnp.full((128, 128), 1.0 / 128, BF)
    vec = lambda ref: ref[...].reshape(1, -1)
    ones = jnp.ones((16, 256), BF)

    @pl.loop(0, 8)
    def _(r):
        c = conv[r]
        centred = c - nn(c.astype(BF), mean_of)
        variance = nn((centred * centred).astype(BF), mean_of)
        inverse = lax.rsqrt(variance + EPS)
        normed = centred * inverse
        scaled = (normed * vec(gain) + vec(nb)).astype(BF)
        g = cot[r].astype(F32)
        branch_cot = (g * vec(ls)).astype(BF)
        hidden = nn(scaled, we[...]) + vec(be)
        active_cot = nt(branch_cot, wr[...])
        square = hidden * hidden
        s = 0.5 + 0.5 * jnp.tanh(hidden * (ROOT + (ROOT * CUBE) * square))
        active = hidden * s
        active_low = active.astype(BF)
        slope = s + active * (1.0 - s) * (2.0 * ROOT + (6.0 * ROOT * CUBE) * square)
        hidden_cot = (active_cot * slope).astype(BF)
        branch = nn(active_low, wr[...]) + vec(br)
        out[r] = (x[r].astype(F32) + vec(ls) * branch).astype(BF)
        left = jnp.concatenate([scaled.T, ones], 0)
        acc_e[...] += nn(left, hidden_cot)
        acc_r[...] += nn(branch_cot.T, active_low)
        scaled_cot = nt(hidden_cot, we[...])
        normed_cot = scaled_cot * vec(gain)
        m1 = nn(normed_cot.astype(BF), mean_of)
        m2 = nn((normed_cot * normed).astype(BF), mean_of)
        conv_cot = inverse * (normed_cot - m1 - normed * m2)
        sums[0] += fold(conv_cot)
        sums[1] += fold(scaled_cot * normed)
        sums[2] += fold(scaled_cot)
        sums[3] += fold(branch_cot.astype(F32))
        sums[4] += fold(g * branch)
        conv[r] = conv_cot

    for q in range(4):
        big[q * 128 : q * 128 + 128, :] = acc_e[0:128, q * 128 : q * 128 + 128].astype(BF)
        big[512 + q * 128 : 640 + q * 128, :] = acc_r[:, q * 128 : q * 128 + 128].T.astype(BF)

    small[...] = jnp.zeros_like(small)
    for b in range(7):

        def step(jb, acc):
            col = pl.multiple_of(jb * 8, 8)
            acc = list(acc)
            cots = [conv[r, pl.ds(col, 8), :] for r in range(8)]
            for row in range(14):
                v = pad[row, pl.ds(col + 5 + b, 8), :]
                for a in range(7):
                    if 0 <= row - a < 8:
                        acc[a] = acc[a] + cots[row - a] * v
            return tuple(acc)

        acc = lax.fori_loop(0, 32, step, (jnp.zeros((8, 128), F32),) * 7)
        for a in range(7):
            small[a * 7 + b : a * 7 + b + 1, :] = jnp.sum(acc[a], 0, keepdims=True)
    for i in range(5):
        small[49 + i : 50 + i, :] = jnp.sum(sums[i], 0, keepdims=True)
    for q in range(4):
        small[54 + q : 55 + q, :] = acc_e[128:129, q * 128 : q * 128 + 128]


def run_block(neighbours, x, cot, halos, params):
    return pl.pallas_call(
        block_kernel,
        out_shape=(
            jax.ShapeDtypeStruct((8, 256, 128), BF),
            jax.ShapeDtypeStruct((1024, 128), BF),
            jax.ShapeDtypeStruct((64, 128), F32),
        ),
        in_specs=[SMEM] + [VMEM] * 15,
        out_specs=(VMEM, VMEM, VMEM),
        scratch_shapes=[
            pltpu.VMEM((14, 272, 128), F32),
            pltpu.VMEM((8, 256, 128), F32),
            pltpu.VMEM((49, 8, 128), F32),
            pltpu.VMEM((144, 512), F32),
            pltpu.VMEM((128, 512), F32),
            pltpu.VMEM((5, 8, 128), F32),
        ],
        compiler_params=pltpu.CompilerParams(vmem_limit_bytes=48 * 1024 * 1024),
        name="block",
    )(neighbours, x, cot, *halos, *params)


def sum_kernel(
    factor, big, small, gath, sgath,
    slots1, sslots1, send2, slots2, parts, fin, sfin,
    s1, r1, ss1, sr1, s2, r2, s3, r3, s4, r4, ss4, sr4, local_sem,
):
    f, t = place()
    hi = t // 16
    s = t % 16
    z = s // 2
    a = hi * 8 + f
    plane = [lax.rem(a + k, 16) for k in range(1, 16)]
    line = [lax.rem(s + k, 16) for k in range(1, 16)]
    stack = [lax.rem(z + k, 8) for k in range(1, 8)]
    faces = [lax.rem(f + k, 8) for k in range(1, 8)]

    def plane_id(p):
        return lax.rem(p, 8), p // 8 * 16 + s

    barrier = pltpu.get_barrier_semaphore()
    for p in plane:
        pl.semaphore_signal(barrier, inc=1, device_id=plane_id(p), device_id_type=MESH)
    for p in line:
        pl.semaphore_signal(barrier, inc=1, device_id=(f, hi * 16 + p), device_id_type=MESH)
    pl.semaphore_wait(barrier, 30)

    def big1(k, p, slot):
        return remote(
            big.at[pl.ds(pl.multiple_of(p * 64, 64), 64)], slots1.at[slot], s1.at[k], r1.at[slot],
            *plane_id(p)
        )

    def small1(k, p, slot):
        rows = pl.ds(pl.multiple_of(lax.rem(p, 8) * 8, 8), 8)
        return remote(small.at[rows], sslots1.at[slot], ss1.at[k], sr1.at[slot], *plane_id(p))

    for k, p in enumerate(plane):
        big1(k, p, a).start()
        small1(k, p, a).start()
    slots1[a] = big[pl.ds(pl.multiple_of(a * 64, 64), 64), :]
    sslots1[a] = small[pl.ds(pl.multiple_of(f * 8, 8), 8), :]
    for k, p in enumerate(plane):
        small1(k, p, p).wait_recv()
    few = sslots1[0]
    for p in range(1, 16):
        few = few + sslots1[p]
    for k, p in enumerate(plane):
        big1(k, p, p).wait_recv()
    total = slots1[0].astype(F32)
    for p in range(1, 16):
        total = total + slots1[p].astype(F32)
    for q in range(8):
        send2[q, 0:8] = total[q * 8 : q * 8 + 8]
        send2[q, 8:16] = few

    def second(k, p, slot):
        return remote(
            send2.at[p // 2], slots2.at[slot], s2.at[k], r2.at[slot], f, hi * 16 + p
        )

    for k, p in enumerate(line):
        second(k, p, s).start()
    slots2[s] = send2[z]
    for k, p in enumerate(line):
        second(k, p, p).wait_recv()
    both = slots2[0]
    for p in range(1, 16):
        both = both + slots2[p]
    both = both * factor
    parts[z] = both[0:8]
    sfin[f] = both[8:16]

    def third(k, q, slot):
        return remote(
            parts.at[z], parts.at[slot], s3.at[k], r3.at[slot], f, hi * 16 + q * 2 + s % 2
        )

    for k, q in enumerate(stack):
        third(k, q, z).start()

    def small4(k, g, slot):
        return remote(sfin.at[f], sfin.at[slot], ss4.at[k], sr4.at[slot], g, t)

    for k, g in enumerate(faces):
        small4(k, g, f).start()
    for k, q in enumerate(stack):
        third(k, q, q).wait_recv()
    fin[a] = parts[...].reshape(64, 128).astype(BF)

    def big4(k, p, slot):
        return remote(fin.at[a], fin.at[slot], s4.at[k], r4.at[slot], *plane_id(p))

    for k, p in enumerate(plane):
        big4(k, p, a).start()
    for k, g in enumerate(faces):
        small4(k, g, g).wait_recv()
    sgath[...] = sfin[...]
    for k, p in enumerate(plane):
        big4(k, p, p).wait_recv()
    gath[...] = fin[...]

    for k, p in enumerate(plane):
        big1(k, p, a).wait_send()
        small1(k, p, a).wait_send()
        big4(k, p, a).wait_send()
    for k, p in enumerate(line):
        second(k, p, s).wait_send()
    for k, q in enumerate(stack):
        third(k, q, z).wait_send()
    for k, g in enumerate(faces):
        small4(k, g, f).wait_send()


def sum_all(big, small, factor):
    dma = pltpu.SemaphoreType.DMA
    return pl.pallas_call(
        functools.partial(sum_kernel, factor),
        out_shape=(
            jax.ShapeDtypeStruct((16, 64, 128), BF),
            jax.ShapeDtypeStruct((8, 8, 128), F32),
        ),
        in_specs=[VMEM, VMEM],
        out_specs=(VMEM, VMEM),
        scratch_shapes=[
            pltpu.VMEM((16, 64, 128), BF),
            pltpu.VMEM((16, 8, 128), F32),
            pltpu.VMEM((8, 16, 128), F32),
            pltpu.VMEM((16, 16, 128), F32),
            pltpu.VMEM((8, 8, 128), F32),
            pltpu.VMEM((16, 64, 128), BF),
            pltpu.VMEM((8, 8, 128), F32),
        ]
        + [dma((16,))] * 12
        + [dma((1,))],
        compiler_params=pltpu.CompilerParams(
            collective_id=1, has_side_effects=True, vmem_limit_bytes=16 * 1024 * 1024
        ),
        name="sum",
    )(big, small)


def unpack_kernel(
    gath, sgath, kernel_grad, cb_grad, gain_grad, nb_grad, we_grad, be_grad, wr_grad, br_grad, ls_grad
):
    rows = gath.reshape(1024, 128)
    few = sgath[...].reshape(64, 128)
    for q in range(4):
        we_grad[:, q * 128 : q * 128 + 128] = rows[q * 128 : q * 128 + 128, :].astype(F32)
        be_grad[q * 128 : q * 128 + 128] = few[54 + q]
    wr_grad[...] = rows[512:1024, :].astype(F32)
    for a in range(7):
        kernel_grad[a] = few[a * 7 : a * 7 + 7]
    for i, ref in enumerate((cb_grad, gain_grad, nb_grad, br_grad, ls_grad)):
        ref[...] = few[49 + i]


def unpack(gath, sgath):
    one = lambda *shape: jax.ShapeDtypeStruct(shape, F32)
    return pl.pallas_call(
        unpack_kernel,
        out_shape=(
            one(7, 7, 128), one(128), one(128), one(128), one(128, 512), one(512),
            one(512, 128), one(128), one(128),
        ),
        in_specs=[VMEM, VMEM],
        out_specs=(VMEM,) * 9,
        name="unpack",
    )(gath, sgath)


def body(
    inputs, kernel, conv_bias, norm_gain, norm_bias, expand_weight, expand_bias,
    reduce_weight, reduce_bias, layer_scale, neighbours, cotangent,
):
    x = inputs[0]
    halos = exchange_halos(neighbours, x)
    params = (
        kernel, conv_bias, norm_gain, norm_bias, expand_weight, expand_bias,
        reduce_weight, reduce_bias, layer_scale,
    )
    out, big, small = run_block(neighbours, x, cotangent[0], halos, params)
    factor = 1.0 / math.sqrt(FACES * 256 * 256)
    gath, sgath = sum_all(big, small, factor)
    return (out[None], *unpack(gath, sgath))


def solution(mesh):
    split = P("face", "tile", None, None)
    return jax.shard_map(
        body,
        mesh=mesh,
        in_specs=(split,) + (P(),) * 10 + (split,),
        out_specs=(split,) + (P(),) * 9,
        check_vma=False,
    )
```

time: 681 us -> 82.9 us (0.12)
  waiting for transfers between devices: 398 us -> 0 us
  blocking collectives: 179 us -> 0 us
  Pallas kernels: 0 us -> 74.4 us
  other arithmetic: 37.4 us -> 0 us
  between operations: 22.5 us -> 0.73 us
  starting transfers between devices: 16.5 us -> 0 us
  matrix products: 12.5 us -> 0 us
    psum x2 -> x0, waiting for transfers between devices: 392 us -> none  [the longest x1 245 us: body(): lax.psum((grads[0], grads[1], grads[2], grads[3], grads[4], grads[5], gra...]
    all_gather x3 -> x0, blocking collectives: 103 us -> none  [the longest x1 37.8 us: body(): lax.all_gather(east_piece, 'tile', axis=1, tiled=True)]
    psum x1 -> x0, blocking collectives: 76.5 us -> none  [body(): lax.psum((grads[0], grads[1], grads[2], grads[3], grads[4], grads[5], gra...]
    pallas_call x0 -> x4, Pallas kernels: none -> 74.4 us  [the longest x1 28.8 us: sum_all(): pl.pallas_call(functools.partial(sum_kernel, factor), out_shape=(jax.Shap...]
    reduce_sum x7 -> x0, other arithmetic: 24.2 us -> none  [the longest x1 10.7 us: block_pass(): mean = jnp.mean(flat, -1, keepdims=True)]
    dot_general x6 -> x0, matrix products: 12.5 us -> none  [the longest x2 6.56 us: contract_cols(): lax.dot_general(left, right, (((1,), (1,)), ((), ())), preferred_element_...]
    all_to_all x2 -> x0, starting transfers between devices: 9.51 us -> none  [the longest x1 6.13 us: body(): lax.all_to_all(polar_part, 'face', split_axis=0, concat_axis=0, tiled=True)]
    mul x9 -> x0, other arithmetic: 7.11 us -> none  [body(): result = [item * factor for item in summed]]
  transfers between devices with their start and end apart: 6 -> 0, of which waited for: 3 -> 0; matrix products, arithmetic and copies ran while one was open for 2% -> 0% of each run, Pallas kernels for 0% -> 0%
where the time goes in v1:
time: 82.9 us; the launch traced here: 82.5 us
  Pallas kernels  74.4 us (90%)
  local copies, waits for them, and re-layouts  7.4 us (9%)
    pallas_call x1, Pallas kernels, sum_all(): pl.pallas_call(functools.partial(sum_kernel, factor), out_shape=(jax.Shap...  28.8 us
    pallas_call x1, Pallas kernels, run_block(): pl.pallas_call(block_kernel, out_shape=(jax.ShapeDtypeStruct((8, 256, 128...  22.1 us
    pallas_call x1, Pallas kernels, exchange_halos(): pl.pallas_call(halo_kernel, out_shape=(jax.ShapeDtypeStruct((3, 256, 128)...  21.7 us
    unnamed x29, local copies, waits for them, and re-layouts  7.4 us
    pallas_call x1, Pallas kernels, unpack(): pl.pallas_call(unpack_kernel, out_shape=(one(7, 7, 128), one(128), one(12...  1.79 us

profile of v1, /device:TPU:1, one launch (start us, length us, event | category | flops | bytes accessed | tf_op | source)
XLA Modules:
  0.0 82.5 jit_solution(17563488740895874502)
XLA Ops:
  0.6 0.8 copy.23.nbr
  1.4 0.0 copy-start
  1.4 1.0 %copy-done = bf16[1,8,256,128]{3,2,1,0:T(8,128)(2,1)S(1)} copy-done((bf16[1,8,256,128]{3,2,1,0:T(8,128)(2,1)S(1)}, bf16[1,8,256,128]{3,2,1,0:T(8,128)(2,1)}, u32[]{:S(2)}) %copy-start) | copy-done | bytes 524312
  2.5 0.0 copy-start.1
  2.5 21.7 %halo.1 = (bf16[3,256,128]{2,1,0:T(8,128)(2,1)S(1)}, bf16[3,256,128]{2,1,0:T(8,128)(2,1)S(1)}, bf16[8,3,32,128]{3,2,1,0:T(8,128)(2,1)S(1)}, bf16[6,3,16,128]{3,2,1,0:T(8,128)(2,1)S(1)}) custom-call(s32[8,4,3]{2,1,0:T(4,128)S(1)} %copy.23.nbr, bf16[8,256,128]{2,1,0:T(8,128)(2,1)S(1)} %bitcast.3), custom_call_target="tpu_custom_call" | custom-call | tf_op jit(solution)/shard_map/halo/pallas_call | solution.py:247
  24.2 0.0 copy-start.12
  24.2 0.0 copy-start.13
  24.2 0.0 copy-start.8
  24.3 0.0 copy-start.9
  24.3 0.0 copy-start.10
  24.3 0.0 copy-start.11
  24.3 0.0 copy-done.1
  24.3 0.6 copy-done.12
  24.9 0.0 copy-done.13
  24.9 0.0 copy-done.8
  24.9 0.0 copy-done.9
  24.9 0.0 copy-done.10
  24.9 0.0 copy-done.11
  25.0 0.0 copy-start.2
  25.0 1.0 %copy-done.2 = bf16[1,8,256,128]{3,2,1,0:T(8,128)(2,1)S(1)} copy-done((bf16[1,8,256,128]{3,2,1,0:T(8,128)(2,1)S(1)}, bf16[1,8,256,128]{3,2,1,0:T(8,128)(2,1)}, u32[]{:S(2)}) %copy-start.2) | copy-done | bytes 524312
  26.0 0.0 copy-start.4
  26.0 0.9 %copy-done.4 = bf16[128,512]{1,0:T(8,128)(2,1)S(1)} copy-done((bf16[128,512]{1,0:T(8,128)(2,1)S(1)}, bf16[128,512]{1,0:T(8,128)(2,1)}, u32[]{:S(2)}) %copy-start.4) | copy-done | bytes 131096
  26.9 0.9 %copy-done.5 = bf16[512,128]{1,0:T(8,128)(2,1)S(1)} copy-done((bf16[512,128]{1,0:T(8,128)(2,1)S(1)}, bf16[512,128]{1,0:T(8,128)(2,1)}, u32[]{:S(2)}) %copy-start.5) | copy-done | bytes 131096
  27.8 0.0 copy-start.7
  27.8 0.7 copy-done.7
  28.6 22.1 %block.1 = (bf16[8,256,128]{2,1,0:T(8,128)(2,1)}, bf16[1024,128]{1,0:T(8,128)(2,1)S(1)}, f32[64,128]{1,0:T(8,128)S(1)}) custom-call(s32[8,4,3]{2,1,0:T(4,128)S(1)} %copy.23.nbr, bf16[8,256,128]{2,1,0:T(8,128)(2,1)S(1)} %bitcast.4, bf16[8,256,128]{2,1,0:T(8,128)(2,1)S(1)} %bitcast.5, bf16[3,256,128]{2,1,0:T(8,128)(2,1)S(1)} %get-tuple-element.28.top, ...), custom_call_target="tpu_custom_call" | custom-call | tf_op jit(solution)/shard_map/block/pallas_call | solution.py:428
  50.6 28.8 %sum.1 = (bf16[16,64,128]{2,1,0:T(8,128)(2,1)S(1)}, f32[8,8,128]{2,1,0:T(8,128)S(1)}) custom-call(bf16[1024,128]{1,0:T(8,128)(2,1)S(1)} %get-tuple-element.33.big, f32[64,128]{1,0:T(8,128)S(1)} %get-tuple-element.34.small), custom_call_target="tpu_custom_call" | custom-call | tf_op jit(solution)/shard_map/sum/pallas_call | solution.py:564
  79.4 0.0 copy-start.3
  79.4 0.7 copy-done.3
  80.1 0.0 copy-start.6
  80.1 0.6 copy-done.6
  80.7 1.8 %unpack.1 = (f32[7,7,128]{2,1,0:T(8,128)}, f32[128]{0:T(128)}, f32[128]{0:T(128)}, f32[128]{0:T(128)}, f32[128,512]{1,0:T(8,128)}, /*index=5*/f32[512]{0:T(512)}...) custom-call(bf16[16,64,128]{2,1,0:T(8,128)(2,1)} %copy-done.3, f32[8,8,128]{2,1,0:T(8,128)} %copy-done.6), custom_call_target="tpu_custom_call" | custom-call | tf_op jit(solution)/shard_map/unpack/pallas_call | solution.py:607
  (1 shorter events, 0.0 us)
Async XLA Ops:
  1.4 1.0 %copy-start = (bf16[1,8,256,128]{3,2,1,0:T(8,128)(2,1)S(1)}, bf16[1,8,256,128]{3,2,1,0:T(8,128)(2,1)}, u32[]{:S(2)}) copy-start(bf16[1,8,256,128]{3,2,1,0:T(8,128)(2,1)} %param.12) | copy-start | bytes 1572868
  2.5 21.8 %copy-start.1 = (bf16[1,8,256,128]{3,2,1,0:T(8,128)(2,1)S(1)}, bf16[1,8,256,128]{3,2,1,0:T(8,128)(2,1)}, u32[]{:S(2)}) copy-start(bf16[1,8,256,128]{3,2,1,0:T(8,128)(2,1)} %param.12) | copy-start | bytes 1572868
  24.2 0.7 copy-start.12
  24.2 0.7 copy-start.13
  24.2 0.7 copy-start.8
  24.3 0.7 copy-start.9
  24.3 0.7 copy-start.10
  24.3 0.7 copy-start.11
  25.0 1.0 %copy-start.2 = (bf16[1,8,256,128]{3,2,1,0:T(8,128)(2,1)S(1)}, bf16[1,8,256,128]{3,2,1,0:T(8,128)(2,1)}, u32[]{:S(2)}) copy-start(bf16[1,8,256,128]{3,2,1,0:T(8,128)(2,1)} %param.23) | copy-start | bytes 1572868
  26.0 0.9 %copy-start.4 = (bf16[128,512]{1,0:T(8,128)(2,1)S(1)}, bf16[128,512]{1,0:T(8,128)(2,1)}, u32[]{:S(2)}) copy-start(bf16[128,512]{1,0:T(8,128)(2,1)} %we.1) | copy-start | bytes 393220
  26.9 0.9 %copy-start.5 = (bf16[512,128]{1,0:T(8,128)(2,1)S(1)}, bf16[512,128]{1,0:T(8,128)(2,1)}, u32[]{:S(2)}) copy-start(bf16[512,128]{1,0:T(8,128)(2,1)} %wr.1) | copy-start | bytes 393220
  27.8 0.7 copy-start.7
  79.4 0.7 copy-start.3
  80.1 0.6 copy-start.6

commit v2 on v1

v2 whole, which is shorter than its diff:
```python
import functools
import math

import jax
import jax.numpy as jnp
from jax import lax
from jax.experimental import pallas as pl
from jax.experimental.pallas import tpu as pltpu
from jax.sharding import PartitionSpec as P

EPS = 1e-06
MESH = pl.DeviceIdType.MESH
BF = jnp.bfloat16
F32 = jnp.float32
ROOT = math.sqrt(2.0 / math.pi)
CUBE = 0.044715
FACES = 8
TILES = 32
VMEM = pl.BlockSpec(memory_space=pltpu.VMEM)
SMEM = pl.BlockSpec(memory_space=pltpu.SMEM)
ANY = pl.BlockSpec(memory_space=pl.ANY)


def place():
    return lax.axis_index("face"), lax.axis_index("tile")


def remote(src, dst, send, recv, face, tile):
    return pltpu.make_async_remote_copy(
        src_ref=src, dst_ref=dst, send_sem=send, recv_sem=recv,
        device_id=(face, tile), device_id_type=MESH,
    )


def nt(left, right):
    return lax.dot_general(left, right, (((1,), (1,)), ((), ())), preferred_element_type=F32)


def nn(left, right):
    return lax.dot_general(left, right, (((1,), (0,)), ((), ())), preferred_element_type=F32)


def one_hot(rows, cols, index):
    r = lax.broadcasted_iota(jnp.int32, (rows, cols), 0)
    c = lax.broadcasted_iota(jnp.int32, (rows, cols), 1)
    return jnp.where(c == index(r), 1.0, 0.0).astype(BF)


def fold(v):
    rows, chans = v.shape
    return jnp.sum(v.reshape(rows // 8, 8, chans), 0)


def main_kernel(
    factor,
    nbr, x_hbm, cot_hbm, kern_hbm, cb_hbm, gain_hbm, nb_hbm, we_hbm, be_hbm, wr_hbm, br_hbm, ls_hbm,
    out_hbm, gath, sgath,
    x, cot, kern, cb, gain, nb, we, be, wr, br, ls, out,
    top, bot, hbuf, side, pieces, chosen, nsbuf, nsend,
    pad, conv, taps, act, acc_e, acc_r, sums,
    bigf, half, bigb, slots1, slotsz, small, sslots1, sslots2, few_ref,
    load_sem, out_sem, row_send, row_recv, piece_send, piece_recv, band_send, band_recv,
    side_send, side_recv, fwd_send, fwd_recv, local_sem,
    core_sem, s1, r1, sz, rz, s4, r4, ss1, sr1, ss2, sr2, ss4, sr4,
):
    f, t = place()
    last = TILES - 1
    mirror = last - t
    is_first = t == 0
    is_last = t == last
    has_up = t > 0
    has_down = t < last
    mir_up = jnp.logical_and(mirror < last, mirror + 1 != t)
    mir_down = jnp.logical_and(mirror > 0, mirror - 1 != t)
    edge = jnp.logical_or(is_first, is_last)
    hi = t // 16
    s = t % 16
    z = s // 2
    core = s % 2
    twin = t + 1 - 2 * core
    a = hi * 8 + f
    others = [lax.rem(f + k, FACES) for k in range(1, FACES)]
    plane = [lax.rem(a + k, 16) for k in range(1, 16)]
    line = [lax.rem(s + k, 16) for k in range(1, 16)]
    stack = [lax.rem(z + k, 8) for k in range(1, 8)]

    def plane_id(p):
        return lax.rem(p, 8), p // 8 * 16 + s

    loads = [
        pltpu.make_async_copy(src, dst, load_sem.at[i])
        for i, (src, dst) in enumerate(
            (
                (x_hbm, x), (kern_hbm, kern), (cb_hbm, cb), (cot_hbm, cot), (we_hbm, we), (wr_hbm, wr),
                (gain_hbm, gain), (nb_hbm, nb), (be_hbm, be), (br_hbm, br), (ls_hbm, ls),
            )
        )
    ]
    for load in loads:
        load.start()

    barrier = pltpu.get_barrier_semaphore()

    def hello(face, tile):
        pl.semaphore_signal(barrier, inc=1, device_id=(face, tile), device_id_type=MESH)

    for p in plane:
        hello(*plane_id(p))
    for p in line:
        hello(f, hi * 16 + p)
    hello(f, mirror)

    @pl.when(has_up)
    def _():
        hello(f, t - 1)

    @pl.when(has_down)
    def _():
        hello(f, t + 1)

    @pl.when(mir_up)
    def _():
        hello(f, mirror + 1)

    @pl.when(mir_down)
    def _():
        hello(f, mirror - 1)

    @pl.when(edge)
    def _():
        for g in range(FACES):
            hello(g, mirror)

    loads[0].wait()
    for d in range(3):
        west = x[:, d : d + 1, :].astype(F32).reshape(8, 128)
        east = x[:, 255 - d : 256 - d, :].astype(F32).reshape(8, 128)
        pieces[f, d] = jnp.concatenate([west, east], 0).astype(BF)
    pad[3:11, 8:264, :] = x[...].astype(F32)
    for load in loads[1:3]:
        load.wait()
    for i in range(7):
        for j in range(7):
            taps[i * 7 + j] = jnp.broadcast_to(kern[i, j : j + 1, :], (8, 128))
    bias = jnp.broadcast_to(cb[...].reshape(1, 128), (8, 128))

    def convolve(col, acc, out_rows, in_rows):
        acc = dict(zip(out_rows, acc))
        for j in range(7):
            for row in in_rows:
                hit = [r for r in out_rows if 0 <= row - r < 7]
                if hit:
                    v = pad[row, pl.ds(col + 5 + j, 8), :]
                    for r in hit:
                        acc[r] = acc[r] + taps[(row - r) * 7 + j] * v
        return [acc[r] for r in out_rows]

    @pl.loop(2, 30)
    def _(jb):
        col = pl.multiple_of(jb * 8, 8)
        for r, v in enumerate(convolve(col, [bias] * 8, range(8), range(3, 11))):
            conv[r, pl.ds(col, 8), :] = v

    one = lambda cond: cond.astype(jnp.int32)
    count = 31 + one(has_up) + one(has_down) + one(mir_up) + one(mir_down) + 8 * one(edge)
    pl.semaphore_wait(barrier, count)

    def band_copy(rows, k, g):
        return remote(
            x.at[pl.ds(rows, 3), pl.ds(pl.multiple_of(g * 32, 32), 32), :], nsbuf.at[f],
            band_send.at[k], band_recv.at[f], g, t,
        )

    def piece_copy(k, g):
        return remote(pieces.at[f], pieces.at[f], piece_send.at[k], piece_recv.at[f], g, t)

    def up_copy():
        return remote(x.at[pl.ds(0, 3)], bot, row_send.at[0], row_recv.at[0], f, t - 1)

    def down_copy():
        return remote(x.at[pl.ds(5, 3)], top, row_send.at[1], row_recv.at[1], f, t + 1)

    for rows, cond in ((0, is_first), (5, is_last)):

        @pl.when(cond)
        def _(rows=rows):
            for k, g in enumerate(others):
                band_copy(rows, k, g).start()
            nsbuf[f] = x[rows : rows + 3, pl.ds(pl.multiple_of(f * 32, 32), 32), :]

    for k, g in enumerate(others):
        piece_copy(k, g).start()

    @pl.when(has_up)
    def _():
        up_copy().start()

    @pl.when(has_down)
    def _():
        down_copy().start()

    for load in loads[3:]:
        load.wait()

    def forward(g):
        return remote(nsend.at[g], hbuf.at[f], fwd_send.at[g], fwd_recv.at[f], g, mirror)

    def side_copy(slot, tile):
        return remote(chosen, side.at[slot], side_send.at[slot], side_recv.at[slot], f, tile)

    def phase_two():
        for side_id, rows, cond in ((0, 5, is_last), (2, 0, is_first)):

            @pl.when(cond)
            def _(side_id=side_id, rows=rows):
                for k, g in enumerate(others):
                    remote(
                        x.at[pl.ds(rows, 3), pl.ds(pl.multiple_of(g * 32, 32), 32), :], nsbuf.at[g],
                        band_send.at[k], band_recv.at[g], g, t,
                    ).wait_recv()
                for g in range(FACES):
                    nsend[g] = nsbuf[nbr[g, side_id, 0]]
                    forward(g).start()

        for k, g in enumerate(others):
            remote(pieces.at[f], pieces.at[g], piece_send.at[k], piece_recv.at[g], g, t).wait_recv()
        from_west = pieces[nbr[f, 3, 0]]
        from_east = pieces[nbr[f, 1, 0]]
        chosen[...] = jnp.concatenate(
            [from_west.astype(F32)[:, 8:16], from_east.astype(F32)[:, 0:8]], 1
        ).astype(BF)
        side_copy(4, mirror).start()

        @pl.when(has_down)
        def _():
            side_copy(0, t + 1).start()

        @pl.when(has_up)
        def _():
            side_copy(2, t - 1).start()

        @pl.when(mir_up)
        def _():
            side_copy(3, mirror + 1).start()

        @pl.when(mir_down)
        def _():
            side_copy(5, mirror - 1).start()

        side[1] = chosen[...]

        @pl.when(mirror + 1 == t)
        def _():
            side[3] = chosen[...]

        @pl.when(mirror - 1 == t)
        def _():
            side[5] = chosen[...]

    def polar(flag, rows):
        for g in range(FACES):
            remote(
                nsend.at[g], hbuf.at[g], fwd_send.at[g], fwd_recv.at[g], g, mirror
            ).wait_recv()
        turn = one_hot(256, 256, lambda r: 255 - r)
        for d in range(3):
            band = jnp.concatenate([hbuf[k, d] for k in range(8)], 0)
            turned = nn(turn, band)
            pad[rows[d], 8:264, :] = jnp.where(flag == 1, turned, band.astype(F32))

    def finish(out_rows, in_rows):
        @pl.loop(2, 30)
        def _(jb):
            col = pl.multiple_of(jb * 8, 8)
            acc = [conv[r, pl.ds(col, 8), :] for r in out_rows]
            for r, v in zip(out_rows, convolve(col, acc, out_rows, in_rows)):
                conv[r, pl.ds(col, 8), :] = v

    def finish_top():
        @pl.when(has_up)
        def _():
            down_copy().wait_recv()
            pad[0:3, 8:264, :] = top[...].astype(F32)

        @pl.when(is_first)
        def _():
            polar(nbr[f, 0, 2], (0, 1, 2))

        finish(range(0, 3), range(0, 3))

    def finish_bottom():
        @pl.when(has_down)
        def _():
            up_copy().wait_recv()
            pad[11:14, 8:264, :] = bot[...].astype(F32)

        @pl.when(is_last)
        def _():
            polar(nbr[f, 2, 2], (11, 12, 13))

        finish(range(5, 8), range(11, 14))

    acc_e[...] = jnp.zeros_like(acc_e)
    acc_r[...] = jnp.zeros_like(acc_r)
    sums[...] = jnp.zeros_like(sums)
    mean_of = jnp.full((128, 128), 1.0 / 128, BF)
    vec = lambda ref: ref[...].reshape(1, -1)

    def mlp(c, cotangent, rows):
        count = c.shape[0]
        centred = c - nn(c.astype(BF), mean_of)
        variance = nn((centred * centred).astype(BF), mean_of)
        inverse = lax.rsqrt(variance + EPS)
        normed = centred * inverse
        scaled = (normed * vec(gain) + vec(nb)).astype(BF)
        branch_cot = (cotangent.astype(F32) * vec(ls)).astype(BF)
        hidden = nn(scaled, we[...]) + vec(be)
        active_cot = nt(branch_cot, wr[...])
        square = hidden * hidden
        gate = 0.5 + 0.5 * jnp.tanh(hidden * (ROOT + (ROOT * CUBE) * square))
        active = hidden * gate
        active_low = active.astype(BF)
        slope = gate + active * (1.0 - gate) * (2.0 * ROOT + (6.0 * ROOT * CUBE) * square)
        hidden_cot = (active_cot * slope).astype(BF)
        act[rows, :] = active_low
        left = jnp.concatenate([scaled.T, jnp.ones((16, count), BF)], 0)
        acc_e[...] += nn(left, hidden_cot)
        acc_r[...] += nn(branch_cot.T, active_low)
        scaled_cot = nt(hidden_cot, we[...])
        normed_cot = scaled_cot * vec(gain)
        m1 = nn(normed_cot.astype(BF), mean_of)
        m2 = nn((normed_cot * normed).astype(BF), mean_of)
        conv_cot = inverse * (normed_cot - m1 - normed * m2)
        sums[0] += fold(conv_cot)
        sums[1] += fold(scaled_cot * normed)
        sums[2] += fold(scaled_cot)
        sums[3] += fold(branch_cot.astype(F32))
        return conv_cot

    low_first = t < 16

    def row_of(i):
        return jnp.where(low_first, 4 - 4 * i, 4 * i)

    @pl.loop(0, 2)
    def _(i):
        r0 = row_of(i)

        @pl.when(r0 == 0)
        def _():
            finish_top()

        @pl.when(r0 == 4)
        def _():
            finish_bottom()

        @pl.when(i == 0)
        def _():
            phase_two()

        four = pl.ds(r0, 4)
        got = mlp(
            conv[four, 16:240, :].reshape(896, 128),
            cot[four, 16:240, :].reshape(896, 128),
            pl.ds(pl.multiple_of(i * 896, 128), 896),
        )
        conv[four, 16:240, :] = got.reshape(4, 224, 128)

    side_copy(4, mirror).wait_recv()

    @pl.when(has_up)
    def _():
        side_copy(0, t - 1).wait_recv()

    @pl.when(has_down)
    def _():
        side_copy(2, t + 1).wait_recv()

    @pl.when(mir_up)
    def _():
        side_copy(3, mirror + 1).wait_recv()

    @pl.when(mir_down)
    def _():
        side_copy(5, mirror - 1).wait_recv()

    @pl.when(is_first)
    def _():
        side[0] = jnp.zeros((3, 16, 128), BF)
        side[3] = jnp.zeros((3, 16, 128), BF)

    @pl.when(is_last)
    def _():
        side[2] = jnp.zeros((3, 16, 128), BF)
        side[5] = jnp.zeros((3, 16, 128), BF)

    turn = one_hot(24, 24, lambda r: r // 8 * 8 + 7 - r % 8)
    for d in range(3):
        slots = [side[i, d].astype(F32) for i in range(6)]
        for first, side_id, col in ((0, 3, 7 - d), (8, 1, 264 + d)):
            straight = jnp.concatenate([slots[i][first : first + 8] for i in (0, 1, 2)], 0)
            turned = jnp.concatenate([slots[i][first : first + 8] for i in (3, 4, 5)], 0)
            turned = nn(turn, turned.astype(BF))
            halo = jnp.where(nbr[f, side_id, 2] == 1, turned, straight)
            pad[0:14, col : col + 1, :] = halo[5:19].reshape(14, 1, 128)

    @pl.loop(0, 4)
    def _(i):
        col = pl.multiple_of((i + i // 2 * 28) * 8, 8)
        for r, v in enumerate(convolve(col, [bias] * 8, range(8), range(14))):
            conv[r, pl.ds(col, 8), :] = v

    got = mlp(
        jnp.concatenate([conv[:, 0:16, :], conv[:, 240:256, :]], 1).reshape(256, 128),
        jnp.concatenate([cot[:, 0:16, :], cot[:, 240:256, :]], 1).reshape(256, 128),
        pl.ds(1792, 256),
    ).reshape(8, 32, 128)
    conv[:, 0:16, :] = got[:, 0:16]
    conv[:, 240:256, :] = got[:, 16:32]

    scale = jnp.zeros((8, 128), F32)
    for q in range(4):
        cols = slice(q * 128, q * 128 + 128)
        bigf[q * 128 : q * 128 + 128, :] = acc_e[0:128, cols]
        turned = acc_r[:, cols].T
        bigf[512 + q * 128 : 640 + q * 128, :] = turned
        scale = scale + fold(turned * wr[cols, :].astype(F32))

    def halve(part):
        return remote(
            bigf.at[pl.ds(pl.multiple_of(part * 512, 512), 512)], half, core_sem.at[0], core_sem.at[1],
            f, twin,
        )

    halve(1 - core).start()

    small[...] = jnp.zeros_like(small)
    totals = [jnp.sum(sums[i], 0, keepdims=True) for i in range(4)]
    totals.append((jnp.sum(scale, 0, keepdims=True) + vec(br) * totals[3]) / vec(ls))
    for i in range(5):
        small[49 + i : 50 + i, :] = totals[i]
    for q in range(4):
        small[54 + q : 55 + q, :] = acc_e[128:129, q * 128 : q * 128 + 128]

    def kernel_grad(first, stop):
        @pl.loop(first, stop)
        def _(j):
            def step(jb, acc):
                col = pl.multiple_of(jb * 8, 8)
                acc = list(acc)
                cots = [conv[r, pl.ds(col, 8), :] for r in range(8)]
                for row in range(14):
                    v = pad[row, pl.ds(col + 5 + j, 8), :]
                    for i in range(7):
                        if 0 <= row - i < 8:
                            acc[i] = acc[i] + cots[row - i] * v
                return tuple(acc)

            acc = lax.fori_loop(0, 32, step, (jnp.zeros((8, 128), F32),) * 7)
            for i in range(7):
                small[pl.ds(i * 7 + j, 1), :] = jnp.sum(acc[i], 0, keepdims=True)

    kernel_grad(0, 2)
    halve(core).wait_recv()
    mine = bigf[pl.ds(pl.multiple_of(core * 512, 512), 512), :] + half[...]
    bigb[...] = mine.astype(BF).reshape(16, 32, 128)

    def big1(k, p, slot):
        return remote(bigb.at[p], slots1.at[slot], s1.at[k], r1.at[slot], *plane_id(p))

    for k, p in enumerate(plane):
        big1(k, p, a).start()
    slots1[a] = bigb[a]
    kernel_grad(2, 7)

    def small1(k, p, slot):
        rows = pl.ds(pl.multiple_of(lax.rem(p, 8) * 8, 8), 8)
        return remote(small.at[rows], sslots1.at[slot], ss1.at[k], sr1.at[slot], *plane_id(p))

    for k, p in enumerate(plane):
        small1(k, p, a).start()
    sslots1[a] = small[pl.ds(pl.multiple_of(f * 8, 8), 8), :]

    for k, p in enumerate(plane):
        big1(k, p, p).wait_recv()
    total = slots1[0].astype(F32)
    for p in range(1, 16):
        total = total + slots1[p].astype(F32)
    slotsz[z] = total.astype(BF)

    def bigz(k, q, slot):
        return remote(
            slotsz.at[z], slotsz.at[slot], sz.at[k], rz.at[slot], f, hi * 16 + q * 2 + core
        )

    for k, q in enumerate(stack):
        bigz(k, q, z).start()

    def output(rows, residual):
        branch = nn(act[rows, :], wr[...]) + vec(br)
        return (residual.astype(F32) + vec(ls) * branch).astype(BF)

    @pl.loop(0, 2)
    def _(i):
        four = pl.ds(row_of(i), 4)
        rows = pl.ds(pl.multiple_of(i * 896, 128), 896)
        out[four, 16:240, :] = output(rows, x[four, 16:240, :].reshape(896, 128)).reshape(4, 224, 128)

    sides = output(
        pl.ds(1792, 256),
        jnp.concatenate([x[:, 0:16, :], x[:, 240:256, :]], 1).reshape(256, 128),
    ).reshape(8, 32, 128)
    out[:, 0:16, :] = sides[:, 0:16]
    out[:, 240:256, :] = sides[:, 16:32]
    store = pltpu.make_async_copy(out, out_hbm, out_sem.at[0])
    store.start()

    for k, p in enumerate(plane):
        small1(k, p, p).wait_recv()
    few = sslots1[0]
    for p in range(1, 16):
        few = few + sslots1[p]
    few_ref[...] = few

    def small2(k, p, slot):
        return remote(few_ref, sslots2.at[slot], ss2.at[k], sr2.at[slot], f, hi * 16 + p)

    for k, p in enumerate(line):
        small2(k, p, s).start()
    sslots2[s] = few

    for k, q in enumerate(stack):
        bigz(k, q, q).wait_recv()
    total = slotsz[0].astype(F32)
    for q in range(1, 8):
        total = total + slotsz[q].astype(F32)
    gath[core, a] = (total * factor).astype(BF)

    def big4(k, p, slot):
        return remote(gath.at[core, a], gath.at[core, slot], s4.at[k], r4.at[slot], *plane_id(p))

    for k, p in enumerate(plane):
        big4(k, p, a).start()

    for k, p in enumerate(line):
        small2(k, p, p).wait_recv()
    few = sslots2[0]
    for p in range(1, 16):
        few = few + sslots2[p]
    sgath[f] = few * factor

    def small4(k, g, slot):
        return remote(sgath.at[f], sgath.at[slot], ss4.at[k], sr4.at[slot], g, t)

    for k, g in enumerate(others):
        small4(k, g, f).start()

    for k, p in enumerate(plane):
        big4(k, p, p).wait_recv()

    def share(part):
        return remote(gath.at[part], gath.at[part], core_sem.at[2], core_sem.at[3], f, twin)

    share(core).start()
    for k, g in enumerate(others):
        small4(k, g, g).wait_recv()
    share(1 - core).wait_recv()

    store.wait()
    for k, g in enumerate(others):
        piece_copy(k, g).wait_send()
        small4(k, g, f).wait_send()
    side_copy(4, mirror).wait_send()

    @pl.when(has_up)
    def _():
        side_copy(2, t - 1).wait_send()
        up_copy().wait_send()

    @pl.when(has_down)
    def _():
        side_copy(0, t + 1).wait_send()
        down_copy().wait_send()

    @pl.when(mir_up)
    def _():
        side_copy(3, mirror + 1).wait_send()

    @pl.when(mir_down)
    def _():
        side_copy(5, mirror - 1).wait_send()

    @pl.when(edge)
    def _():
        for k, g in enumerate(others):
            band_copy(0, k, g).wait_send()
        for g in range(FACES):
            forward(g).wait_send()

    halve(1 - core).wait_send()
    share(core).wait_send()
    for k, p in enumerate(plane):
        big1(k, p, a).wait_send()
        small1(k, p, a).wait_send()
        big4(k, p, a).wait_send()
    for k, p in enumerate(line):
        small2(k, p, s).wait_send()
    for k, q in enumerate(stack):
        bigz(k, q, z).wait_send()


def run_main(factor, neighbours, *operands):
    dma = pltpu.SemaphoreType.DMA
    shape = lambda *dims: jax.ShapeDtypeStruct(dims, BF)
    return pl.pallas_call(
        functools.partial(main_kernel, factor),
        out_shape=(
            shape(8, 256, 128),
            shape(2, 16, 32, 128),
            jax.ShapeDtypeStruct((8, 8, 128), F32),
        ),
        in_specs=[SMEM] + [ANY] * 11,
        out_specs=(ANY, VMEM, VMEM),
        scratch_shapes=[pltpu.VMEM(item.shape, item.dtype) for item in operands]
        + [
            pltpu.VMEM((8, 256, 128), BF),
            pltpu.VMEM((3, 256, 128), BF),
            pltpu.VMEM((3, 256, 128), BF),
            pltpu.VMEM((8, 3, 32, 128), BF),
            pltpu.VMEM((6, 3, 16, 128), BF),
            pltpu.VMEM((8, 3, 16, 128), BF),
            pltpu.VMEM((3, 16, 128), BF),
            pltpu.VMEM((8, 3, 32, 128), BF),
            pltpu.VMEM((8, 3, 32, 128), BF),
            pltpu.VMEM((14, 272, 128), F32),
            pltpu.VMEM((8, 256, 128), F32),
            pltpu.VMEM((49, 8, 128), F32),
            pltpu.VMEM((2048, 512), BF),
            pltpu.VMEM((144, 512), F32),
            pltpu.VMEM((128, 512), F32),
            pltpu.VMEM((4, 8, 128), F32),
            pltpu.VMEM((1024, 128), F32),
            pltpu.VMEM((512, 128), F32),
            pltpu.VMEM((16, 32, 128), BF),
            pltpu.VMEM((16, 32, 128), BF),
            pltpu.VMEM((8, 32, 128), BF),
            pltpu.VMEM((64, 128), F32),
            pltpu.VMEM((16, 8, 128), F32),
            pltpu.VMEM((16, 8, 128), F32),
            pltpu.VMEM((8, 128), F32),
            dma((11,)), dma((1,)), dma((2,)), dma((2,)), dma((8,)), dma((8,)), dma((8,)), dma((8,)),
            dma((6,)), dma((6,)), dma((8,)), dma((8,)), dma((2,)),
            dma((4,)),
        ]
        + [dma((16,))] * 12,
        compiler_params=pltpu.CompilerParams(
            collective_id=0, has_side_effects=True, vmem_limit_bytes=56 * 1024 * 1024
        ),
        name="main",
    )(neighbours, *operands)


def unpack_kernel(
    raw, gath, sgath,
    out, kernel_grad, cb_grad, gain_grad, nb_grad, we_grad, be_grad, wr_grad, br_grad, ls_grad,
    sem,
):
    copy = pltpu.make_async_copy(raw, out, sem.at[0])
    copy.start()
    rows = gath.reshape(1024, 128)
    few = sgath[...].reshape(64, 128)
    for q in range(4):
        we_grad[:, q * 128 : q * 128 + 128] = rows[q * 128 : q * 128 + 128, :].astype(F32)
        be_grad[q * 128 : q * 128 + 128] = few[54 + q]
    wr_grad[...] = rows[512:1024, :].astype(F32)
    for i in range(7):
        kernel_grad[i] = few[i * 7 : i * 7 + 7]
    for i, ref in enumerate((cb_grad, gain_grad, nb_grad, br_grad, ls_grad)):
        ref[...] = few[49 + i]
    copy.wait()


def unpack(raw, gath, sgath):
    one = lambda *shape: jax.ShapeDtypeStruct(shape, F32)
    return pl.pallas_call(
        unpack_kernel,
        out_shape=(
            jax.ShapeDtypeStruct(raw.shape, raw.dtype),
            one(7, 7, 128), one(128), one(128), one(128), one(128, 512), one(512),
            one(512, 128), one(128), one(128),
        ),
        in_specs=[ANY, VMEM, VMEM],
        out_specs=(ANY,) + (VMEM,) * 9,
        scratch_shapes=[pltpu.SemaphoreType.DMA((1,))],
        name="unpack",
    )(raw, gath, sgath)


def body(
    inputs, kernel, conv_bias, norm_gain, norm_bias, expand_weight, expand_bias,
    reduce_weight, reduce_bias, layer_scale, neighbours, cotangent,
):
    factor = 1.0 / math.sqrt(FACES * 256 * 256)
    raw, gath, sgath = run_main(
        factor, neighbours, inputs[0], cotangent[0], kernel, conv_bias, norm_gain, norm_bias,
        expand_weight, expand_bias, reduce_weight, reduce_bias, layer_scale,
    )
    out, *grads = unpack(raw, gath, sgath)
    return (out[None], *grads)


def solution(mesh):
    split = P("face", "tile", None, None)
    return jax.shard_map(
        body,
        mesh=mesh,
        in_specs=(split,) + (P(),) * 10 + (split,),
        out_specs=(split,) + (P(),) * 9,
        check_vma=False,
    )
```

time: 82.9 us -> 72.3 us (0.87)
  local copies, waits for them, and re-layouts: 7.4 us -> 1.39 us
  Pallas kernels: 74.4 us -> 70 us
    unnamed x29 -> x1, local copies, waits for them, and re-layouts: 7.4 us -> 1.39 us
    pallas_call x4 -> x2, Pallas kernels: 74.4 us -> 70 us  [the longest x1 51.3 us: run_main(): pl.pallas_call(functools.partial(main_kernel, factor), out_shape=(shape(8...]
where the time goes in v2:
time: 72.3 us; the launch traced here: 72.1 us
  Pallas kernels  70 us (97%)
  local copies, waits for them, and re-layouts  1.39 us (2%)
    pallas_call x1, Pallas kernels, run_main(): pl.pallas_call(functools.partial(main_kernel, factor), out_shape=(shape(8...  51.3 us
    pallas_call x1, Pallas kernels, unpack(): pl.pallas_call(unpack_kernel, out_shape=(jax.ShapeDtypeStruct(raw.shape,...  18.8 us

profile of v2, /device:TPU:1, one launch (start us, length us, event | category | flops | bytes accessed | tf_op | source)
XLA Modules:
  0.0 72.1 jit_solution(6145153349388382515)
XLA Ops:
  0.6 1.4 %copy.22.nbr = s32[8,4,3]{2,1,0:T(4,128)} copy(s32[8,4,3]{0,1,2:T(4,128)} %param.22) | data formatting | bytes 768 | tf_op args[10]
  2.0 51.3 %main.1 = (bf16[8,256,128]{2,1,0:T(8,128)(2,1)}, bf16[2,16,32,128]{3,2,1,0:T(8,128)(2,1)}, f32[8,8,128]{2,1,0:T(8,128)}) custom-call(s32[8,4,3]{2,1,0:T(4,128)} %copy.22.nbr, bf16[8,256,128]{2,1,0:T(8,128)(2,1)} %bitcast.3, bf16[8,256,128]{2,1,0:T(8,128)(2,1)} %bitcast.4, f32[7,7,128]{2,1,0:T(8,128)} %kern_hbm.1, f32[128]{0:T(128)} %cb_hbm.1, f32[128]{0:T(128)} %gain_hbm.1, ...), custom_call_target="tpu_custom_call" | custom-call | tf_op jit(solution)/shard_map/main/pallas_call | solution.py:615
  53.3 18.8 %unpack.1 = (bf16[8,256,128]{2,1,0:T(8,128)(2,1)}, f32[7,7,128]{2,1,0:T(8,128)}, f32[128]{0:T(128)}, f32[128]{0:T(128)}, f32[128]{0:T(128)}, /*index=5*/f32[128,...) custom-call(bf16[8,256,128]{2,1,0:T(8,128)(2,1)} %get-tuple-element.23.raw, ...), custom_call_target="tpu_custom_call" | custom-call | tf_op jit(solution)/shard_map/unpack/pallas_call | solution.py:685

commit v3 on v2

--- a/solution.py
+++ b/solution.py
@@ -53,9 +53,9 @@
 
 def main_kernel(
     factor,
-    nbr, x_hbm, cot_hbm, kern_hbm, cb_hbm, gain_hbm, nb_hbm, we_hbm, be_hbm, wr_hbm, br_hbm, ls_hbm,
+    nbr_hbm, x_hbm, cot_hbm, kern_hbm, cb_hbm, gain_hbm, nb_hbm, we_hbm, be_hbm, wr_hbm, br_hbm, ls_hbm,
     out_hbm, gath, sgath,
-    x, cot, kern, cb, gain, nb, we, be, wr, br, ls, out,
+    nbr, x, cot, kern, cb, gain, nb, we, be, wr, br, ls, out,
     top, bot, hbuf, side, pieces, chosen, nsbuf, nsend,
     pad, conv, taps, act, acc_e, acc_r, sums,
     bigf, half, bigb, slots1, slotsz, small, sslots1, sslots2, few_ref,
@@ -92,7 +92,7 @@
         for i, (src, dst) in enumerate(
             (
                 (x_hbm, x), (kern_hbm, kern), (cb_hbm, cb), (cot_hbm, cot), (we_hbm, we), (wr_hbm, wr),
-                (gain_hbm, gain), (nb_hbm, nb), (be_hbm, be), (br_hbm, br), (ls_hbm, ls),
+                (nbr_hbm, nbr), (gain_hbm, gain), (nb_hbm, nb), (be_hbm, be), (br_hbm, br), (ls_hbm, ls),
             )
         )
     ]
@@ -219,13 +219,13 @@
                         band_send.at[k], band_recv.at[g], g, t,
                     ).wait_recv()
                 for g in range(FACES):
-                    nsend[g] = nsbuf[nbr[g, side_id, 0]]
+                    nsend[g] = nsbuf[nbr[0, side_id, g]]
                     forward(g).start()
 
         for k, g in enumerate(others):
             remote(pieces.at[f], pieces.at[g], piece_send.at[k], piece_recv.at[g], g, t).wait_recv()
-        from_west = pieces[nbr[f, 3, 0]]
-        from_east = pieces[nbr[f, 1, 0]]
+        from_west = pieces[nbr[0, 3, f]]
+        from_east = pieces[nbr[0, 1, f]]
         chosen[...] = jnp.concatenate(
             [from_west.astype(F32)[:, 8:16], from_east.astype(F32)[:, 0:8]], 1
         ).astype(BF)
@@ -284,7 +284,7 @@
 
         @pl.when(is_first)
         def _():
-            polar(nbr[f, 0, 2], (0, 1, 2))
+            polar(nbr[2, 0, f], (0, 1, 2))
 
         finish(range(0, 3), range(0, 3))
 
@@ -296,7 +296,7 @@
 
         @pl.when(is_last)
         def _():
-            polar(nbr[f, 2, 2], (11, 12, 13))
+            polar(nbr[2, 2, f], (11, 12, 13))
 
         finish(range(5, 8), range(11, 14))
 
@@ -401,7 +401,7 @@
             straight = jnp.concatenate([slots[i][first : first + 8] for i in (0, 1, 2)], 0)
             turned = jnp.concatenate([slots[i][first : first + 8] for i in (3, 4, 5)], 0)
             turned = nn(turn, turned.astype(BF))
-            halo = jnp.where(nbr[f, side_id, 2] == 1, turned, straight)
+            halo = jnp.where(nbr[2, side_id, f] == 1, turned, straight)
             pad[0:14, col : col + 1, :] = halo[5:19].reshape(14, 1, 128)
 
     @pl.loop(0, 4)
@@ -619,9 +619,10 @@
             shape(2, 16, 32, 128),
             jax.ShapeDtypeStruct((8, 8, 128), F32),
         ),
-        in_specs=[SMEM] + [ANY] * 11,
+        in_specs=[ANY] * 12,
         out_specs=(ANY, VMEM, VMEM),
-        scratch_shapes=[pltpu.VMEM(item.shape, item.dtype) for item in operands]
+        scratch_shapes=[pltpu.SMEM(neighbours.shape, jnp.int32)]
+        + [pltpu.VMEM(item.shape, item.dtype) for item in operands]
         + [
             pltpu.VMEM((8, 256, 128), BF),
             pltpu.VMEM((3, 256, 128), BF),
@@ -648,7 +649,7 @@
             pltpu.VMEM((16, 8, 128), F32),
             pltpu.VMEM((16, 8, 128), F32),
             pltpu.VMEM((8, 128), F32),
-            dma((11,)), dma((1,)), dma((2,)), dma((2,)), dma((8,)), dma((8,)), dma((8,)), dma((8,)),
+            dma((12,)), dma((1,)), dma((2,)), dma((2,)), dma((8,)), dma((8,)), dma((8,)), dma((8,)),
             dma((6,)), dma((6,)), dma((8,)), dma((8,)), dma((2,)),
             dma((4,)),
         ]
@@ -663,21 +664,24 @@
 def unpack_kernel(
     raw, gath, sgath,
     out, kernel_grad, cb_grad, gain_grad, nb_grad, we_grad, be_grad, wr_grad, br_grad, ls_grad,
-    sem,
+    stage, sem,
 ):
-    copy = pltpu.make_async_copy(raw, out, sem.at[0])
-    copy.start()
+    fetch = pltpu.make_async_copy(raw, stage, sem.at[0])
+    store = pltpu.make_async_copy(stage, out, sem.at[1])
+    fetch.start()
     rows = gath.reshape(1024, 128)
     few = sgath[...].reshape(64, 128)
     for q in range(4):
         we_grad[:, q * 128 : q * 128 + 128] = rows[q * 128 : q * 128 + 128, :].astype(F32)
         be_grad[q * 128 : q * 128 + 128] = few[54 + q]
+    fetch.wait()
+    store.start()
     wr_grad[...] = rows[512:1024, :].astype(F32)
     for i in range(7):
         kernel_grad[i] = few[i * 7 : i * 7 + 7]
     for i, ref in enumerate((cb_grad, gain_grad, nb_grad, br_grad, ls_grad)):
         ref[...] = few[49 + i]
-    copy.wait()
+    store.wait()
 
 
 def unpack(raw, gath, sgath):
@@ -691,7 +695,7 @@
         ),
         in_specs=[ANY, VMEM, VMEM],
         out_specs=(ANY,) + (VMEM,) * 9,
-        scratch_shapes=[pltpu.SemaphoreType.DMA((1,))],
+        scratch_shapes=[pltpu.VMEM(raw.shape, raw.dtype), pltpu.SemaphoreType.DMA((2,))],
         name="unpack",
     )(raw, gath, sgath)
 
@@ -702,7 +706,7 @@
 ):
     factor = 1.0 / math.sqrt(FACES * 256 * 256)
     raw, gath, sgath = run_main(
-        factor, neighbours, inputs[0], cotangent[0], kernel, conv_bias, norm_gain, norm_bias,
+        factor, jnp.transpose(neighbours, (2, 1, 0)), inputs[0], cotangent[0], kernel, conv_bias, norm_gain, norm_bias,
         expand_weight, expand_bias, reduce_weight, reduce_bias, layer_scale,
     )
     out, *grads = unpack(raw, gath, sgath)

time: 72.3 us -> 55 us (0.76)
  Pallas kernels: 70 us -> 54.1 us
  local copies, waits for them, and re-layouts: 1.39 us -> 0 us
    pallas_call x1, Pallas kernels: 18.8 us -> 3.63 us  [unpack(): pl.pallas_call(unpack_kernel, out_shape=(jax.ShapeDtypeStruct(raw.shape,...]
    unnamed x1 -> x0, local copies, waits for them, and re-layouts: 1.39 us -> none
    pallas_call x1, Pallas kernels: 51.3 us -> 50.5 us  [run_main(): pl.pallas_call(functools.partial(main_kernel, factor), out_shape=(shape(8...]
where the time goes in v3:
time: 55 us; the launch traced here: 54.8 us
  Pallas kernels  54.1 us (98%)
  between operations  0.66 us (1%)
    pallas_call x1, Pallas kernels, run_main(): pl.pallas_call(functools.partial(main_kernel, factor), out_shape=(shape(8...  50.5 us
    pallas_call x1, Pallas kernels, unpack(): pl.pallas_call(unpack_kernel, out_shape=(jax.ShapeDtypeStruct(raw.shape,...  3.63 us

profile of v3, /device:TPU:1, one launch (start us, length us, event | category | flops | bytes accessed | tf_op | source)
XLA Modules:
  0.0 54.8 jit_solution(10627042148824749716)
XLA Ops:
  0.6 50.5 %main.1 = (bf16[8,256,128]{2,1,0:T(8,128)(2,1)}, bf16[2,16,32,128]{3,2,1,0:T(8,128)(2,1)}, f32[8,8,128]{2,1,0:T(8,128)}) custom-call(s32[3,4,8]{2,1,0:T(4,128)} %bitcast.6, bf16[8,256,128]{2,1,0:T(8,128)(2,1)} %bitcast.4, bf16[8,256,128]{2,1,0:T(8,128)(2,1)} %bitcast.5, f32[7,7,128]{2,1,0:T(8,128)} %kern_hbm.1, f32[128]{0:T(128)} %cb_hbm.1, f32[128]{0:T(128)} %gain_hbm.1, ...), custom_call_target="tpu_custom_call" | custom-call | tf_op jit(solution)/shard_map/main/pallas_call | solution.py:615
  51.2 3.6 %unpack.1 = (bf16[8,256,128]{2,1,0:T(8,128)(2,1)}, f32[7,7,128]{2,1,0:T(8,128)}, f32[128]{0:T(128)}, f32[128]{0:T(128)}, f32[128]{0:T(128)}, /*index=5*/f32[128,...) custom-call(bf16[8,256,128]{2,1,0:T(8,128)(2,1)} %get-tuple-element.23.raw, ...), custom_call_target="tpu_custom_call" | custom-call | tf_op jit(solution)/shard_map/unpack/pallas_call | solution.py:689

commit v4 on v3

--- a/solution.py
+++ b/solution.py
@@ -57,11 +57,9 @@
     out_hbm, gath, sgath,
     nbr, x, cot, kern, cb, gain, nb, we, be, wr, br, ls, out,
     top, bot, hbuf, side, pieces, chosen, nsbuf, nsend,
-    pad, conv, taps, act, acc_e, acc_r, sums,
-    bigf, half, bigb, slots1, slotsz, small, sslots1, sslots2, few_ref,
-    load_sem, out_sem, row_send, row_recv, piece_send, piece_recv, band_send, band_recv,
-    side_send, side_recv, fwd_send, fwd_recv, local_sem,
-    core_sem, s1, r1, sz, rz, s4, r4, ss1, sr1, ss2, sr2, ss4, sr4,
+    pad, conv, taps, act, acc_e, acc_r, sums, ksum,
+    big, slots1, slotsz, fin, small, sslots1, sslots2, few_ref, sfin,
+    load_sem, out_sem, row_send, row_recv, side_send, side_recv, sem,
 ):
     f, t = place()
     last = TILES - 1
@@ -77,15 +75,22 @@
     s = t % 16
     z = s // 2
     core = s % 2
-    twin = t + 1 - 2 * core
     a = hi * 8 + f
+    me = a * 2 + core
     others = [lax.rem(f + k, FACES) for k in range(1, FACES)]
     plane = [lax.rem(a + k, 16) for k in range(1, 16)]
+    near = [lax.rem(me + k, 32) for k in range(1, 32)]
     line = [lax.rem(s + k, 16) for k in range(1, 16)]
     stack = [lax.rem(z + k, 8) for k in range(1, 8)]
 
     def plane_id(p):
         return lax.rem(p, 8), p // 8 * 16 + s
+
+    def near_id(q):
+        return lax.rem(q // 2, 8), q // 16 * 16 + z * 2 + q % 2
+
+    def drain(ref, which):
+        pltpu.make_async_copy(ref, ref, sem.at[which]).wait()
 
     loads = [
         pltpu.make_async_copy(src, dst, load_sem.at[i])
@@ -104,8 +109,8 @@
     def hello(face, tile):
         pl.semaphore_signal(barrier, inc=1, device_id=(face, tile), device_id_type=MESH)
 
-    for p in plane:
-        hello(*plane_id(p))
+    for q in near:
+        hello(*near_id(q))
     for p in line:
         hello(f, hi * 16 + p)
     hello(f, mirror)
@@ -155,24 +160,25 @@
                         acc[r] = acc[r] + taps[(row - r) * 7 + j] * v
         return [acc[r] for r in out_rows]
 
-    @pl.loop(2, 30)
-    def _(jb):
-        col = pl.multiple_of(jb * 8, 8)
-        for r, v in enumerate(convolve(col, [bias] * 8, range(8), range(3, 11))):
-            conv[r, pl.ds(col, 8), :] = v
+    @pl.loop(0, 7)
+    def _(i):
+        for u in range(4):
+            col = pl.multiple_of(16 + i * 32 + u * 8, 8)
+            for r, v in enumerate(convolve(col, [bias] * 8, range(8), range(3, 11))):
+                conv[r, pl.ds(col, 8), :] = v
 
     one = lambda cond: cond.astype(jnp.int32)
-    count = 31 + one(has_up) + one(has_down) + one(mir_up) + one(mir_down) + 8 * one(edge)
+    count = 47 + one(has_up) + one(has_down) + one(mir_up) + one(mir_down) + 8 * one(edge)
     pl.semaphore_wait(barrier, count)
 
     def band_copy(rows, k, g):
         return remote(
             x.at[pl.ds(rows, 3), pl.ds(pl.multiple_of(g * 32, 32), 32), :], nsbuf.at[f],
-            band_send.at[k], band_recv.at[f], g, t,
+            sem.at[0], sem.at[1], g, t,
         )
 
     def piece_copy(k, g):
-        return remote(pieces.at[f], pieces.at[f], piece_send.at[k], piece_recv.at[f], g, t)
+        return remote(pieces.at[f], pieces.at[f], sem.at[2], sem.at[3], g, t)
 
     def up_copy():
         return remote(x.at[pl.ds(0, 3)], bot, row_send.at[0], row_recv.at[0], f, t - 1)
@@ -203,7 +209,7 @@
         load.wait()
 
     def forward(g):
-        return remote(nsend.at[g], hbuf.at[f], fwd_send.at[g], fwd_recv.at[f], g, mirror)
+        return remote(nsend.at[g], hbuf.at[f], sem.at[4], sem.at[5], g, mirror)
 
     def side_copy(slot, tile):
         return remote(chosen, side.at[slot], side_send.at[slot], side_recv.at[slot], f, tile)
@@ -213,17 +219,12 @@
 
             @pl.when(cond)
             def _(side_id=side_id, rows=rows):
-                for k, g in enumerate(others):
-                    remote(
-                        x.at[pl.ds(rows, 3), pl.ds(pl.multiple_of(g * 32, 32), 32), :], nsbuf.at[g],
-                        band_send.at[k], band_recv.at[g], g, t,
-                    ).wait_recv()
+                drain(nsbuf.at[pl.ds(0, 7)], 1)
                 for g in range(FACES):
                     nsend[g] = nsbuf[nbr[0, side_id, g]]
                     forward(g).start()
 
-        for k, g in enumerate(others):
-            remote(pieces.at[f], pieces.at[g], piece_send.at[k], piece_recv.at[g], g, t).wait_recv()
+        drain(pieces.at[pl.ds(0, 7)], 3)
         from_west = pieces[nbr[0, 3, f]]
         from_east = pieces[nbr[0, 1, f]]
         chosen[...] = jnp.concatenate(
@@ -258,10 +259,7 @@
             side[5] = chosen[...]
 
     def polar(flag, rows):
-        for g in range(FACES):
-            remote(
-                nsend.at[g], hbuf.at[g], fwd_send.at[g], fwd_recv.at[g], g, mirror
-            ).wait_recv()
+        drain(hbuf, 5)
         turn = one_hot(256, 256, lambda r: 255 - r)
         for d in range(3):
             band = jnp.concatenate([hbuf[k, d] for k in range(8)], 0)
@@ -269,12 +267,13 @@
             pad[rows[d], 8:264, :] = jnp.where(flag == 1, turned, band.astype(F32))
 
     def finish(out_rows, in_rows):
-        @pl.loop(2, 30)
-        def _(jb):
-            col = pl.multiple_of(jb * 8, 8)
-            acc = [conv[r, pl.ds(col, 8), :] for r in out_rows]
-            for r, v in zip(out_rows, convolve(col, acc, out_rows, in_rows)):
-                conv[r, pl.ds(col, 8), :] = v
+        @pl.loop(0, 7)
+        def _(i):
+            for u in range(4):
+                col = pl.multiple_of(16 + i * 32 + u * 8, 8)
+                acc = [conv[r, pl.ds(col, 8), :] for r in out_rows]
+                for r, v in zip(out_rows, convolve(col, acc, out_rows, in_rows)):
+                    conv[r, pl.ds(col, 8), :] = v
 
     def finish_top():
         @pl.when(has_up)
@@ -337,34 +336,65 @@
         sums[3] += fold(branch_cot.astype(F32))
         return conv_cot
 
+    def kernel_grad(base, rows, cols):
+        steps = len(cols) // 4
+
+        @pl.loop(0, 7)
+        def _(j):
+            def step(k, acc):
+                acc = list(acc)
+                for u in range(4):
+                    col = cols[u] if steps == 1 else pl.multiple_of(cols[0] + k * 32 + u * 8, 8)
+                    cots = [conv[base + r, pl.ds(col, 8), :] for r in range(rows)]
+                    for row in range(rows + 6):
+                        v = pad[base + row, pl.ds(col + 5 + j, 8), :]
+                        for i in range(7):
+                            if 0 <= row - i < rows:
+                                acc[i] = acc[i] + cots[row - i] * v
+                return tuple(acc)
+
+            zero = (jnp.zeros((8, 128), F32),) * 7
+            acc = step(0, zero) if steps == 1 else lax.fori_loop(0, steps, step, zero)
+            for i in range(7):
+                ksum[i * 7 + j] += acc[i]
+
+    inner = range(16, 240, 8)
     low_first = t < 16
-
-    def row_of(i):
-        return jnp.where(low_first, 4 - 4 * i, 4 * i)
-
-    @pl.loop(0, 2)
-    def _(i):
-        r0 = row_of(i)
-
-        @pl.when(r0 == 0)
-        def _():
-            finish_top()
-
-        @pl.when(r0 == 4)
-        def _():
-            finish_bottom()
-
-        @pl.when(i == 0)
-        def _():
-            phase_two()
-
-        four = pl.ds(r0, 4)
-        got = mlp(
-            conv[four, 16:240, :].reshape(896, 128),
-            cot[four, 16:240, :].reshape(896, 128),
-            pl.ds(pl.multiple_of(i * 896, 128), 896),
-        )
-        conv[four, 16:240, :] = got.reshape(4, 224, 128)
+    base1 = jnp.where(low_first, 5, 0)
+    base2 = 5 - base1
+    mid, three1, three2 = pl.ds(3, 2), pl.ds(base1, 3), pl.ds(base2, 3)
+
+    def inside(ref, rows, count):
+        return ref[rows, 16:240, :].reshape(count * 224, 128)
+
+    def outside(ref):
+        return jnp.concatenate([ref[:, 0:16, :], ref[:, 240:256, :]], 1).reshape(256, 128)
+
+    got = mlp(inside(conv, mid, 2), inside(cot, mid, 2), pl.ds(0, 448))
+    conv[mid, 16:240, :] = got.reshape(2, 224, 128)
+    ksum[...] = jnp.zeros_like(ksum)
+    kernel_grad(3, 2, inner)
+    phase_two()
+
+    @pl.when(low_first)
+    def _():
+        finish_bottom()
+
+    @pl.when(jnp.logical_not(low_first))
+    def _():
+        finish_top()
+
+    got = mlp(inside(conv, three1, 3), inside(cot, three1, 3), pl.ds(448, 672))
+    conv[three1, 16:240, :] = got.reshape(3, 224, 128)
+    kernel_grad(base1, 3, inner)
+
+    @pl.when(low_first)
+    def _():
+        finish_top()
+
+    @pl.when(jnp.logical_not(low_first))
+    def _():
+        finish_bottom()
 
     side_copy(4, mirror).wait_recv()
 
@@ -404,35 +434,31 @@
             halo = jnp.where(nbr[2, side_id, f] == 1, turned, straight)
             pad[0:14, col : col + 1, :] = halo[5:19].reshape(14, 1, 128)
 
-    @pl.loop(0, 4)
-    def _(i):
-        col = pl.multiple_of((i + i // 2 * 28) * 8, 8)
+    for col in (0, 8, 240, 248):
         for r, v in enumerate(convolve(col, [bias] * 8, range(8), range(14))):
             conv[r, pl.ds(col, 8), :] = v
 
     got = mlp(
-        jnp.concatenate([conv[:, 0:16, :], conv[:, 240:256, :]], 1).reshape(256, 128),
-        jnp.concatenate([cot[:, 0:16, :], cot[:, 240:256, :]], 1).reshape(256, 128),
-        pl.ds(1792, 256),
-    ).reshape(8, 32, 128)
-    conv[:, 0:16, :] = got[:, 0:16]
-    conv[:, 240:256, :] = got[:, 16:32]
+        jnp.concatenate([inside(conv, three2, 3), outside(conv)], 0),
+        jnp.concatenate([inside(cot, three2, 3), outside(cot)], 0),
+        pl.ds(1120, 928),
+    )
+    conv[three2, 16:240, :] = got[0:672].reshape(3, 224, 128)
+    ends = got[672:928].reshape(8, 32, 128)
+    conv[:, 0:16, :] = ends[:, 0:16]
+    conv[:, 240:256, :] = ends[:, 16:32]
 
     scale = jnp.zeros((8, 128), F32)
     for q in range(4):
         cols = slice(q * 128, q * 128 + 128)
-        bigf[q * 128 : q * 128 + 128, :] = acc_e[0:128, cols]
+        big[q * 4 : q * 4 + 4] = acc_e[0:128, cols].astype(BF).reshape(4, 32, 128)
         turned = acc_r[:, cols].T
-        bigf[512 + q * 128 : 640 + q * 128, :] = turned
+        big[16 + q * 4 : 20 + q * 4] = turned.astype(BF).reshape(4, 32, 128)
         scale = scale + fold(turned * wr[cols, :].astype(F32))
 
-    def halve(part):
-        return remote(
-            bigf.at[pl.ds(pl.multiple_of(part * 512, 512), 512)], half, core_sem.at[0], core_sem.at[1],
-            f, twin,
-        )
-
-    halve(1 - core).start()
+    for q in near:
+        remote(big.at[q], slots1.at[me], sem.at[6], sem.at[7], *near_id(q)).start()
+    slots1[me] = big[me]
 
     small[...] = jnp.zeros_like(small)
     totals = [jnp.sum(sums[i], 0, keepdims=True) for i in range(4)]
@@ -442,134 +468,77 @@
     for q in range(4):
         small[54 + q : 55 + q, :] = acc_e[128:129, q * 128 : q * 128 + 128]
 
-    def kernel_grad(first, stop):
-        @pl.loop(first, stop)
-        def _(j):
-            def step(jb, acc):
-                col = pl.multiple_of(jb * 8, 8)
-                acc = list(acc)
-                cots = [conv[r, pl.ds(col, 8), :] for r in range(8)]
-                for row in range(14):
-                    v = pad[row, pl.ds(col + 5 + j, 8), :]
-                    for i in range(7):
-                        if 0 <= row - i < 8:
-                            acc[i] = acc[i] + cots[row - i] * v
-                return tuple(acc)
-
-            acc = lax.fori_loop(0, 32, step, (jnp.zeros((8, 128), F32),) * 7)
-            for i in range(7):
-                small[pl.ds(i * 7 + j, 1), :] = jnp.sum(acc[i], 0, keepdims=True)
-
-    kernel_grad(0, 2)
-    halve(core).wait_recv()
-    mine = bigf[pl.ds(pl.multiple_of(core * 512, 512), 512), :] + half[...]
-    bigb[...] = mine.astype(BF).reshape(16, 32, 128)
-
-    def big1(k, p, slot):
-        return remote(bigb.at[p], slots1.at[slot], s1.at[k], r1.at[slot], *plane_id(p))
-
-    for k, p in enumerate(plane):
-        big1(k, p, a).start()
-    slots1[a] = bigb[a]
-    kernel_grad(2, 7)
-
-    def small1(k, p, slot):
+    kernel_grad(base2, 3, inner)
+    kernel_grad(0, 8, (0, 8, 240, 248))
+    for i in range(49):
+        small[i : i + 1, :] = jnp.sum(ksum[i], 0, keepdims=True)
+
+    for p in plane:
         rows = pl.ds(pl.multiple_of(lax.rem(p, 8) * 8, 8), 8)
-        return remote(small.at[rows], sslots1.at[slot], ss1.at[k], sr1.at[slot], *plane_id(p))
-
-    for k, p in enumerate(plane):
-        small1(k, p, a).start()
+        remote(small.at[rows], sslots1.at[a], sem.at[8], sem.at[9], *plane_id(p)).start()
     sslots1[a] = small[pl.ds(pl.multiple_of(f * 8, 8), 8), :]
-
-    for k, p in enumerate(plane):
-        big1(k, p, p).wait_recv()
-    total = slots1[0].astype(F32)
-    for p in range(1, 16):
-        total = total + slots1[p].astype(F32)
-    slotsz[z] = total.astype(BF)
-
-    def bigz(k, q, slot):
-        return remote(
-            slotsz.at[z], slotsz.at[slot], sz.at[k], rz.at[slot], f, hi * 16 + q * 2 + core
-        )
-
-    for k, q in enumerate(stack):
-        bigz(k, q, z).start()
 
     def output(rows, residual):
         branch = nn(act[rows, :], wr[...]) + vec(br)
         return (residual.astype(F32) + vec(ls) * branch).astype(BF)
 
-    @pl.loop(0, 2)
-    def _(i):
-        four = pl.ds(row_of(i), 4)
-        rows = pl.ds(pl.multiple_of(i * 896, 128), 896)
-        out[four, 16:240, :] = output(rows, x[four, 16:240, :].reshape(896, 128)).reshape(4, 224, 128)
-
-    sides = output(
-        pl.ds(1792, 256),
-        jnp.concatenate([x[:, 0:16, :], x[:, 240:256, :]], 1).reshape(256, 128),
-    ).reshape(8, 32, 128)
-    out[:, 0:16, :] = sides[:, 0:16]
-    out[:, 240:256, :] = sides[:, 16:32]
+    def output_inside(rows, three, count):
+        out[three, 16:240, :] = output(rows, inside(x, three, count)).reshape(count, 224, 128)
+
+    output_inside(pl.ds(0, 448), mid, 2)
+    output_inside(pl.ds(448, 672), three1, 3)
+
+    drain(slots1.at[pl.ds(0, 31)], 7)
+    total = slots1[0].astype(F32)
+    for q in range(1, 32):
+        total = total + slots1[q].astype(F32)
+    slotsz[z] = total.astype(BF)
+    for q in stack:
+        remote(
+            slotsz.at[z], slotsz.at[z], sem.at[10], sem.at[11], f, hi * 16 + q * 2 + core
+        ).start()
+
+    output_inside(pl.ds(1120, 672), three2, 3)
+    ends = output(pl.ds(1792, 256), outside(x)).reshape(8, 32, 128)
+    out[:, 0:16, :] = ends[:, 0:16]
+    out[:, 240:256, :] = ends[:, 16:32]
     store = pltpu.make_async_copy(out, out_hbm, out_sem.at[0])
     store.start()
 
-    for k, p in enumerate(plane):
-        small1(k, p, p).wait_recv()
+    drain(sslots1.at[pl.ds(0, 15)], 9)
     few = sslots1[0]
     for p in range(1, 16):
         few = few + sslots1[p]
     few_ref[...] = few
-
-    def small2(k, p, slot):
-        return remote(few_ref, sslots2.at[slot], ss2.at[k], sr2.at[slot], f, hi * 16 + p)
-
-    for k, p in enumerate(line):
-        small2(k, p, s).start()
+    for p in line:
+        remote(few_ref, sslots2.at[s], sem.at[12], sem.at[13], f, hi * 16 + p).start()
     sslots2[s] = few
 
-    for k, q in enumerate(stack):
-        bigz(k, q, q).wait_recv()
+    drain(slotsz.at[pl.ds(0, 7)], 11)
     total = slotsz[0].astype(F32)
     for q in range(1, 8):
         total = total + slotsz[q].astype(F32)
-    gath[core, a] = (total * factor).astype(BF)
-
-    def big4(k, p, slot):
-        return remote(gath.at[core, a], gath.at[core, slot], s4.at[k], r4.at[slot], *plane_id(p))
-
-    for k, p in enumerate(plane):
-        big4(k, p, a).start()
-
-    for k, p in enumerate(line):
-        small2(k, p, p).wait_recv()
+    fin[...] = (total * factor).astype(BF)
+    for q in near:
+        remote(fin, gath.at[me], sem.at[14], sem.at[15], *near_id(q)).start()
+    own = pltpu.make_async_copy(fin, gath.at[me], out_sem.at[1])
+    own.start()
+
+    drain(sslots2.at[pl.ds(0, 15)], 13)
     few = sslots2[0]
     for p in range(1, 16):
         few = few + sslots2[p]
-    sgath[f] = few * factor
-
-    def small4(k, g, slot):
-        return remote(sgath.at[f], sgath.at[slot], ss4.at[k], sr4.at[slot], g, t)
-
-    for k, g in enumerate(others):
-        small4(k, g, f).start()
-
-    for k, p in enumerate(plane):
-        big4(k, p, p).wait_recv()
-
-    def share(part):
-        return remote(gath.at[part], gath.at[part], core_sem.at[2], core_sem.at[3], f, twin)
-
-    share(core).start()
-    for k, g in enumerate(others):
-        small4(k, g, g).wait_recv()
-    share(1 - core).wait_recv()
+    sfin[...] = few * factor
+    for g in others:
+        remote(sfin, sgath.at[f], sem.at[16], sem.at[17], g, t).start()
+    own_small = pltpu.make_async_copy(sfin, sgath.at[f], out_sem.at[2])
+    own_small.start()
+    drain(sgath.at[pl.ds(0, 7)], 17)
+    drain(gath.at[pl.ds(0, 31)], 15)
 
     store.wait()
-    for k, g in enumerate(others):
-        piece_copy(k, g).wait_send()
-        small4(k, g, f).wait_send()
+    own.wait()
+    own_small.wait()
     side_copy(4, mirror).wait_send()
 
     @pl.when(has_up)
@@ -592,21 +561,16 @@
 
     @pl.when(edge)
     def _():
-        for k, g in enumerate(others):
-            band_copy(0, k, g).wait_send()
-        for g in range(FACES):
-            forward(g).wait_send()
-
-    halve(1 - core).wait_send()
-    share(core).wait_send()
-    for k, p in enumerate(plane):
-        big1(k, p, a).wait_send()
-        small1(k, p, a).wait_send()
-        big4(k, p, a).wait_send()
-    for k, p in enumerate(line):
-        small2(k, p, s).wait_send()
-    for k, q in enumerate(stack):
-        bigz(k, q, z).wait_send()
+        drain(nsbuf.at[pl.ds(0, 7)], 0)
+        drain(hbuf, 4)
+
+    drain(pieces.at[pl.ds(0, 7)], 2)
+    drain(slots1.at[pl.ds(0, 31)], 6)
+    drain(sslots1.at[pl.ds(0, 15)], 8)
+    drain(slotsz.at[pl.ds(0, 7)], 10)
+    drain(sslots2.at[pl.ds(0, 15)], 12)
+    drain(gath.at[pl.ds(0, 31)], 14)
+    drain(sgath.at[pl.ds(0, 7)], 16)
 
 
 def run_main(factor, neighbours, *operands):
@@ -616,11 +580,11 @@
         functools.partial(main_kernel, factor),
         out_shape=(
             shape(8, 256, 128),
-            shape(2, 16, 32, 128),
+            shape(32, 32, 128),
             jax.ShapeDtypeStruct((8, 8, 128), F32),
         ),
         in_specs=[ANY] * 12,
-        out_specs=(ANY, VMEM, VMEM),
+        out_specs=(ANY, ANY, ANY),
         scratch_shapes=[pltpu.SMEM(neighbours.shape, jnp.int32)]
         + [pltpu.VMEM(item.shape, item.dtype) for item in operands]
         + [
@@ -640,20 +604,18 @@
             pltpu.VMEM((144, 512), F32),
             pltpu.VMEM((128, 512), F32),
             pltpu.VMEM((4, 8, 128), F32),
-            pltpu.VMEM((1024, 128), F32),
-            pltpu.VMEM((512, 128), F32),
-            pltpu.VMEM((16, 32, 128), BF),
-            pltpu.VMEM((16, 32, 128), BF),
+            pltpu.VMEM((49, 8, 128), F32),
+            pltpu.VMEM((32, 32, 128), BF),
+            pltpu.VMEM((32, 32, 128), BF),
             pltpu.VMEM((8, 32, 128), BF),
+            pltpu.VMEM((32, 128), BF),
             pltpu.VMEM((64, 128), F32),
             pltpu.VMEM((16, 8, 128), F32),
             pltpu.VMEM((16, 8, 128), F32),
             pltpu.VMEM((8, 128), F32),
-            dma((12,)), dma((1,)), dma((2,)), dma((2,)), dma((8,)), dma((8,)), dma((8,)), dma((8,)),
-            dma((6,)), dma((6,)), dma((8,)), dma((8,)), dma((2,)),
-            dma((4,)),
-        ]
-        + [dma((16,))] * 12,
+            pltpu.VMEM((8, 128), F32),
+            dma((12,)), dma((3,)), dma((2,)), dma((2,)), dma((6,)), dma((6,)), dma((18,)),
+        ],
         compiler_params=pltpu.CompilerParams(
             collective_id=0, has_side_effects=True, vmem_limit_bytes=56 * 1024 * 1024
         ),
@@ -664,18 +626,24 @@
 def unpack_kernel(
     raw, gath, sgath,
     out, kernel_grad, cb_grad, gain_grad, nb_grad, we_grad, be_grad, wr_grad, br_grad, ls_grad,
-    stage, sem,
+    stage, rows_in, few_in, sem,
 ):
-    fetch = pltpu.make_async_copy(raw, stage, sem.at[0])
-    store = pltpu.make_async_copy(stage, out, sem.at[1])
-    fetch.start()
-    rows = gath.reshape(1024, 128)
-    few = sgath[...].reshape(64, 128)
+    fetches = [
+        pltpu.make_async_copy(src, dst, sem.at[i])
+        for i, (src, dst) in enumerate(((raw, stage), (gath, rows_in), (sgath, few_in)))
+    ]
+    for fetch in fetches:
+        fetch.start()
+    store = pltpu.make_async_copy(stage, out, sem.at[3])
+    fetches[0].wait()
+    store.start()
+    fetches[1].wait()
+    fetches[2].wait()
+    rows = rows_in.reshape(1024, 128)
+    few = few_in[...].reshape(64, 128)
     for q in range(4):
         we_grad[:, q * 128 : q * 128 + 128] = rows[q * 128 : q * 128 + 128, :].astype(F32)
         be_grad[q * 128 : q * 128 + 128] = few[54 + q]
-    fetch.wait()
-    store.start()
     wr_grad[...] = rows[512:1024, :].astype(F32)
     for i in range(7):
         kernel_grad[i] = few[i * 7 : i * 7 + 7]
@@ -693,9 +661,15 @@
             one(7, 7, 128), one(128), one(128), one(128), one(128, 512), one(512),
             one(512, 128), one(128), one(128),
         ),
-        in_specs=[ANY, VMEM, VMEM],
+        in_specs=[ANY, ANY, ANY],
         out_specs=(ANY,) + (VMEM,) * 9,
-        scratch_shapes=[pltpu.VMEM(raw.shape, raw.dtype), pltpu.SemaphoreType.DMA((2,))],
+        scratch_shapes=[
+            pltpu.VMEM(raw.shape, raw.dtype),
+            pltpu.VMEM(gath.shape, gath.dtype),
+            pltpu.VMEM(sgath.shape, sgath.dtype),
+            pltpu.SemaphoreType.DMA((4,)),
+        ],
+        compiler_params=pltpu.CompilerParams(vmem_limit_bytes=56 * 1024 * 1024),
         name="unpack",
     )(raw, gath, sgath)
 

time: 55 us -> 48.3 us (0.88)
  Pallas kernels: 54.1 us -> 47.6 us
    pallas_call x1, Pallas kernels: 50.5 us -> 44.9 us  [run_main(): pl.pallas_call(functools.partial(main_kernel, factor), out_shape=(shape(8...]
    pallas_call x1, Pallas kernels: 3.63 us -> 2.69 us  [unpack(): pl.pallas_call(unpack_kernel, out_shape=(jax.ShapeDtypeStruct(raw.shape,...]
where the time goes in v4:
time: 48.3 us; the launch traced here: 48.2 us
  Pallas kernels  47.6 us (99%)
  between operations  0.66 us (1%)
    pallas_call x1, Pallas kernels, run_main(): pl.pallas_call(functools.partial(main_kernel, factor), out_shape=(shape(8...  44.9 us
    pallas_call x1, Pallas kernels, unpack(): pl.pallas_call(unpack_kernel, out_shape=(jax.ShapeDtypeStruct(raw.shape,...  2.69 us

profile of v4, /device:TPU:1, one launch (start us, length us, event | category | flops | bytes accessed | tf_op | source)
XLA Modules:
  0.0 48.2 jit_solution(7707192281835331341)
XLA Ops:
  0.6 44.9 %main.1 = (bf16[8,256,128]{2,1,0:T(8,128)(2,1)}, bf16[32,32,128]{2,1,0:T(8,128)(2,1)}, f32[8,8,128]{2,1,0:T(8,128)}) custom-call(s32[3,4,8]{2,1,0:T(4,128)} %bitcast.6, bf16[8,256,128]{2,1,0:T(8,128)(2,1)} %bitcast.4, bf16[8,256,128]{2,1,0:T(8,128)(2,1)} %bitcast.5, f32[7,7,128]{2,1,0:T(8,128)} %kern_hbm.1, f32[128]{0:T(128)} %cb_hbm.1, f32[128]{0:T(128)} %gain_hbm.1, ...), custom_call_target="tpu_custom_call" | custom-call | tf_op jit(solution)/shard_map/main/pallas_call | solution.py:579
  45.5 2.7 %unpack.1 = (bf16[8,256,128]{2,1,0:T(8,128)(2,1)}, f32[7,7,128]{2,1,0:T(8,128)}, f32[128]{0:T(128)}, f32[128]{0:T(128)}, f32[128]{0:T(128)}, /*index=5*/f32[128,...) custom-call(bf16[8,256,128]{2,1,0:T(8,128)(2,1)} %get-tuple-element.23.raw, ...), custom_call_target="tpu_custom_call" | custom-call | tf_op jit(solution)/shard_map/unpack/pallas_call | solution.py:657

commit v5 on v4

--- a/solution.py
+++ b/solution.py
@@ -56,7 +56,7 @@
     nbr_hbm, x_hbm, cot_hbm, kern_hbm, cb_hbm, gain_hbm, nb_hbm, we_hbm, be_hbm, wr_hbm, br_hbm, ls_hbm,
     out_hbm, gath, sgath,
     nbr, x, cot, kern, cb, gain, nb, we, be, wr, br, ls, out,
-    top, bot, hbuf, side, pieces, chosen, nsbuf, nsend,
+    top, bot, hbuf, side, pieces, chosen, near_band, far_band, near_out, far_out,
     pad, conv, taps, act, acc_e, acc_r, sums, ksum,
     big, slots1, slotsz, fin, small, sslots1, sslots2, few_ref, sfin,
     load_sem, out_sem, row_send, row_recv, side_send, side_recv, sem,
@@ -109,6 +109,11 @@
     def hello(face, tile):
         pl.semaphore_signal(barrier, inc=1, device_id=(face, tile), device_id_type=MESH)
 
+    @pl.when(edge)
+    def _():
+        for g in range(FACES):
+            hello(g, mirror)
+
     for q in near:
         hello(*near_id(q))
     for p in line:
@@ -130,11 +135,6 @@
     @pl.when(mir_down)
     def _():
         hello(f, mirror - 1)
-
-    @pl.when(edge)
-    def _():
-        for g in range(FACES):
-            hello(g, mirror)
 
     loads[0].wait()
     for d in range(3):
@@ -149,13 +149,13 @@
             taps[i * 7 + j] = jnp.broadcast_to(kern[i, j : j + 1, :], (8, 128))
     bias = jnp.broadcast_to(cb[...].reshape(1, 128), (8, 128))
 
-    def convolve(col, acc, out_rows, in_rows):
+    def convolve(col, acc, out_rows, in_rows, base=0):
         acc = dict(zip(out_rows, acc))
         for j in range(7):
             for row in in_rows:
                 hit = [r for r in out_rows if 0 <= row - r < 7]
                 if hit:
-                    v = pad[row, pl.ds(col + 5 + j, 8), :]
+                    v = pad[base + row, pl.ds(col + 5 + j, 8), :]
                     for r in hit:
                         acc[r] = acc[r] + taps[(row - r) * 7 + j] * v
         return [acc[r] for r in out_rows]
@@ -171,11 +171,8 @@
     count = 47 + one(has_up) + one(has_down) + one(mir_up) + one(mir_down) + 8 * one(edge)
     pl.semaphore_wait(barrier, count)
 
-    def band_copy(rows, k, g):
-        return remote(
-            x.at[pl.ds(rows, 3), pl.ds(pl.multiple_of(g * 32, 32), 32), :], nsbuf.at[f],
-            sem.at[0], sem.at[1], g, t,
-        )
+    def columns(c):
+        return pl.ds(pl.multiple_of(c * 16, 16), 16)
 
     def piece_copy(k, g):
         return remote(pieces.at[f], pieces.at[f], sem.at[2], sem.at[3], g, t)
@@ -190,12 +187,14 @@
 
         @pl.when(cond)
         def _(rows=rows):
-            for k, g in enumerate(others):
-                band_copy(rows, k, g).start()
-            nsbuf[f] = x[rows : rows + 3, pl.ds(pl.multiple_of(f * 32, 32), 32), :]
-
-    for k, g in enumerate(others):
-        piece_copy(k, g).start()
+            three = pl.ds(rows, 3)
+            for g in others:
+                remote(x.at[three, columns(g), :], near_band.at[f], sem.at[0], sem.at[1], g, t).start()
+            for g in range(FACES):
+                remote(
+                    x.at[three, columns(g + 8), :], far_band.at[f], sem.at[18], sem.at[19], g, mirror
+                ).start()
+            near_band[f] = x[three, columns(f), :]
 
     @pl.when(has_up)
     def _():
@@ -208,21 +207,23 @@
     for load in loads[3:]:
         load.wait()
 
-    def forward(g):
-        return remote(nsend.at[g], hbuf.at[f], sem.at[4], sem.at[5], g, mirror)
-
     def side_copy(slot, tile):
         return remote(chosen, side.at[slot], side_send.at[slot], side_recv.at[slot], f, tile)
 
     def phase_two():
-        for side_id, rows, cond in ((0, 5, is_last), (2, 0, is_first)):
+        for near_side, far_side, cond in ((0, 2, is_last), (2, 0, is_first)):
 
             @pl.when(cond)
-            def _(side_id=side_id, rows=rows):
-                drain(nsbuf.at[pl.ds(0, 7)], 1)
+            def _(near_side=near_side, far_side=far_side):
+                drain(near_band.at[pl.ds(0, 7)], 1)
                 for g in range(FACES):
-                    nsend[g] = nsbuf[nbr[0, side_id, g]]
-                    forward(g).start()
+                    near_out[g] = near_band[nbr[0, near_side, g]]
+                    remote(near_out.at[g], hbuf.at[f], sem.at[4], sem.at[5], g, mirror).start()
+                drain(far_band, 19)
+                for k, g in enumerate(others):
+                    far_out[k] = far_band[nbr[0, far_side, g]]
+                    remote(far_out.at[k], hbuf.at[f + 8], sem.at[4], sem.at[5], g, t).start()
+                hbuf[f + 8] = far_band[nbr[0, far_side, f]]
 
         drain(pieces.at[pl.ds(0, 7)], 3)
         from_west = pieces[nbr[0, 3, f]]
@@ -259,10 +260,10 @@
             side[5] = chosen[...]
 
     def polar(flag, rows):
-        drain(hbuf, 5)
+        drain(hbuf.at[pl.ds(0, 15)], 5)
         turn = one_hot(256, 256, lambda r: 255 - r)
         for d in range(3):
-            band = jnp.concatenate([hbuf[k, d] for k in range(8)], 0)
+            band = jnp.concatenate([hbuf[k, d] for k in range(16)], 0)
             turned = nn(turn, band)
             pad[rows[d], 8:264, :] = jnp.where(flag == 1, turned, band.astype(F32))
 
@@ -305,7 +306,7 @@
     mean_of = jnp.full((128, 128), 1.0 / 128, BF)
     vec = lambda ref: ref[...].reshape(1, -1)
 
-    def mlp(c, cotangent, rows):
+    def mlp(c, cotangent, rows, between=None):
         count = c.shape[0]
         centred = c - nn(c.astype(BF), mean_of)
         variance = nn((centred * centred).astype(BF), mean_of)
@@ -325,6 +326,8 @@
         left = jnp.concatenate([scaled.T, jnp.ones((16, count), BF)], 0)
         acc_e[...] += nn(left, hidden_cot)
         acc_r[...] += nn(branch_cot.T, active_low)
+        if between is not None:
+            between()
         scaled_cot = nt(hidden_cot, we[...])
         normed_cot = scaled_cot * vec(gain)
         m1 = nn(normed_cot.astype(BF), mean_of)
@@ -362,16 +365,20 @@
     low_first = t < 16
     base1 = jnp.where(low_first, 5, 0)
     base2 = 5 - base1
+    base5 = jnp.where(low_first, 3, 0)
     mid, three1, three2 = pl.ds(3, 2), pl.ds(base1, 3), pl.ds(base2, 3)
+    five = pl.ds(base5, 5)
 
     def inside(ref, rows, count):
         return ref[rows, 16:240, :].reshape(count * 224, 128)
 
     def outside(ref):
-        return jnp.concatenate([ref[:, 0:16, :], ref[:, 240:256, :]], 1).reshape(256, 128)
+        return jnp.concatenate([ref[five, 0:16, :], ref[five, 240:256, :]], 1).reshape(160, 128)
 
     got = mlp(inside(conv, mid, 2), inside(cot, mid, 2), pl.ds(0, 448))
     conv[mid, 16:240, :] = got.reshape(2, 224, 128)
+    for k, g in enumerate(others):
+        piece_copy(k, g).start()
     ksum[...] = jnp.zeros_like(ksum)
     kernel_grad(3, 2, inner)
     phase_two()
@@ -387,14 +394,6 @@
     got = mlp(inside(conv, three1, 3), inside(cot, three1, 3), pl.ds(448, 672))
     conv[three1, 16:240, :] = got.reshape(3, 224, 128)
     kernel_grad(base1, 3, inner)
-
-    @pl.when(low_first)
-    def _():
-        finish_top()
-
-    @pl.when(jnp.logical_not(low_first))
-    def _():
-        finish_bottom()
 
     side_copy(4, mirror).wait_recv()
 
@@ -434,32 +433,48 @@
             halo = jnp.where(nbr[2, side_id, f] == 1, turned, straight)
             pad[0:14, col : col + 1, :] = halo[5:19].reshape(14, 1, 128)
 
-    for col in (0, 8, 240, 248):
-        for r, v in enumerate(convolve(col, [bias] * 8, range(8), range(14))):
-            conv[r, pl.ds(col, 8), :] = v
+    ends = (0, 8, 240, 248)
+
+    def convolve_ends(base, rows):
+        for col in ends:
+            got = convolve(col, [bias] * rows, range(rows), range(rows + 6), base)
+            for r, v in enumerate(got):
+                conv[base + r, pl.ds(col, 8), :] = v
+
+    convolve_ends(base5, 5)
+    got = mlp(outside(conv), outside(cot), pl.ds(1120, 160)).reshape(5, 32, 128)
+    conv[five, 0:16, :] = got[:, 0:16]
+    conv[five, 240:256, :] = got[:, 16:32]
+    kernel_grad(base5, 5, ends)
+
+    @pl.when(low_first)
+    def _():
+        finish_top()
+
+    @pl.when(jnp.logical_not(low_first))
+    def _():
+        finish_bottom()
+
+    convolve_ends(base2, 3)
+
+    def send_large():
+        for q in range(4):
+            cols = slice(q * 128, q * 128 + 128)
+            big[q * 4 : q * 4 + 4] = acc_e[0:128, cols].astype(BF).reshape(4, 32, 128)
+            big[16 + q * 4 : 20 + q * 4] = acc_r[:, cols].T.astype(BF).reshape(4, 32, 128)
+        for q in near:
+            remote(big.at[q], slots1.at[me], sem.at[6], sem.at[7], *near_id(q)).start()
 
     got = mlp(
-        jnp.concatenate([inside(conv, three2, 3), outside(conv)], 0),
-        jnp.concatenate([inside(cot, three2, 3), outside(cot)], 0),
-        pl.ds(1120, 928),
+        conv[three2, :, :].reshape(768, 128), cot[three2, :, :].reshape(768, 128), pl.ds(1280, 768), send_large
     )
-    conv[three2, 16:240, :] = got[0:672].reshape(3, 224, 128)
-    ends = got[672:928].reshape(8, 32, 128)
-    conv[:, 0:16, :] = ends[:, 0:16]
-    conv[:, 240:256, :] = ends[:, 16:32]
+    conv[three2, :, :] = got.reshape(3, 256, 128)
+    slots1[me] = big[me]
 
     scale = jnp.zeros((8, 128), F32)
     for q in range(4):
         cols = slice(q * 128, q * 128 + 128)
-        big[q * 4 : q * 4 + 4] = acc_e[0:128, cols].astype(BF).reshape(4, 32, 128)
-        turned = acc_r[:, cols].T
-        big[16 + q * 4 : 20 + q * 4] = turned.astype(BF).reshape(4, 32, 128)
-        scale = scale + fold(turned * wr[cols, :].astype(F32))
-
-    for q in near:
-        remote(big.at[q], slots1.at[me], sem.at[6], sem.at[7], *near_id(q)).start()
-    slots1[me] = big[me]
-
+        scale = scale + fold(acc_r[:, cols].T * wr[cols, :].astype(F32))
     small[...] = jnp.zeros_like(small)
     totals = [jnp.sum(sums[i], 0, keepdims=True) for i in range(4)]
     totals.append((jnp.sum(scale, 0, keepdims=True) + vec(br) * totals[3]) / vec(ls))
@@ -468,8 +483,7 @@
     for q in range(4):
         small[54 + q : 55 + q, :] = acc_e[128:129, q * 128 : q * 128 + 128]
 
-    kernel_grad(base2, 3, inner)
-    kernel_grad(0, 8, (0, 8, 240, 248))
+    kernel_grad(base2, 3, range(0, 256, 8))
     for i in range(49):
         small[i : i + 1, :] = jnp.sum(ksum[i], 0, keepdims=True)
 
@@ -498,10 +512,11 @@
             slotsz.at[z], slotsz.at[z], sem.at[10], sem.at[11], f, hi * 16 + q * 2 + core
         ).start()
 
-    output_inside(pl.ds(1120, 672), three2, 3)
-    ends = output(pl.ds(1792, 256), outside(x)).reshape(8, 32, 128)
-    out[:, 0:16, :] = ends[:, 0:16]
-    out[:, 240:256, :] = ends[:, 16:32]
+    got = output(pl.ds(1120, 160), outside(x)).reshape(5, 32, 128)
+    out[five, 0:16, :] = got[:, 0:16]
+    out[five, 240:256, :] = got[:, 16:32]
+    got = output(pl.ds(1280, 768), x[three2, :, :].reshape(768, 128))
+    out[three2, :, :] = got.reshape(3, 256, 128)
     store = pltpu.make_async_copy(out, out_hbm, out_sem.at[0])
     store.start()
 
@@ -561,8 +576,9 @@
 
     @pl.when(edge)
     def _():
-        drain(nsbuf.at[pl.ds(0, 7)], 0)
-        drain(hbuf, 4)
+        drain(near_band.at[pl.ds(0, 7)], 0)
+        drain(far_band, 18)
+        drain(hbuf.at[pl.ds(0, 15)], 4)
 
     drain(pieces.at[pl.ds(0, 7)], 2)
     drain(slots1.at[pl.ds(0, 31)], 6)
@@ -591,12 +607,14 @@
             pltpu.VMEM((8, 256, 128), BF),
             pltpu.VMEM((3, 256, 128), BF),
             pltpu.VMEM((3, 256, 128), BF),
-            pltpu.VMEM((8, 3, 32, 128), BF),
+            pltpu.VMEM((16, 3, 16, 128), BF),
             pltpu.VMEM((6, 3, 16, 128), BF),
             pltpu.VMEM((8, 3, 16, 128), BF),
             pltpu.VMEM((3, 16, 128), BF),
-            pltpu.VMEM((8, 3, 32, 128), BF),
-            pltpu.VMEM((8, 3, 32, 128), BF),
+            pltpu.VMEM((8, 3, 16, 128), BF),
+            pltpu.VMEM((8, 3, 16, 128), BF),
+            pltpu.VMEM((8, 3, 16, 128), BF),
+            pltpu.VMEM((7, 3, 16, 128), BF),
             pltpu.VMEM((14, 272, 128), F32),
             pltpu.VMEM((8, 256, 128), F32),
             pltpu.VMEM((49, 8, 128), F32),
@@ -614,7 +632,7 @@
             pltpu.VMEM((16, 8, 128), F32),
             pltpu.VMEM((8, 128), F32),
             pltpu.VMEM((8, 128), F32),
-            dma((12,)), dma((3,)), dma((2,)), dma((2,)), dma((6,)), dma((6,)), dma((18,)),
+            dma((12,)), dma((3,)), dma((2,)), dma((2,)), dma((6,)), dma((6,)), dma((20,)),
         ],
         compiler_params=pltpu.CompilerParams(
             collective_id=0, has_side_effects=True, vmem_limit_bytes=56 * 1024 * 1024

time: 48.3 us -> 48.6 us (level)
  no operation moved by 1% of the time
where the time goes in v5:
time: 48.6 us; the launch traced here: 48.5 us
  Pallas kernels  47.9 us (99%)
  between operations  0.66 us (1%)
    pallas_call x1, Pallas kernels, run_main(): pl.pallas_call(functools.partial(main_kernel, factor), out_shape=(shape(8...  45.2 us
    pallas_call x1, Pallas kernels, unpack(): pl.pallas_call(unpack_kernel, out_shape=(jax.ShapeDtypeStruct(raw.shape,...  2.69 us

profile of v5, /device:TPU:1, one launch (start us, length us, event | category | flops | bytes accessed | tf_op | source)
XLA Modules:
  0.0 48.5 jit_solution(11623440829954224867)
XLA Ops:
  0.6 45.2 %main.1 = (bf16[8,256,128]{2,1,0:T(8,128)(2,1)}, bf16[32,32,128]{2,1,0:T(8,128)(2,1)}, f32[8,8,128]{2,1,0:T(8,128)}) custom-call(s32[3,4,8]{2,1,0:T(4,128)} %bitcast.6, bf16[8,256,128]{2,1,0:T(8,128)(2,1)} %bitcast.4, bf16[8,256,128]{2,1,0:T(8,128)(2,1)} %bitcast.5, f32[7,7,128]{2,1,0:T(8,128)} %kern_hbm.1, f32[128]{0:T(128)} %cb_hbm.1, f32[128]{0:T(128)} %gain_hbm.1, ...), custom_call_target="tpu_custom_call" | custom-call | tf_op jit(solution)/shard_map/main/pallas_call | solution.py:595
  45.8 2.7 %unpack.1 = (bf16[8,256,128]{2,1,0:T(8,128)(2,1)}, f32[7,7,128]{2,1,0:T(8,128)}, f32[128]{0:T(128)}, f32[128]{0:T(128)}, f32[128]{0:T(128)}, /*index=5*/f32[128,...) custom-call(bf16[8,256,128]{2,1,0:T(8,128)(2,1)} %get-tuple-element.23.raw, ...), custom_call_target="tpu_custom_call" | custom-call | tf_op jit(solution)/shard_map/unpack/pallas_call | solution.py:675

commit v6 on v5

--- a/solution.py
+++ b/solution.py
@@ -56,7 +56,7 @@
     nbr_hbm, x_hbm, cot_hbm, kern_hbm, cb_hbm, gain_hbm, nb_hbm, we_hbm, be_hbm, wr_hbm, br_hbm, ls_hbm,
     out_hbm, gath, sgath,
     nbr, x, cot, kern, cb, gain, nb, we, be, wr, br, ls, out,
-    top, bot, hbuf, side, pieces, chosen, near_band, far_band, near_out, far_out,
+    top, bot, hbuf, side, piece, pieces, chosen, near_band, far_band, near_out, far_out,
     pad, conv, taps, act, acc_e, acc_r, sums, ksum,
     big, slots1, slotsz, fin, small, sslots1, sslots2, few_ref, sfin,
     load_sem, out_sem, row_send, row_recv, side_send, side_recv, sem,
@@ -68,8 +68,20 @@
     is_last = t == last
     has_up = t > 0
     has_down = t < last
-    mir_up = jnp.logical_and(mirror < last, mirror + 1 != t)
-    mir_down = jnp.logical_and(mirror > 0, mirror - 1 != t)
+    ward = lax.rem(t + 16, TILES)
+    image = last - ward
+    ward_up = ward > 0
+    ward_down = ward < last
+    image_up = jnp.logical_and(image > 0, image - 1 != t)
+    image_down = jnp.logical_and(image < last, image + 1 != t)
+    origin = [lax.rem(v + TILES, TILES) for v in (t + 15, t + 16, t + 17, 16 - t, 15 - t, 14 - t)]
+    own3 = jnp.logical_and(has_up, origin[3] == t)
+    own5 = jnp.logical_and(has_down, origin[5] == t)
+    true = t >= 0
+    valid = [
+        has_up, true, has_down, jnp.logical_and(has_up, origin[3] != t), true,
+        jnp.logical_and(has_down, origin[5] != t),
+    ]
     edge = jnp.logical_or(is_first, is_last)
     hi = t // 16
     s = t % 16
@@ -118,7 +130,6 @@
         hello(*near_id(q))
     for p in line:
         hello(f, hi * 16 + p)
-    hello(f, mirror)
 
     @pl.when(has_up)
     def _():
@@ -128,19 +139,17 @@
     def _():
         hello(f, t + 1)
 
-    @pl.when(mir_up)
-    def _():
-        hello(f, mirror + 1)
-
-    @pl.when(mir_down)
-    def _():
-        hello(f, mirror - 1)
+    for tile, cond in zip(origin, valid):
+
+        @pl.when(cond)
+        def _(tile=tile):
+            hello(f, tile)
 
     loads[0].wait()
     for d in range(3):
         west = x[:, d : d + 1, :].astype(F32).reshape(8, 128)
         east = x[:, 255 - d : 256 - d, :].astype(F32).reshape(8, 128)
-        pieces[f, d] = jnp.concatenate([west, east], 0).astype(BF)
+        piece[d] = jnp.concatenate([west, east], 0).astype(BF)
     pad[3:11, 8:264, :] = x[...].astype(F32)
     for load in loads[1:3]:
         load.wait()
@@ -168,14 +177,15 @@
                 conv[r, pl.ds(col, 8), :] = v
 
     one = lambda cond: cond.astype(jnp.int32)
-    count = 47 + one(has_up) + one(has_down) + one(mir_up) + one(mir_down) + 8 * one(edge)
+    targets = one(ward_up) + one(ward_down) + one(image_up) + one(image_down) + 2
+    count = 46 + one(has_up) + one(has_down) + targets + 8 * one(edge)
     pl.semaphore_wait(barrier, count)
 
     def columns(c):
         return pl.ds(pl.multiple_of(c * 16, 16), 16)
 
     def piece_copy(k, g):
-        return remote(pieces.at[f], pieces.at[f], sem.at[2], sem.at[3], g, t)
+        return remote(piece, pieces.at[f], sem.at[2], sem.at[3], g, ward)
 
     def up_copy():
         return remote(x.at[pl.ds(0, 3)], bot, row_send.at[0], row_recv.at[0], f, t - 1)
@@ -196,6 +206,9 @@
                 ).start()
             near_band[f] = x[three, columns(f), :]
 
+    for k, g in enumerate(others):
+        piece_copy(k, g).start()
+
     @pl.when(has_up)
     def _():
         up_copy().start()
@@ -210,7 +223,33 @@
     def side_copy(slot, tile):
         return remote(chosen, side.at[slot], side_send.at[slot], side_recv.at[slot], f, tile)
 
-    def phase_two():
+    routes = (
+        (0, ward + 1, ward_down), (1, ward, true), (2, ward - 1, ward_up),
+        (3, image + 1, image_down), (4, image, true), (5, image - 1, image_up),
+    )
+
+    def pass_sides():
+        drain(pieces.at[pl.ds(0, 7)], 3)
+        from_west = pieces[nbr[0, 3, f]]
+        from_east = pieces[nbr[0, 1, f]]
+        chosen[...] = jnp.concatenate(
+            [from_west.astype(F32)[:, 8:16], from_east.astype(F32)[:, 0:8]], 1
+        ).astype(BF)
+        for slot, tile, cond in routes:
+
+            @pl.when(cond)
+            def _(slot=slot, tile=tile):
+                side_copy(slot, tile).start()
+
+        @pl.when(own3)
+        def _():
+            side[3] = chosen[...]
+
+        @pl.when(own5)
+        def _():
+            side[5] = chosen[...]
+
+    def pass_bands():
         for near_side, far_side, cond in ((0, 2, is_last), (2, 0, is_first)):
 
             @pl.when(cond)
@@ -224,40 +263,6 @@
                     far_out[k] = far_band[nbr[0, far_side, g]]
                     remote(far_out.at[k], hbuf.at[f + 8], sem.at[4], sem.at[5], g, t).start()
                 hbuf[f + 8] = far_band[nbr[0, far_side, f]]
-
-        drain(pieces.at[pl.ds(0, 7)], 3)
-        from_west = pieces[nbr[0, 3, f]]
-        from_east = pieces[nbr[0, 1, f]]
-        chosen[...] = jnp.concatenate(
-            [from_west.astype(F32)[:, 8:16], from_east.astype(F32)[:, 0:8]], 1
-        ).astype(BF)
-        side_copy(4, mirror).start()
-
-        @pl.when(has_down)
-        def _():
-            side_copy(0, t + 1).start()
-
-        @pl.when(has_up)
-        def _():
-            side_copy(2, t - 1).start()
-
-        @pl.when(mir_up)
-        def _():
-            side_copy(3, mirror + 1).start()
-
-        @pl.when(mir_down)
-        def _():
-            side_copy(5, mirror - 1).start()
-
-        side[1] = chosen[...]
-
-        @pl.when(mirror + 1 == t)
-        def _():
-            side[3] = chosen[...]
-
-        @pl.when(mirror - 1 == t)
-        def _():
-            side[5] = chosen[...]
 
     def polar(flag, rows):
         drain(hbuf.at[pl.ds(0, 15)], 5)
@@ -377,11 +382,9 @@
 
     got = mlp(inside(conv, mid, 2), inside(cot, mid, 2), pl.ds(0, 448))
     conv[mid, 16:240, :] = got.reshape(2, 224, 128)
-    for k, g in enumerate(others):
-        piece_copy(k, g).start()
     ksum[...] = jnp.zeros_like(ksum)
     kernel_grad(3, 2, inner)
-    phase_two()
+    pass_sides()
 
     @pl.when(low_first)
     def _():
@@ -393,25 +396,14 @@
 
     got = mlp(inside(conv, three1, 3), inside(cot, three1, 3), pl.ds(448, 672))
     conv[three1, 16:240, :] = got.reshape(3, 224, 128)
+    pass_bands()
     kernel_grad(base1, 3, inner)
 
-    side_copy(4, mirror).wait_recv()
-
-    @pl.when(has_up)
-    def _():
-        side_copy(0, t - 1).wait_recv()
-
-    @pl.when(has_down)
-    def _():
-        side_copy(2, t + 1).wait_recv()
-
-    @pl.when(mir_up)
-    def _():
-        side_copy(3, mirror + 1).wait_recv()
-
-    @pl.when(mir_down)
-    def _():
-        side_copy(5, mirror - 1).wait_recv()
+    for slot, cond in enumerate(valid):
+
+        @pl.when(cond)
+        def _(slot=slot):
+            side_copy(slot, origin[slot]).wait_recv()
 
     @pl.when(is_first)
     def _():
@@ -554,25 +546,19 @@
     store.wait()
     own.wait()
     own_small.wait()
-    side_copy(4, mirror).wait_send()
+    for slot, tile, cond in routes:
+
+        @pl.when(cond)
+        def _(slot=slot, tile=tile):
+            side_copy(slot, tile).wait_send()
 
     @pl.when(has_up)
     def _():
-        side_copy(2, t - 1).wait_send()
         up_copy().wait_send()
 
     @pl.when(has_down)
     def _():
-        side_copy(0, t + 1).wait_send()
         down_copy().wait_send()
-
-    @pl.when(mir_up)
-    def _():
-        side_copy(3, mirror + 1).wait_send()
-
-    @pl.when(mir_down)
-    def _():
-        side_copy(5, mirror - 1).wait_send()
 
     @pl.when(edge)
     def _():
@@ -609,6 +595,7 @@
             pltpu.VMEM((3, 256, 128), BF),
             pltpu.VMEM((16, 3, 16, 128), BF),
             pltpu.VMEM((6, 3, 16, 128), BF),
+            pltpu.VMEM((3, 16, 128), BF),
             pltpu.VMEM((8, 3, 16, 128), BF),
             pltpu.VMEM((3, 16, 128), BF),
             pltpu.VMEM((8, 3, 16, 128), BF),

time: 48.6 us -> 46.1 us (0.949)
  Pallas kernels: 47.9 us -> 45.3 us
    pallas_call x1, Pallas kernels: 45.2 us -> 42.6 us  [run_main(): pl.pallas_call(functools.partial(main_kernel, factor), out_shape=(shape(8...]
where the time goes in v6:
time: 46.1 us; the launch traced here: 46 us
  Pallas kernels  45.3 us (98%)
  between operations  0.66 us (1%)
    pallas_call x1, Pallas kernels, run_main(): pl.pallas_call(functools.partial(main_kernel, factor), out_shape=(shape(8...  42.6 us
    pallas_call x1, Pallas kernels, unpack(): pl.pallas_call(unpack_kernel, out_shape=(jax.ShapeDtypeStruct(raw.shape,...  2.69 us

profile of v6, /device:TPU:1, one launch (start us, length us, event | category | flops | bytes accessed | tf_op | source)
XLA Modules:
  0.0 46.0 jit_solution(12387720197307640320)
XLA Ops:
  0.6 42.6 %main.1 = (bf16[8,256,128]{2,1,0:T(8,128)(2,1)}, bf16[32,32,128]{2,1,0:T(8,128)(2,1)}, f32[8,8,128]{2,1,0:T(8,128)}) custom-call(s32[3,4,8]{2,1,0:T(4,128)} %bitcast.6, bf16[8,256,128]{2,1,0:T(8,128)(2,1)} %bitcast.4, bf16[8,256,128]{2,1,0:T(8,128)(2,1)} %bitcast.5, f32[7,7,128]{2,1,0:T(8,128)} %kern_hbm.1, f32[128]{0:T(128)} %cb_hbm.1, f32[128]{0:T(128)} %gain_hbm.1, ...), custom_call_target="tpu_custom_call" | custom-call | tf_op jit(solution)/shard_map/main/pallas_call | solution.py:581
  43.3 2.7 %unpack.1 = (bf16[8,256,128]{2,1,0:T(8,128)(2,1)}, f32[7,7,128]{2,1,0:T(8,128)}, f32[128]{0:T(128)}, f32[128]{0:T(128)}, f32[128]{0:T(128)}, /*index=5*/f32[128,...) custom-call(bf16[8,256,128]{2,1,0:T(8,128)(2,1)} %get-tuple-element.23.raw, ...), custom_call_target="tpu_custom_call" | custom-call | tf_op jit(solution)/shard_map/unpack/pallas_call | solution.py:662

commit v7 on v6

--- a/solution.py
+++ b/solution.py
@@ -57,7 +57,7 @@
     out_hbm, gath, sgath,
     nbr, x, cot, kern, cb, gain, nb, we, be, wr, br, ls, out,
     top, bot, hbuf, side, piece, pieces, chosen, near_band, far_band, near_out, far_out,
-    pad, conv, taps, act, acc_e, acc_r, sums, ksum,
+    pad, conv, taps, act, pulled, pulled_wide, acc_e, acc_r, sums, ksum,
     big, slots1, slotsz, fin, small, sslots1, sslots2, few_ref, sfin,
     load_sem, out_sem, row_send, row_recv, side_send, side_recv, sem,
 ):
@@ -126,11 +126,6 @@
         for g in range(FACES):
             hello(g, mirror)
 
-    for q in near:
-        hello(*near_id(q))
-    for p in line:
-        hello(f, hi * 16 + p)
-
     @pl.when(has_up)
     def _():
         hello(f, t - 1)
@@ -144,6 +139,11 @@
         @pl.when(cond)
         def _(tile=tile):
             hello(f, tile)
+
+    for p in line:
+        hello(f, hi * 16 + p)
+    for q in near:
+        hello(*near_id(q))
 
     loads[0].wait()
     for d in range(3):
@@ -311,16 +311,20 @@
     mean_of = jnp.full((128, 128), 1.0 / 128, BF)
     vec = lambda ref: ref[...].reshape(1, -1)
 
-    def mlp(c, cotangent, rows, between=None):
+    def pull_back(cotangent):
+        branch_cot = (cotangent.astype(F32) * vec(ls)).astype(BF)
+        sums[3] += fold(branch_cot.astype(F32))
+        return branch_cot, nt(branch_cot, wr[...])
+
+    def mlp(c, pulled, rows, between=None):
         count = c.shape[0]
         centred = c - nn(c.astype(BF), mean_of)
         variance = nn((centred * centred).astype(BF), mean_of)
         inverse = lax.rsqrt(variance + EPS)
         normed = centred * inverse
         scaled = (normed * vec(gain) + vec(nb)).astype(BF)
-        branch_cot = (cotangent.astype(F32) * vec(ls)).astype(BF)
         hidden = nn(scaled, we[...]) + vec(be)
-        active_cot = nt(branch_cot, wr[...])
+        branch_cot, active_cot = pulled
         square = hidden * hidden
         gate = 0.5 + 0.5 * jnp.tanh(hidden * (ROOT + (ROOT * CUBE) * square))
         active = hidden * gate
@@ -341,7 +345,6 @@
         sums[0] += fold(conv_cot)
         sums[1] += fold(scaled_cot * normed)
         sums[2] += fold(scaled_cot)
-        sums[3] += fold(branch_cot.astype(F32))
         return conv_cot
 
     def kernel_grad(base, rows, cols):
@@ -380,7 +383,7 @@
     def outside(ref):
         return jnp.concatenate([ref[five, 0:16, :], ref[five, 240:256, :]], 1).reshape(160, 128)
 
-    got = mlp(inside(conv, mid, 2), inside(cot, mid, 2), pl.ds(0, 448))
+    got = mlp(inside(conv, mid, 2), pull_back(inside(cot, mid, 2)), pl.ds(0, 448))
     conv[mid, 16:240, :] = got.reshape(2, 224, 128)
     ksum[...] = jnp.zeros_like(ksum)
     kernel_grad(3, 2, inner)
@@ -394,9 +397,9 @@
     def _():
         finish_top()
 
-    got = mlp(inside(conv, three1, 3), inside(cot, three1, 3), pl.ds(448, 672))
+    pass_bands()
+    got = mlp(inside(conv, three1, 3), pull_back(inside(cot, three1, 3)), pl.ds(448, 672))
     conv[three1, 16:240, :] = got.reshape(3, 224, 128)
-    pass_bands()
     kernel_grad(base1, 3, inner)
 
     for slot, cond in enumerate(valid):
@@ -434,10 +437,12 @@
                 conv[base + r, pl.ds(col, 8), :] = v
 
     convolve_ends(base5, 5)
-    got = mlp(outside(conv), outside(cot), pl.ds(1120, 160)).reshape(5, 32, 128)
+    got = mlp(outside(conv), pull_back(outside(cot)), pl.ds(1120, 160)).reshape(5, 32, 128)
     conv[five, 0:16, :] = got[:, 0:16]
     conv[five, 240:256, :] = got[:, 16:32]
     kernel_grad(base5, 5, ends)
+
+    pulled[...], pulled_wide[...] = pull_back(cot[three2, :, :].reshape(768, 128))
 
     @pl.when(low_first)
     def _():
@@ -458,7 +463,7 @@
             remote(big.at[q], slots1.at[me], sem.at[6], sem.at[7], *near_id(q)).start()
 
     got = mlp(
-        conv[three2, :, :].reshape(768, 128), cot[three2, :, :].reshape(768, 128), pl.ds(1280, 768), send_large
+        conv[three2, :, :].reshape(768, 128), (pulled[...], pulled_wide[...]), pl.ds(1280, 768), send_large
     )
     conv[three2, :, :] = got.reshape(3, 256, 128)
     slots1[me] = big[me]
@@ -606,6 +611,8 @@
             pltpu.VMEM((8, 256, 128), F32),
             pltpu.VMEM((49, 8, 128), F32),
             pltpu.VMEM((2048, 512), BF),
+            pltpu.VMEM((768, 128), BF),
+            pltpu.VMEM((768, 512), F32),
             pltpu.VMEM((144, 512), F32),
             pltpu.VMEM((128, 512), F32),
             pltpu.VMEM((4, 8, 128), F32),
@@ -635,15 +642,21 @@
 ):
     fetches = [
         pltpu.make_async_copy(src, dst, sem.at[i])
-        for i, (src, dst) in enumerate(((raw, stage), (gath, rows_in), (sgath, few_in)))
+        for i, (src, dst) in enumerate(((gath, rows_in), (sgath, few_in)))
     ]
+    parts = [pl.ds(i * 2, 2) for i in range(4)]
+    loads = [
+        pltpu.make_async_copy(raw.at[part], stage.at[part], sem.at[2 + i])
+        for i, part in enumerate(parts)
+    ]
+    stores = [
+        pltpu.make_async_copy(stage.at[part], out.at[part], sem.at[6 + i])
+        for i, part in enumerate(parts)
+    ]
+    for fetch in fetches + loads:
+        fetch.start()
     for fetch in fetches:
-        fetch.start()
-    store = pltpu.make_async_copy(stage, out, sem.at[3])
-    fetches[0].wait()
-    store.start()
-    fetches[1].wait()
-    fetches[2].wait()
+        fetch.wait()
     rows = rows_in.reshape(1024, 128)
     few = few_in[...].reshape(64, 128)
     for q in range(4):
@@ -654,7 +667,11 @@
         kernel_grad[i] = few[i * 7 : i * 7 + 7]
     for i, ref in enumerate((cb_grad, gain_grad, nb_grad, br_grad, ls_grad)):
         ref[...] = few[49 + i]
-    store.wait()
+    for load, store in zip(loads, stores):
+        load.wait()
+        store.start()
+    for store in stores:
+        store.wait()
 
 
 def unpack(raw, gath, sgath):
@@ -672,7 +689,7 @@
             pltpu.VMEM(raw.shape, raw.dtype),
             pltpu.VMEM(gath.shape, gath.dtype),
             pltpu.VMEM(sgath.shape, sgath.dtype),
-            pltpu.SemaphoreType.DMA((4,)),
+            pltpu.SemaphoreType.DMA((10,)),
         ],
         compiler_params=pltpu.CompilerParams(vmem_limit_bytes=56 * 1024 * 1024),
         name="unpack",

time: 46.1 us -> 47.2 us (1.024)
  Pallas kernels: 45.3 us -> 46.3 us
    pallas_call x1, Pallas kernels: 42.6 us -> 43.5 us  [run_main(): pl.pallas_call(functools.partial(main_kernel, factor), out_shape=(shape(8...]
where the time goes in v7:
time: 47.2 us; the launch traced here: 47.1 us
  Pallas kernels  46.3 us (98%)
  between operations  0.82 us (2%)
    pallas_call x1, Pallas kernels, run_main(): pl.pallas_call(functools.partial(main_kernel, factor), out_shape=(shape(8...  43.5 us
    pallas_call x1, Pallas kernels, unpack(): pl.pallas_call(unpack_kernel, out_shape=(jax.ShapeDtypeStruct(raw.shape,...  2.74 us

profile of v7, /device:TPU:1, one launch (start us, length us, event | category | flops | bytes accessed | tf_op | source)
XLA Modules:
  0.0 47.1 jit_solution(15478502405842031848)
XLA Ops:
  0.6 43.5 %main.1 = (bf16[8,256,128]{2,1,0:T(8,128)(2,1)}, bf16[32,32,128]{2,1,0:T(8,128)(2,1)}, f32[8,8,128]{2,1,0:T(8,128)}) custom-call(s32[3,4,8]{2,1,0:T(4,128)} %bitcast.6, bf16[8,256,128]{2,1,0:T(8,128)(2,1)} %bitcast.4, bf16[8,256,128]{2,1,0:T(8,128)(2,1)} %bitcast.5, f32[7,7,128]{2,1,0:T(8,128)} %kern_hbm.1, f32[128]{0:T(128)} %cb_hbm.1, f32[128]{0:T(128)} %gain_hbm.1, ...), custom_call_target="tpu_custom_call" | custom-call | tf_op jit(solution)/shard_map/main/pallas_call | solution.py:586
  44.2 2.7 %unpack.1 = (bf16[8,256,128]{2,1,0:T(8,128)(2,1)}, f32[7,7,128]{2,1,0:T(8,128)}, f32[128]{0:T(128)}, f32[128]{0:T(128)}, f32[128]{0:T(128)}, /*index=5*/f32[128,...) custom-call(bf16[8,256,128]{2,1,0:T(8,128)(2,1)} %get-tuple-element.23.raw, ...), custom_call_target="tpu_custom_call" | custom-call | tf_op jit(solution)/shard_map/unpack/pallas_call | solution.py:679

commit v8 on v7

--- a/solution.py
+++ b/solution.py
@@ -88,7 +88,8 @@
     z = s // 2
     core = s % 2
     a = hi * 8 + f
-    me = a * 2 + core
+    me = core * 16 + a
+    twin = t + 1 - 2 * core
     others = [lax.rem(f + k, FACES) for k in range(1, FACES)]
     plane = [lax.rem(a + k, 16) for k in range(1, 16)]
     near = [lax.rem(me + k, 32) for k in range(1, 32)]
@@ -99,7 +100,7 @@
         return lax.rem(p, 8), p // 8 * 16 + s
 
     def near_id(q):
-        return lax.rem(q // 2, 8), q // 16 * 16 + z * 2 + q % 2
+        return lax.rem(q, 8), q % 16 // 8 * 16 + z * 2 + q // 16
 
     def drain(ref, which):
         pltpu.make_async_copy(ref, ref, sem.at[which]).wait()
@@ -383,10 +384,17 @@
     def outside(ref):
         return jnp.concatenate([ref[five, 0:16, :], ref[five, 240:256, :]], 1).reshape(160, 128)
 
+    def put_outside(ref, value):
+        value = value.reshape(5, 32, 128)
+        ref[five, 0:16, :] = value[:, 0:16]
+        ref[five, 240:256, :] = value[:, 16:32]
+
     got = mlp(inside(conv, mid, 2), pull_back(inside(cot, mid, 2)), pl.ds(0, 448))
     conv[mid, 16:240, :] = got.reshape(2, 224, 128)
     ksum[...] = jnp.zeros_like(ksum)
     kernel_grad(3, 2, inner)
+    later = (inside(cot, three1, 3), outside(cot), cot[three2, :, :].reshape(768, 128))
+    pulled[...], pulled_wide[...] = pull_back(jnp.concatenate(later, 0))
     pass_sides()
 
     @pl.when(low_first)
@@ -398,7 +406,7 @@
         finish_top()
 
     pass_bands()
-    got = mlp(inside(conv, three1, 3), pull_back(inside(cot, three1, 3)), pl.ds(448, 672))
+    got = mlp(inside(conv, three1, 3), (pulled[0:672, :], pulled_wide[0:672, :]), pl.ds(448, 672))
     conv[three1, 16:240, :] = got.reshape(3, 224, 128)
     kernel_grad(base1, 3, inner)
 
@@ -437,12 +445,6 @@
                 conv[base + r, pl.ds(col, 8), :] = v
 
     convolve_ends(base5, 5)
-    got = mlp(outside(conv), pull_back(outside(cot)), pl.ds(1120, 160)).reshape(5, 32, 128)
-    conv[five, 0:16, :] = got[:, 0:16]
-    conv[five, 240:256, :] = got[:, 16:32]
-    kernel_grad(base5, 5, ends)
-
-    pulled[...], pulled_wide[...] = pull_back(cot[three2, :, :].reshape(768, 128))
 
     @pl.when(low_first)
     def _():
@@ -463,9 +465,11 @@
             remote(big.at[q], slots1.at[me], sem.at[6], sem.at[7], *near_id(q)).start()
 
     got = mlp(
-        conv[three2, :, :].reshape(768, 128), (pulled[...], pulled_wide[...]), pl.ds(1280, 768), send_large
+        jnp.concatenate([outside(conv), conv[three2, :, :].reshape(768, 128)], 0),
+        (pulled[672:1600, :], pulled_wide[672:1600, :]), pl.ds(1120, 928), send_large,
     )
-    conv[three2, :, :] = got.reshape(3, 256, 128)
+    put_outside(conv, got[0:160])
+    conv[three2, :, :] = got[160:928].reshape(3, 256, 128)
     slots1[me] = big[me]
 
     scale = jnp.zeros((8, 128), F32)
@@ -481,6 +485,7 @@
         small[54 + q : 55 + q, :] = acc_e[128:129, q * 128 : q * 128 + 128]
 
     kernel_grad(base2, 3, range(0, 256, 8))
+    kernel_grad(base5, 5, ends)
     for i in range(49):
         small[i : i + 1, :] = jnp.sum(ksum[i], 0, keepdims=True)
 
@@ -509,9 +514,7 @@
             slotsz.at[z], slotsz.at[z], sem.at[10], sem.at[11], f, hi * 16 + q * 2 + core
         ).start()
 
-    got = output(pl.ds(1120, 160), outside(x)).reshape(5, 32, 128)
-    out[five, 0:16, :] = got[:, 0:16]
-    out[five, 240:256, :] = got[:, 16:32]
+    put_outside(out, output(pl.ds(1120, 160), outside(x)))
     got = output(pl.ds(1280, 768), x[three2, :, :].reshape(768, 128))
     out[three2, :, :] = got.reshape(3, 256, 128)
     store = pltpu.make_async_copy(out, out_hbm, out_sem.at[0])
@@ -530,11 +533,9 @@
     total = slotsz[0].astype(F32)
     for q in range(1, 8):
         total = total + slotsz[q].astype(F32)
-    fin[...] = (total * factor).astype(BF)
-    for q in near:
-        remote(fin, gath.at[me], sem.at[14], sem.at[15], *near_id(q)).start()
-    own = pltpu.make_async_copy(fin, gath.at[me], out_sem.at[1])
-    own.start()
+    fin[a] = (total * factor).astype(BF)
+    for p in plane:
+        remote(fin.at[a], fin.at[a], sem.at[14], sem.at[15], *plane_id(p)).start()
 
     drain(sslots2.at[pl.ds(0, 15)], 13)
     few = sslots2[0]
@@ -545,8 +546,13 @@
         remote(sfin, sgath.at[f], sem.at[16], sem.at[17], g, t).start()
     own_small = pltpu.make_async_copy(sfin, sgath.at[f], out_sem.at[2])
     own_small.start()
+    drain(fin.at[pl.ds(0, 15)], 15)
+    mine = gath.at[pl.ds(pl.multiple_of(core * 16, 16), 16)]
+    remote(fin, mine, sem.at[20], sem.at[21], f, twin).start()
+    own = pltpu.make_async_copy(fin, mine, out_sem.at[1])
+    own.start()
     drain(sgath.at[pl.ds(0, 7)], 17)
-    drain(gath.at[pl.ds(0, 31)], 15)
+    drain(gath.at[pl.ds(0, 16)], 21)
 
     store.wait()
     own.wait()
@@ -576,7 +582,8 @@
     drain(sslots1.at[pl.ds(0, 15)], 8)
     drain(slotsz.at[pl.ds(0, 7)], 10)
     drain(sslots2.at[pl.ds(0, 15)], 12)
-    drain(gath.at[pl.ds(0, 31)], 14)
+    drain(fin.at[pl.ds(0, 15)], 14)
+    drain(fin, 20)
     drain(sgath.at[pl.ds(0, 7)], 16)
 
 
@@ -611,8 +618,8 @@
             pltpu.VMEM((8, 256, 128), F32),
             pltpu.VMEM((49, 8, 128), F32),
             pltpu.VMEM((2048, 512), BF),
-            pltpu.VMEM((768, 128), BF),
-            pltpu.VMEM((768, 512), F32),
+            pltpu.VMEM((1600, 128), BF),
+            pltpu.VMEM((1600, 512), F32),
             pltpu.VMEM((144, 512), F32),
             pltpu.VMEM((128, 512), F32),
             pltpu.VMEM((4, 8, 128), F32),
@@ -620,13 +627,13 @@
             pltpu.VMEM((32, 32, 128), BF),
             pltpu.VMEM((32, 32, 128), BF),
             pltpu.VMEM((8, 32, 128), BF),
-            pltpu.VMEM((32, 128), BF),
+            pltpu.VMEM((16, 32, 128), BF),
             pltpu.VMEM((64, 128), F32),
             pltpu.VMEM((16, 8, 128), F32),
             pltpu.VMEM((16, 8, 128), F32),
             pltpu.VMEM((8, 128), F32),
             pltpu.VMEM((8, 128), F32),
-            dma((12,)), dma((3,)), dma((2,)), dma((2,)), dma((6,)), dma((6,)), dma((20,)),
+            dma((12,)), dma((3,)), dma((2,)), dma((2,)), dma((6,)), dma((6,)), dma((22,)),
         ],
         compiler_params=pltpu.CompilerParams(
             collective_id=0, has_side_effects=True, vmem_limit_bytes=56 * 1024 * 1024

time: 47.2 us -> 45.3 us (0.960)
  Pallas kernels: 46.3 us -> 44.5 us
    pallas_call x1, Pallas kernels: 43.5 us -> 41.8 us  [run_main(): pl.pallas_call(functools.partial(main_kernel, factor), out_shape=(shape(8...]
where the time goes in v8:
time: 45.3 us; the launch traced here: 45.2 us
  Pallas kernels  44.5 us (98%)
  between operations  0.66 us (1%)
    pallas_call x1, Pallas kernels, run_main(): pl.pallas_call(functools.partial(main_kernel, factor), out_shape=(shape(8...  41.8 us
    pallas_call x1, Pallas kernels, unpack(): pl.pallas_call(unpack_kernel, out_shape=(jax.ShapeDtypeStruct(raw.shape,...  2.74 us

profile of v8, /device:TPU:1, one launch (start us, length us, event | category | flops | bytes accessed | tf_op | source)
XLA Modules:
  0.0 45.2 jit_solution(14425578432861419566)
XLA Ops:
  0.6 41.8 %main.1 = (bf16[8,256,128]{2,1,0:T(8,128)(2,1)}, bf16[32,32,128]{2,1,0:T(8,128)(2,1)}, f32[8,8,128]{2,1,0:T(8,128)}) custom-call(s32[3,4,8]{2,1,0:T(4,128)} %bitcast.6, bf16[8,256,128]{2,1,0:T(8,128)(2,1)} %bitcast.4, bf16[8,256,128]{2,1,0:T(8,128)(2,1)} %bitcast.5, f32[7,7,128]{2,1,0:T(8,128)} %kern_hbm.1, f32[128]{0:T(128)} %cb_hbm.1, f32[128]{0:T(128)} %gain_hbm.1, ...), custom_call_target="tpu_custom_call" | custom-call | tf_op jit(solution)/shard_map/main/pallas_call | solution.py:593
  42.5 2.7 %unpack.1 = (bf16[8,256,128]{2,1,0:T(8,128)(2,1)}, f32[7,7,128]{2,1,0:T(8,128)}, f32[128]{0:T(128)}, f32[128]{0:T(128)}, f32[128]{0:T(128)}, /*index=5*/f32[128,...) custom-call(bf16[8,256,128]{2,1,0:T(8,128)(2,1)} %get-tuple-element.23.raw, ...), custom_call_target="tpu_custom_call" | custom-call | tf_op jit(solution)/shard_map/unpack/pallas_call | solution.py:686

commit v9 on v8

--- a/solution.py
+++ b/solution.py
@@ -16,6 +16,19 @@
 CUBE = 0.044715
 FACES = 8
 TILES = 32
+
+
+def ring(step, size):
+    return min(step, size - step)
+
+
+FACE_STEPS = sorted(
+    ((dy, dx) for dy in range(2) for dx in range(4) if dy or dx), key=lambda d: -2 * d[0] - ring(d[1], 4)
+)
+PLANE_STEPS = sorted(
+    ((dy, dx) for dy in range(4) for dx in range(4) if dy or dx), key=lambda d: -ring(d[0], 4) - ring(d[1], 4)
+)
+STACK_STEPS = sorted(range(1, 8), key=lambda d: -ring(d, 8))
 VMEM = pl.BlockSpec(memory_space=pltpu.VMEM)
 SMEM = pl.BlockSpec(memory_space=pltpu.SMEM)
 ANY = pl.BlockSpec(memory_space=pl.ANY)
@@ -90,11 +103,18 @@
     a = hi * 8 + f
     me = core * 16 + a
     twin = t + 1 - 2 * core
-    others = [lax.rem(f + k, FACES) for k in range(1, FACES)]
-    plane = [lax.rem(a + k, 16) for k in range(1, 16)]
-    near = [lax.rem(me + k, 32) for k in range(1, 32)]
-    line = [lax.rem(s + k, 16) for k in range(1, 16)]
-    stack = [lax.rem(z + k, 8) for k in range(1, 8)]
+    yh, across = f // 4, f % 4
+    row = yh * 2 + hi
+
+    def plane_at(dy, dx):
+        to = lax.rem(row + dy, 4)
+        return to % 2 * 8 + to // 2 * 4 + lax.rem(across + dx, 4)
+
+    others = [lax.rem(yh + dy, 2) * 4 + lax.rem(across + dx, 4) for dy, dx in FACE_STEPS]
+    plane = [plane_at(dy, dx) for dy, dx in PLANE_STEPS]
+    near = [c * 16 + p for p in plane for c in (core, 1 - core)] + [(1 - core) * 16 + a]
+    stack = [lax.rem(z + dz, 8) for dz in STACK_STEPS]
+    line = [q * 2 + c for q in stack for c in (core, 1 - core)] + [z * 2 + 1 - core]
 
     def plane_id(p):
         return lax.rem(p, 8), p // 8 * 16 + s
@@ -201,7 +221,7 @@
             three = pl.ds(rows, 3)
             for g in others:
                 remote(x.at[three, columns(g), :], near_band.at[f], sem.at[0], sem.at[1], g, t).start()
-            for g in range(FACES):
+            for g in others + [f]:
                 remote(
                     x.at[three, columns(g + 8), :], far_band.at[f], sem.at[18], sem.at[19], g, mirror
                 ).start()
@@ -256,7 +276,7 @@
             @pl.when(cond)
             def _(near_side=near_side, far_side=far_side):
                 drain(near_band.at[pl.ds(0, 7)], 1)
-                for g in range(FACES):
+                for g in others + [f]:
                     near_out[g] = near_band[nbr[0, near_side, g]]
                     remote(near_out.at[g], hbuf.at[f], sem.at[4], sem.at[5], g, mirror).start()
                 drain(far_band, 19)
@@ -446,6 +466,11 @@
 
     convolve_ends(base5, 5)
 
+    @pl.when(edge)
+    def _():
+        put_outside(conv, mlp(outside(conv), (pulled[672:832, :], pulled_wide[672:832, :]), pl.ds(1120, 160)))
+        kernel_grad(base5, 5, ends)
+
     @pl.when(low_first)
     def _():
         finish_top()
@@ -464,12 +489,23 @@
         for q in near:
             remote(big.at[q], slots1.at[me], sem.at[6], sem.at[7], *near_id(q)).start()
 
-    got = mlp(
-        jnp.concatenate([outside(conv), conv[three2, :, :].reshape(768, 128)], 0),
-        (pulled[672:1600, :], pulled_wide[672:1600, :]), pl.ds(1120, 928), send_large,
-    )
-    put_outside(conv, got[0:160])
-    conv[three2, :, :] = got[160:928].reshape(3, 256, 128)
+    def last_rows():
+        return conv[three2, :, :].reshape(768, 128)
+
+    @pl.when(edge)
+    def _():
+        got = mlp(last_rows(), (pulled[832:1600, :], pulled_wide[832:1600, :]), pl.ds(1280, 768), send_large)
+        conv[three2, :, :] = got.reshape(3, 256, 128)
+
+    @pl.when(jnp.logical_not(edge))
+    def _():
+        got = mlp(
+            jnp.concatenate([outside(conv), last_rows()], 0),
+            (pulled[672:1600, :], pulled_wide[672:1600, :]), pl.ds(1120, 928), send_large,
+        )
+        put_outside(conv, got[0:160])
+        conv[three2, :, :] = got[160:928].reshape(3, 256, 128)
+
     slots1[me] = big[me]
 
     scale = jnp.zeros((8, 128), F32)
@@ -485,7 +521,11 @@
         small[54 + q : 55 + q, :] = acc_e[128:129, q * 128 : q * 128 + 128]
 
     kernel_grad(base2, 3, range(0, 256, 8))
-    kernel_grad(base5, 5, ends)
+
+    @pl.when(jnp.logical_not(edge))
+    def _():
+        kernel_grad(base5, 5, ends)
+
     for i in range(49):
         small[i : i + 1, :] = jnp.sum(ksum[i], 0, keepdims=True)
 

time: 45.3 us -> 44.4 us (0.980)
  Pallas kernels: 44.5 us -> 43.5 us
    pallas_call x1, Pallas kernels: 41.8 us -> 40.7 us  [run_main(): pl.pallas_call(functools.partial(main_kernel, factor), out_shape=(shape(8...]
where the time goes in v9:
time: 44.4 us; the launch traced here: 44.3 us
  Pallas kernels  43.5 us (98%)
  between operations  0.82 us (2%)
    pallas_call x1, Pallas kernels, run_main(): pl.pallas_call(functools.partial(main_kernel, factor), out_shape=(shape(8...  40.7 us
    pallas_call x1, Pallas kernels, unpack(): pl.pallas_call(unpack_kernel, out_shape=(jax.ShapeDtypeStruct(raw.shape,...  2.74 us

profile of v9, /device:TPU:1, one launch (start us, length us, event | category | flops | bytes accessed | tf_op | source)
XLA Modules:
  0.0 44.3 jit_solution(3372010017472148530)
XLA Ops:
  0.6 40.7 %main.1 = (bf16[8,256,128]{2,1,0:T(8,128)(2,1)}, bf16[32,32,128]{2,1,0:T(8,128)(2,1)}, f32[8,8,128]{2,1,0:T(8,128)}) custom-call(s32[3,4,8]{2,1,0:T(4,128)} %bitcast.6, bf16[8,256,128]{2,1,0:T(8,128)(2,1)} %bitcast.4, bf16[8,256,128]{2,1,0:T(8,128)(2,1)} %bitcast.5, f32[7,7,128]{2,1,0:T(8,128)} %kern_hbm.1, f32[128]{0:T(128)} %cb_hbm.1, f32[128]{0:T(128)} %gain_hbm.1, ...), custom_call_target="tpu_custom_call" | custom-call | tf_op jit(solution)/shard_map/main/pallas_call | solution.py:633
  41.4 2.7 %unpack.1 = (bf16[8,256,128]{2,1,0:T(8,128)(2,1)}, f32[7,7,128]{2,1,0:T(8,128)}, f32[128]{0:T(128)}, f32[128]{0:T(128)}, f32[128]{0:T(128)}, /*index=5*/f32[128,...) custom-call(bf16[8,256,128]{2,1,0:T(8,128)(2,1)} %get-tuple-element.23.raw, ...), custom_call_target="tpu_custom_call" | custom-call | tf_op jit(solution)/shard_map/unpack/pallas_call | solution.py:726

commit v10 on v9

--- a/solution.py
+++ b/solution.py
@@ -71,7 +71,7 @@
     nbr, x, cot, kern, cb, gain, nb, we, be, wr, br, ls, out,
     top, bot, hbuf, side, piece, pieces, chosen, near_band, far_band, near_out, far_out,
     pad, conv, taps, act, pulled, pulled_wide, acc_e, acc_r, sums, ksum,
-    big, slots1, slotsz, fin, small, sslots1, sslots2, few_ref, sfin,
+    big, slots1, slotsz, fin, small, few_half, fews, fewz, sfin,
     load_sem, out_sem, row_send, row_recv, side_send, side_recv, sem,
 ):
     f, t = place()
@@ -529,10 +529,10 @@
     for i in range(49):
         small[i : i + 1, :] = jnp.sum(ksum[i], 0, keepdims=True)
 
-    for p in plane:
-        rows = pl.ds(pl.multiple_of(lax.rem(p, 8) * 8, 8), 8)
-        remote(small.at[rows], sslots1.at[a], sem.at[8], sem.at[9], *plane_id(p)).start()
-    sslots1[a] = small[pl.ds(pl.multiple_of(f * 8, 8), 8), :]
+    def half_of(part):
+        return small.at[pl.ds(pl.multiple_of(part * 32, 32), 32)]
+
+    remote(half_of(1 - core), few_half, sem.at[8], sem.at[9], f, twin).start()
 
     def output(rows, residual):
         branch = nn(act[rows, :], wr[...]) + vec(br)
@@ -542,6 +542,12 @@
         out[three, 16:240, :] = output(rows, inside(x, three, count)).reshape(count, 224, 128)
 
     output_inside(pl.ds(0, 448), mid, 2)
+
+    drain(few_half, 9)
+    fews[a] = (half_of(core)[...] + few_half[...]).astype(BF)
+    for p in plane:
+        remote(fews.at[a], fews.at[a], sem.at[22], sem.at[23], *plane_id(p)).start()
+
     output_inside(pl.ds(448, 672), three1, 3)
 
     drain(slots1.at[pl.ds(0, 31)], 7)
@@ -560,14 +566,15 @@
     store = pltpu.make_async_copy(out, out_hbm, out_sem.at[0])
     store.start()
 
-    drain(sslots1.at[pl.ds(0, 15)], 9)
-    few = sslots1[0]
+    drain(fews.at[pl.ds(0, 15)], 23)
+    few = fews[0].astype(F32)
     for p in range(1, 16):
-        few = few + sslots1[p]
-    few_ref[...] = few
-    for p in line:
-        remote(few_ref, sslots2.at[s], sem.at[12], sem.at[13], f, hi * 16 + p).start()
-    sslots2[s] = few
+        few = few + fews[p].astype(F32)
+    fewz[z] = few.astype(BF)
+    for q in stack:
+        remote(
+            fewz.at[z], fewz.at[z], sem.at[12], sem.at[13], f, hi * 16 + q * 2 + core
+        ).start()
 
     drain(slotsz.at[pl.ds(0, 7)], 11)
     total = slotsz[0].astype(F32)
@@ -577,21 +584,21 @@
     for p in plane:
         remote(fin.at[a], fin.at[a], sem.at[14], sem.at[15], *plane_id(p)).start()
 
-    drain(sslots2.at[pl.ds(0, 15)], 13)
-    few = sslots2[0]
-    for p in range(1, 16):
-        few = few + sslots2[p]
+    drain(fewz.at[pl.ds(0, 7)], 13)
+    few = fewz[0].astype(F32)
+    for q in range(1, 8):
+        few = few + fewz[q].astype(F32)
     sfin[...] = few * factor
-    for g in others:
-        remote(sfin, sgath.at[f], sem.at[16], sem.at[17], g, t).start()
-    own_small = pltpu.make_async_copy(sfin, sgath.at[f], out_sem.at[2])
+    mine_small = sgath.at[pl.ds(pl.multiple_of(core * 32, 32), 32)]
+    remote(sfin, mine_small, sem.at[16], sem.at[17], f, twin).start()
+    own_small = pltpu.make_async_copy(sfin, mine_small, out_sem.at[2])
     own_small.start()
     drain(fin.at[pl.ds(0, 15)], 15)
     mine = gath.at[pl.ds(pl.multiple_of(core * 16, 16), 16)]
     remote(fin, mine, sem.at[20], sem.at[21], f, twin).start()
     own = pltpu.make_async_copy(fin, mine, out_sem.at[1])
     own.start()
-    drain(sgath.at[pl.ds(0, 7)], 17)
+    drain(sgath.at[pl.ds(0, 32)], 17)
     drain(gath.at[pl.ds(0, 16)], 21)
 
     store.wait()
@@ -619,12 +626,13 @@
 
     drain(pieces.at[pl.ds(0, 7)], 2)
     drain(slots1.at[pl.ds(0, 31)], 6)
-    drain(sslots1.at[pl.ds(0, 15)], 8)
+    drain(few_half, 8)
+    drain(fews.at[pl.ds(0, 15)], 22)
     drain(slotsz.at[pl.ds(0, 7)], 10)
-    drain(sslots2.at[pl.ds(0, 15)], 12)
+    drain(fewz.at[pl.ds(0, 7)], 12)
     drain(fin.at[pl.ds(0, 15)], 14)
     drain(fin, 20)
-    drain(sgath.at[pl.ds(0, 7)], 16)
+    drain(sfin, 16)
 
 
 def run_main(factor, neighbours, *operands):
@@ -635,7 +643,7 @@
         out_shape=(
             shape(8, 256, 128),
             shape(32, 32, 128),
-            jax.ShapeDtypeStruct((8, 8, 128), F32),
+            jax.ShapeDtypeStruct((64, 128), F32),
         ),
         in_specs=[ANY] * 12,
         out_specs=(ANY, ANY, ANY),
@@ -669,11 +677,11 @@
             pltpu.VMEM((8, 32, 128), BF),
             pltpu.VMEM((16, 32, 128), BF),
             pltpu.VMEM((64, 128), F32),
-            pltpu.VMEM((16, 8, 128), F32),
-            pltpu.VMEM((16, 8, 128), F32),
-            pltpu.VMEM((8, 128), F32),
-            pltpu.VMEM((8, 128), F32),
-            dma((12,)), dma((3,)), dma((2,)), dma((2,)), dma((6,)), dma((6,)), dma((22,)),
+            pltpu.VMEM((32, 128), F32),
+            pltpu.VMEM((16, 32, 128), BF),
+            pltpu.VMEM((8, 32, 128), BF),
+            pltpu.VMEM((32, 128), F32),
+            dma((12,)), dma((3,)), dma((2,)), dma((2,)), dma((6,)), dma((6,)), dma((24,)),
         ],
         compiler_params=pltpu.CompilerParams(
             collective_id=0, has_side_effects=True, vmem_limit_bytes=56 * 1024 * 1024
@@ -705,7 +713,7 @@
     for fetch in fetches:
         fetch.wait()
     rows = rows_in.reshape(1024, 128)
-    few = few_in[...].reshape(64, 128)
+    few = few_in
     for q in range(4):
         we_grad[:, q * 128 : q * 128 + 128] = rows[q * 128 : q * 128 + 128, :].astype(F32)
         be_grad[q * 128 : q * 128 + 128] = few[54 + q]

time: 44.4 us -> 44.5 us (level)
  no operation moved by 1% of the time
where the time goes in v10:
time: 44.5 us; the launch traced here: 44.3 us
  Pallas kernels  43.5 us (98%)
  between operations  0.82 us (2%)
    pallas_call x1, Pallas kernels, run_main(): pl.pallas_call(functools.partial(main_kernel, factor), out_shape=(shape(8...  40.8 us
    pallas_call x1, Pallas kernels, unpack(): pl.pallas_call(unpack_kernel, out_shape=(jax.ShapeDtypeStruct(raw.shape,...  2.74 us

profile of v10, /device:TPU:1, one launch (start us, length us, event | category | flops | bytes accessed | tf_op | source)
XLA Modules:
  0.0 44.3 jit_solution(2354404085313210151)
XLA Ops:
  0.6 40.8 %main.1 = (bf16[8,256,128]{2,1,0:T(8,128)(2,1)}, bf16[32,32,128]{2,1,0:T(8,128)(2,1)}, f32[64,128]{1,0:T(8,128)}) custom-call(s32[3,4,8]{2,1,0:T(4,128)} %bitcast.6, bf16[8,256,128]{2,1,0:T(8,128)(2,1)} %bitcast.4, bf16[8,256,128]{2,1,0:T(8,128)(2,1)} %bitcast.5, f32[7,7,128]{2,1,0:T(8,128)} %kern_hbm.1, f32[128]{0:T(128)} %cb_hbm.1, f32[128]{0:T(128)} %gain_hbm.1, ...), custom_call_target="tpu_custom_call" | custom-call | tf_op jit(solution)/shard_map/main/pallas_call | solution.py:641
  41.5 2.7 %unpack.1 = (bf16[8,256,128]{2,1,0:T(8,128)(2,1)}, f32[7,7,128]{2,1,0:T(8,128)}, f32[128]{0:T(128)}, f32[128]{0:T(128)}, f32[128]{0:T(128)}, /*index=5*/f32[128,...) custom-call(bf16[8,256,128]{2,1,0:T(8,128)(2,1)} %get-tuple-element.23.raw, ...), custom_call_target="tpu_custom_call" | custom-call | tf_op jit(solution)/shard_map/unpack/pallas_call | solution.py:734

commit v11 on v10

--- a/solution.py
+++ b/solution.py
@@ -190,10 +190,10 @@
                         acc[r] = acc[r] + taps[(row - r) * 7 + j] * v
         return [acc[r] for r in out_rows]
 
-    @pl.loop(0, 7)
+    @pl.loop(0, 4)
     def _(i):
-        for u in range(4):
-            col = pl.multiple_of(16 + i * 32 + u * 8, 8)
+        for u in range(7):
+            col = pl.multiple_of(16 + i * 56 + u * 8, 8)
             for r, v in enumerate(convolve(col, [bias] * 8, range(8), range(3, 11))):
                 conv[r, pl.ds(col, 8), :] = v
 
@@ -294,10 +294,10 @@
             pad[rows[d], 8:264, :] = jnp.where(flag == 1, turned, band.astype(F32))
 
     def finish(out_rows, in_rows):
-        @pl.loop(0, 7)
+        @pl.loop(0, 4)
         def _(i):
-            for u in range(4):
-                col = pl.multiple_of(16 + i * 32 + u * 8, 8)
+            for u in range(7):
+                col = pl.multiple_of(16 + i * 56 + u * 8, 8)
                 acc = [conv[r, pl.ds(col, 8), :] for r in out_rows]
                 for r, v in zip(out_rows, convolve(col, acc, out_rows, in_rows)):
                     conv[r, pl.ds(col, 8), :] = v
@@ -369,14 +369,15 @@
         return conv_cot
 
     def kernel_grad(base, rows, cols):
-        steps = len(cols) // 4
+        steps = 1 if len(cols) == 4 else 4
+        width = len(cols) // steps
 
         @pl.loop(0, 7)
         def _(j):
             def step(k, acc):
                 acc = list(acc)
-                for u in range(4):
-                    col = cols[u] if steps == 1 else pl.multiple_of(cols[0] + k * 32 + u * 8, 8)
+                for u in range(width):
+                    col = cols[u] if steps == 1 else pl.multiple_of(cols[0] + k * width * 8 + u * 8, 8)
                     cots = [conv[base + r, pl.ds(col, 8), :] for r in range(rows)]
                     for row in range(rows + 6):
                         v = pad[base + row, pl.ds(col + 5 + j, 8), :]
@@ -690,62 +691,66 @@
     )(neighbours, *operands)
 
 
-def unpack_kernel(
-    raw, gath, sgath,
-    out, kernel_grad, cb_grad, gain_grad, nb_grad, we_grad, be_grad, wr_grad, br_grad, ls_grad,
-    stage, rows_in, few_in, sem,
-):
+def unpack_kernel(raw, gath, sgath, *refs):
+    outs, stages, (rows_in, few_in, sem) = refs[:10], refs[10:20], refs[20:]
+    stage, kernel_grad, cb_grad, gain_grad, nb_grad, we_grad, be_grad, wr_grad, br_grad, ls_grad = stages
     fetches = [
         pltpu.make_async_copy(src, dst, sem.at[i])
         for i, (src, dst) in enumerate(((gath, rows_in), (sgath, few_in)))
     ]
-    parts = [pl.ds(i * 2, 2) for i in range(4)]
+    parts = [pl.ds(i * 4, 4) for i in range(2)]
     loads = [
         pltpu.make_async_copy(raw.at[part], stage.at[part], sem.at[2 + i])
         for i, part in enumerate(parts)
     ]
     stores = [
-        pltpu.make_async_copy(stage.at[part], out.at[part], sem.at[6 + i])
+        pltpu.make_async_copy(stage.at[part], outs[0].at[part], sem.at[4 + i])
         for i, part in enumerate(parts)
+    ]
+    stores += [
+        pltpu.make_async_copy(src, dst, sem.at[6 + i])
+        for i, (src, dst) in enumerate(zip(stages[1:], outs[1:]))
     ]
     for fetch in fetches + loads:
         fetch.start()
-    for fetch in fetches:
-        fetch.wait()
     rows = rows_in.reshape(1024, 128)
     few = few_in
+    fetches[1].wait()
     for q in range(4):
-        we_grad[:, q * 128 : q * 128 + 128] = rows[q * 128 : q * 128 + 128, :].astype(F32)
         be_grad[q * 128 : q * 128 + 128] = few[54 + q]
-    wr_grad[...] = rows[512:1024, :].astype(F32)
     for i in range(7):
         kernel_grad[i] = few[i * 7 : i * 7 + 7]
     for i, ref in enumerate((cb_grad, gain_grad, nb_grad, br_grad, ls_grad)):
         ref[...] = few[49 + i]
-    for load, store in zip(loads, stores):
-        load.wait()
-        store.start()
+    for i in (2, 3, 4, 5, 7, 9, 10):
+        stores[i].start()
+    fetches[0].wait()
+    for q in range(4):
+        we_grad[:, q * 128 : q * 128 + 128] = rows[q * 128 : q * 128 + 128, :].astype(F32)
+    stores[6].start()
+    wr_grad[...] = rows[512:1024, :].astype(F32)
+    stores[8].start()
+    for i in range(2):
+        loads[i].wait()
+        stores[i].start()
     for store in stores:
         store.wait()
 
 
 def unpack(raw, gath, sgath):
     one = lambda *shape: jax.ShapeDtypeStruct(shape, F32)
+    shapes = (
+        jax.ShapeDtypeStruct(raw.shape, raw.dtype),
+        one(7, 7, 128), one(128), one(128), one(128), one(128, 512), one(512),
+        one(512, 128), one(128), one(128),
+    )
     return pl.pallas_call(
         unpack_kernel,
-        out_shape=(
-            jax.ShapeDtypeStruct(raw.shape, raw.dtype),
-            one(7, 7, 128), one(128), one(128), one(128), one(128, 512), one(512),
-            one(512, 128), one(128), one(128),
-        ),
+        out_shape=shapes,
         in_specs=[ANY, ANY, ANY],
-        out_specs=(ANY,) + (VMEM,) * 9,
-        scratch_shapes=[
-            pltpu.VMEM(raw.shape, raw.dtype),
-            pltpu.VMEM(gath.shape, gath.dtype),
-            pltpu.VMEM(sgath.shape, sgath.dtype),
-            pltpu.SemaphoreType.DMA((10,)),
-        ],
+        out_specs=(ANY,) * 10,
+        scratch_shapes=[pltpu.VMEM(item.shape, item.dtype) for item in shapes + (gath, sgath)]
+        + [pltpu.SemaphoreType.DMA((15,))],
         compiler_params=pltpu.CompilerParams(vmem_limit_bytes=56 * 1024 * 1024),
         name="unpack",
     )(raw, gath, sgath)

time: 44.5 us -> 43.5 us (0.978)
  Pallas kernels: 43.5 us -> 42.5 us
    pallas_call x1, Pallas kernels: 2.74 us -> 2.09 us  [unpack(): pl.pallas_call(unpack_kernel, out_shape=shapes, in_specs=[ANY, ANY, ANY],...]
where the time goes in v11:
time: 43.5 us; the launch traced here: 43.3 us
  Pallas kernels  42.5 us (98%)
  between operations  0.82 us (2%)
    pallas_call x1, Pallas kernels, run_main(): pl.pallas_call(functools.partial(main_kernel, factor), out_shape=(shape(8...  40.4 us
    pallas_call x1, Pallas kernels, unpack(): pl.pallas_call(unpack_kernel, out_shape=shapes, in_specs=[ANY, ANY, ANY],...  2.09 us

profile of v11, /device:TPU:1, one launch (start us, length us, event | category | flops | bytes accessed | tf_op | source)
XLA Modules:
  0.0 43.3 jit_solution(13158358359713856415)
XLA Ops:
  0.6 40.4 %main.1 = (bf16[8,256,128]{2,1,0:T(8,128)(2,1)}, bf16[32,32,128]{2,1,0:T(8,128)(2,1)}, f32[64,128]{1,0:T(8,128)}) custom-call(s32[3,4,8]{2,1,0:T(4,128)} %bitcast.6, bf16[8,256,128]{2,1,0:T(8,128)(2,1)} %bitcast.4, bf16[8,256,128]{2,1,0:T(8,128)(2,1)} %bitcast.5, f32[7,7,128]{2,1,0:T(8,128)} %kern_hbm.1, f32[128]{0:T(128)} %cb_hbm.1, f32[128]{0:T(128)} %gain_hbm.1, ...), custom_call_target="tpu_custom_call" | custom-call | tf_op jit(solution)/shard_map/main/pallas_call | solution.py:642
  41.1 2.1 %unpack.1 = (bf16[8,256,128]{2,1,0:T(8,128)(2,1)}, f32[7,7,128]{2,1,0:T(8,128)}, f32[128]{0:T(128)}, f32[128]{0:T(128)}, f32[128]{0:T(128)}, /*index=5*/f32[128,...) custom-call(bf16[8,256,128]{2,1,0:T(8,128)(2,1)} %get-tuple-element.23.raw, ...), custom_call_target="tpu_custom_call" | custom-call | tf_op jit(solution)/shard_map/unpack/pallas_call | solution.py:747

commit v12 on v11

--- a/solution.py
+++ b/solution.py
@@ -227,16 +227,16 @@
                 ).start()
             near_band[f] = x[three, columns(f), :]
 
+    @pl.when(has_up)
+    def _():
+        up_copy().start()
+
+    @pl.when(has_down)
+    def _():
+        down_copy().start()
+
     for k, g in enumerate(others):
         piece_copy(k, g).start()
-
-    @pl.when(has_up)
-    def _():
-        up_copy().start()
-
-    @pl.when(has_down)
-    def _():
-        down_copy().start()
 
     for load in loads[3:]:
         load.wait()
@@ -470,7 +470,6 @@
     @pl.when(edge)
     def _():
         put_outside(conv, mlp(outside(conv), (pulled[672:832, :], pulled_wide[672:832, :]), pl.ds(1120, 160)))
-        kernel_grad(base5, 5, ends)
 
     @pl.when(low_first)
     def _():
@@ -522,10 +521,7 @@
         small[54 + q : 55 + q, :] = acc_e[128:129, q * 128 : q * 128 + 128]
 
     kernel_grad(base2, 3, range(0, 256, 8))
-
-    @pl.when(jnp.logical_not(edge))
-    def _():
-        kernel_grad(base5, 5, ends)
+    kernel_grad(base5, 5, ends)
 
     for i in range(49):
         small[i : i + 1, :] = jnp.sum(ksum[i], 0, keepdims=True)
@@ -581,9 +577,11 @@
     total = slotsz[0].astype(F32)
     for q in range(1, 8):
         total = total + slotsz[q].astype(F32)
-    fin[a] = (total * factor).astype(BF)
-    for p in plane:
-        remote(fin.at[a], fin.at[a], sem.at[14], sem.at[15], *plane_id(p)).start()
+    fin[...] = (total * factor).astype(BF)
+    for q in near:
+        remote(fin, gath.at[me], sem.at[14], sem.at[15], *near_id(q)).start()
+    own = pltpu.make_async_copy(fin, gath.at[me], out_sem.at[1])
+    own.start()
 
     drain(fewz.at[pl.ds(0, 7)], 13)
     few = fewz[0].astype(F32)
@@ -594,13 +592,8 @@
     remote(sfin, mine_small, sem.at[16], sem.at[17], f, twin).start()
     own_small = pltpu.make_async_copy(sfin, mine_small, out_sem.at[2])
     own_small.start()
-    drain(fin.at[pl.ds(0, 15)], 15)
-    mine = gath.at[pl.ds(pl.multiple_of(core * 16, 16), 16)]
-    remote(fin, mine, sem.at[20], sem.at[21], f, twin).start()
-    own = pltpu.make_async_copy(fin, mine, out_sem.at[1])
-    own.start()
+    drain(gath.at[pl.ds(0, 31)], 15)
     drain(sgath.at[pl.ds(0, 32)], 17)
-    drain(gath.at[pl.ds(0, 16)], 21)
 
     store.wait()
     own.wait()
@@ -631,8 +624,7 @@
     drain(fews.at[pl.ds(0, 15)], 22)
     drain(slotsz.at[pl.ds(0, 7)], 10)
     drain(fewz.at[pl.ds(0, 7)], 12)
-    drain(fin.at[pl.ds(0, 15)], 14)
-    drain(fin, 20)
+    drain(gath.at[pl.ds(0, 31)], 14)
     drain(sfin, 16)
 
 
@@ -676,7 +668,7 @@
             pltpu.VMEM((32, 32, 128), BF),
             pltpu.VMEM((32, 32, 128), BF),
             pltpu.VMEM((8, 32, 128), BF),
-            pltpu.VMEM((16, 32, 128), BF),
+            pltpu.VMEM((32, 128), BF),
             pltpu.VMEM((64, 128), F32),
             pltpu.VMEM((32, 128), F32),
             pltpu.VMEM((16, 32, 128), BF),

time: 43.5 us -> 43.3 us (level)
  no operation moved by 1% of the time
where the time goes in v12:
time: 43.3 us; the launch traced here: 43.2 us
  Pallas kernels  42.4 us (98%)
  between operations  0.82 us (2%)
    pallas_call x1, Pallas kernels, run_main(): pl.pallas_call(functools.partial(main_kernel, factor), out_shape=(shape(8...  40.3 us
    pallas_call x1, Pallas kernels, unpack(): pl.pallas_call(unpack_kernel, out_shape=shapes, in_specs=[ANY, ANY, ANY],...  2.09 us

profile of v12, /device:TPU:1, one launch (start us, length us, event | category | flops | bytes accessed | tf_op | source)
XLA Modules:
  0.0 43.2 jit_solution(7024069468229222355)
XLA Ops:
  0.6 40.3 %main.1 = (bf16[8,256,128]{2,1,0:T(8,128)(2,1)}, bf16[32,32,128]{2,1,0:T(8,128)(2,1)}, f32[64,128]{1,0:T(8,128)}) custom-call(s32[3,4,8]{2,1,0:T(4,128)} %bitcast.6, bf16[8,256,128]{2,1,0:T(8,128)(2,1)} %bitcast.4, bf16[8,256,128]{2,1,0:T(8,128)(2,1)} %bitcast.5, f32[7,7,128]{2,1,0:T(8,128)} %kern_hbm.1, f32[128]{0:T(128)} %cb_hbm.1, f32[128]{0:T(128)} %gain_hbm.1, ...), custom_call_target="tpu_custom_call" | custom-call | tf_op jit(solution)/shard_map/main/pallas_call | solution.py:634
  40.9 2.1 %unpack.1 = (bf16[8,256,128]{2,1,0:T(8,128)(2,1)}, f32[7,7,128]{2,1,0:T(8,128)}, f32[128]{0:T(128)}, f32[128]{0:T(128)}, f32[128]{0:T(128)}, /*index=5*/f32[128,...) custom-call(bf16[8,256,128]{2,1,0:T(8,128)(2,1)} %get-tuple-element.23.raw, ...), custom_call_target="tpu_custom_call" | custom-call | tf_op jit(solution)/shard_map/unpack/pallas_call | solution.py:739
